TPU v7x, 256 devices: a whole 4x4x8 slice. The times are simulated.
256 devices in a mesh: shot: 16 (over y, x_lo, core), slab: 16 (over x_hi, z).
Axes of the slice: x: 4 (x_hi: 2, x_lo: 2; x = x_hi * 2 + x_lo), y: 4, z: 8, core: 2. Of those that a mesh axis runs over, the one named last changes fastest.
Arguments:
- velocity: float32 [256, 64, 128], P('slab', 'shot'), may hold values from 0.2 to 0.42
- fields_prev: float32 [16, 2, 256, 64, 128], P('shot', None, 'slab'), may hold values from -6 to 6
- fields_now: float32 [16, 2, 256, 64, 128], P('shot', None, 'slab'), may hold values from -6 to 6
- source_cells: int32 [16, 32], P('shot', 'slab'), may hold values from 32768 to 98303
- source_traces: float32 [16, 8, 32], P('shot', None, 'slab'), may hold values from -6 to 6
- receiver_cells: int32 [16, 4096], P('shot', 'slab'), may hold values from 32768 to 98303
- receiver_traces: float32 [16, 8, 4096], P('shot', None, 'slab'), may hold values from -6 to 6
Outputs:
- gradient: float32 [256, 64, 128], P('slab', 'shot')
- fields_before: float32 [16, 2, 256, 64, 128], P('shot', None, 'slab')
- fields_after: float32 [16, 2, 256, 64, 128], P('shot', None, 'slab')
Inputs may be any that keep to these rules, and one draw needn't show every extreme that they name: `receiver_cells`: block j of each row (entries j * 256 onward) numbers cells of depth slab j, counted from that slab's first plane, plane then first then second lateral index, on planes 4 to 11 of the slab. `source_cells`: block j of each row (entries j * 2 onward) numbers cells of depth slab j, counted from that slab's first plane, plane then first then second lateral index, on planes 4 to 11 of the slab.
All inputs are finite; a program needn't handle non-finite values.
Results may differ from a plain program's by a relative error of at most 0.0003.
Values sent between devices are 32-bit elements; how exact they have to be, the bound alone decides.
No kernel may reach another device: no remote copies, remote signals or barrier semaphores. Data moves between devices by JAX's collectives and lax.ppermute only.
A program may use at most 64 MiB of HBM per device.

v0:
```python
import jax
import jax.numpy as jnp
from jax import lax
from jax.sharding import PartitionSpec as P

STEPS = 8


STENCIL = (-205.0 / 72.0, 8.0 / 5.0, -1.0 / 5.0, 8.0 / 315.0, -1.0 / 560.0)


def extended_2(array, sides, width):
    for axis, dim in sides:
        count, length = (lax.axis_size(axis), array.shape[dim])
        up = [(i, (i + 1) % count) for i in range(count - 1)]
        down = [(j, i) for i, j in up]
        last = lax.slice_in_dim(array, length - width, length, axis=dim)
        first = lax.slice_in_dim(array, 0, width, axis=dim)
        before = lax.ppermute(last, axis, up)
        after = lax.ppermute(first, axis, down)
        array = jnp.concatenate([before, array, after], axis=dim)
    return array


def laplacian(field):
    depth_rows = field.shape[-3]
    width_x = field.shape[-2]
    width_y = field.shape[-1]
    centre = field[..., 4 : depth_rows - 4, :, :]
    padded = jnp.pad(centre, [(0, 0)] * (centre.ndim - 2) + [(4, 4), (4, 4)])
    result = 3.0 * STENCIL[0] * centre
    for reach in range(1, 5):
        result = result + STENCIL[reach] * (
            field[..., 4 + reach : depth_rows - 4 + reach, :, :]
            + field[..., 4 - reach : depth_rows - 4 - reach, :, :]
        )
        result = result + STENCIL[reach] * (
            padded[..., 4 + reach : 4 + reach + width_x, 4 : 4 + width_y]
            + padded[..., 4 - reach : 4 - reach + width_x, 4 : 4 + width_y]
        )
        result = result + STENCIL[reach] * (
            padded[..., 4 : 4 + width_x, 4 + reach : 4 + reach + width_y]
            + padded[..., 4 : 4 + width_x, 4 - reach : 4 - reach + width_y]
        )
    return result


def inject(field, source_index, source_amps, receiver_index, receiver_amps):
    flattened = field.reshape(2, -1)
    source_row = flattened[0].at[source_index].add(source_amps)
    adjoint_row = flattened[1].at[receiver_index].add(receiver_amps)
    return jnp.stack((source_row, adjoint_row)).reshape(field.shape)


def body(
    velocity, fields_prev, fields_now, source_cells, source_traces, receiver_cells, receiver_traces
):
    courant = lax.all_gather(velocity, "shot", axis=1, tiled=True)
    planes, width_x, width_y = courant.shape
    previous = fields_prev[0]
    current = fields_now[0]
    imaging = jnp.zeros((planes, width_x, width_y), jnp.float32)
    for step_index in range(STEPS):
        extended = extended_2(current, (("slab", 1),), 4)
        rows_out = extended.shape[1] - 8
        margin = (rows_out - planes) // 2
        earlier_mid = previous
        present_mid = extended[:, 4 : 4 + rows_out]
        advanced = 2.0 * present_mid - earlier_mid + courant * courant * laplacian(extended)
        offset_cells = margin * width_x * width_y
        advanced = inject(
            advanced,
            source_cells[0] + offset_cells,
            source_traces[0, step_index],
            receiver_cells[0] + offset_cells,
            receiver_traces[0, step_index],
        )
        imaging = imaging + (advanced[0] - 2.0 * current[0] + previous[0]) * current[1]
        previous, current = (current, advanced)
    summed = lax.psum(imaging, "shot")
    owned_part = lax.dynamic_slice_in_dim(
        summed, lax.axis_index("shot") * velocity.shape[1], velocity.shape[1], 1
    )
    factor = -2.0 / (lax.axis_size("shot") * STEPS)
    gradient = factor * owned_part / (velocity * velocity * velocity)
    return (gradient, previous[None], current[None])


def solution(mesh):
    return jax.shard_map(
        body,
        mesh=mesh,
        in_specs=(
            P("slab", "shot", None),
            P("shot", None, "slab", None, None),
            P("shot", None, "slab", None, None),
            P("shot", "slab"),
            P("shot", None, "slab"),
            P("shot", "slab"),
            P("shot", None, "slab"),
        ),
        out_specs=(
            P("slab", "shot", None),
            P("shot", None, "slab", None, None),
            P("shot", None, "slab", None, None),
        ),
        check_vma=False,
    )
```

profile of v0, /device:TPU:1, one launch (start us, length us, event | category | flops | bytes accessed | tf_op | source)
XLA Modules:
  0.0 337.1 jit_solution(2099861718413771662)
XLA Ops:
  9.6 5.0 %collective-permute-start.1 = (f32[2,4,64,128]{3,2,1,0:T(8,128)S(1)}, f32[2,4,64,128]{3,2,1,0:T(8,128)S(1)}, u32[]{:S(2)}, u32[]{:S(2)}) collective-permute-start(f32[2,4,64,128]{3,2,1,0:T(8,128)S(1)} %get-tuple-element.56), channel_id=1, source_target_pairs={{0,1},{1,2},{2,3},{3,4},{4,5},{5,6},{6,7},{7,8},{8,9},{9,10},{10,1... | collective-permute-start | bytes 786440 | tf_op jit(solution)/shard_map/ppermute | solution.py:19
  15.4 28.7 %all_gather.3 = f32[16,64,128]{2,0,1:T(8,128)S(1)} all-gather(f32[16,4,128]{2,0,1:T(8,128)S(1)} %copy.10), channel_id=1, replica_groups=mesh['shot'=16,'slab'=16] {'shot'}, dimensions={1}, use_global_device_ids=true | all-gather | bytes 557056 | tf_op jit(solution)/shard_map/all_gather | solution.py:58
  46.0 3.6 %fusion.10 = f32[2,16,64,128]{3,2,1,0:T(8,128)S(1)} fusion(f32[2,16,64,128]{3,2,1,0:T(8,128)S(1)} %bitcast.186, f32[2,4,64,128]{3,2,1,0:T(8,128)S(1)} %collective-permute-done.1, f32[2,4,64,128]{3,2,1,0:T(8,128)S(1)} %collective-permute-done, f32[1,2,16,64,128]{4,3,2,1,0:T(8,128)S(1)} %copy-done.16, f32[16,64,128]{2,1,0:T(8,128)S(1)} %copy.11), kind=kLoop, calls=%fused_computation.215 | loop fusion | flops 12845056 | bytes 4194304 | tf_op jit(solution)/shard_map/add | solution.py:69
  49.6 2.2 scatter_fusion.1
  54.0 4.0 %collective-permute-start.3 = (f32[2,4,64,128]{3,2,1,0:T(8,128)S(1)}, f32[2,4,64,128]{3,2,1,0:T(8,128)S(1)}, u32[]{:S(2)}, u32[]{:S(2)}) collective-permute-start(f32[2,4,64,128]{3,2,1,0:T(8,128)S(1)} %get-tuple-element.52), channel_id=1, source_target_pairs={{0,1},{1,2},{2,3},{3,4},{4,5},{5,6},{6,7},{7,8},{8,9},{9,10},{10,1... | collective-permute-start | bytes 786440 | tf_op jit(solution)/shard_map/ppermute | solution.py:19
  58.1 4.3 %collective-permute-done.2 = f32[2,4,64,128]{3,2,1,0:T(8,128)S(1)} collective-permute-done((f32[2,4,64,128]{3,2,1,0:T(8,128)S(1)}, f32[2,4,64,128]{3,2,1,0:T(8,128)S(1)}, u32[]{:S(2)}, u32[]{:S(2)}) %collective-permute-start.2) | collective-permute-done | bytes 262176 | tf_op jit(solution)/shard_map/ppermute | solution.py:20
  63.5 2.5 fusion.56
  66.9 2.2 scatter_fusion.3
  70.5 4.7 %collective-permute-start.5 = (f32[2,4,64,128]{3,2,1,0:T(8,128)S(1)}, f32[2,4,64,128]{3,2,1,0:T(8,128)S(1)}, u32[]{:S(2)}, u32[]{:S(2)}) collective-permute-start(f32[2,4,64,128]{3,2,1,0:T(8,128)S(1)} %get-tuple-element.46), channel_id=1, source_target_pairs={{0,1},{1,2},{2,3},{3,4},{4,5},{5,6},{6,7},{7,8},{8,9},{9,10},{10,1... | collective-permute-start | bytes 786440 | tf_op jit(solution)/shard_map/ppermute | solution.py:19
  75.3 3.3 collective-permute-done.4
  79.8 2.5 fusion.85
  83.2 2.2 scatter_fusion.5
  86.7 4.9 %collective-permute-start.7 = (f32[2,4,64,128]{3,2,1,0:T(8,128)S(1)}, f32[2,4,64,128]{3,2,1,0:T(8,128)S(1)}, u32[]{:S(2)}, u32[]{:S(2)}) collective-permute-start(f32[2,4,64,128]{3,2,1,0:T(8,128)S(1)} %get-tuple-element.40), channel_id=1, source_target_pairs={{0,1},{1,2},{2,3},{3,4},{4,5},{5,6},{6,7},{7,8},{8,9},{9,10},{10,1... | collective-permute-start | bytes 786440 | tf_op jit(solution)/shard_map/ppermute | solution.py:19
  91.8 2.2 collective-permute-done.6
  95.1 2.5 fusion.114
  98.5 2.2 scatter_fusion.7
  102.0 4.8 %collective-permute-start.9 = (f32[2,4,64,128]{3,2,1,0:T(8,128)S(1)}, f32[2,4,64,128]{3,2,1,0:T(8,128)S(1)}, u32[]{:S(2)}, u32[]{:S(2)}) collective-permute-start(f32[2,4,64,128]{3,2,1,0:T(8,128)S(1)} %get-tuple-element.34), channel_id=1, source_target_pairs={{0,1},{1,2},{2,3},{3,4},{4,5},{5,6},{6,7},{7,8},{8,9},{9,10},{10,1... | collective-permute-start | bytes 786440 | tf_op jit(solution)/shard_map/ppermute | solution.py:19
  110.5 2.5 fusion.143
  113.9 2.2 scatter_fusion.9
  117.4 4.7 %collective-permute-start.11 = (f32[2,4,64,128]{3,2,1,0:T(8,128)S(1)}, f32[2,4,64,128]{3,2,1,0:T(8,128)S(1)}, u32[]{:S(2)}, u32[]{:S(2)}) collective-permute-start(f32[2,4,64,128]{3,2,1,0:T(8,128)S(1)} %get-tuple-element.28), channel_id=1, source_target_pairs={{0,1},{1,2},{2,3},{3,4},{4,5},{5,6},{6,7},{7,8},{8,9},{9,10},{10,1... | collective-permute-start | bytes 786440 | tf_op jit(solution)/shard_map/ppermute | solution.py:19
  126.9 2.5 fusion.172
  130.3 2.4 scatter_fusion.10
  137.2 4.7 %collective-permute-start.13 = (f32[2,4,64,128]{3,2,1,0:T(8,128)S(1)}, f32[2,4,64,128]{3,2,1,0:T(8,128)S(1)}, u32[]{:S(2)}, u32[]{:S(2)}) collective-permute-start(f32[2,4,64,128]{3,2,1,0:T(8,128)S(1)} %get-tuple-element.22), channel_id=1, source_target_pairs={{0,1},{1,2},{2,3},{3,4},{4,5},{5,6},{6,7},{7,8},{8,9},{9,10},{10,1... | collective-permute-start | bytes 786440 | tf_op jit(solution)/shard_map/ppermute | solution.py:19
  145.6 2.5 fusion.201
  149.1 2.4 scatter_fusion.12
  151.5 3.8 %scatter_fusion.13 = f32[131072]{0:T(1024)} fusion(f32[131072]{0:T(1024)} %bitcast.131, s32[256]{0:T(256)S(1)} %bitcast.198, f32[256]{0:T(256)S(1)} %bitcast.201), kind=kCustom, calls=%fused_computation.13 | custom fusion | flops 256 | bytes 4096 | tf_op jit(solution)/shard_map/scatter-add | solution.py:51
  157.7 4.5 %collective-permute-start.15 = (f32[2,4,64,128]{3,2,1,0:T(8,128)S(1)}, f32[2,4,64,128]{3,2,1,0:T(8,128)S(1)}, u32[]{:S(2)}, u32[]{:S(2)}) collective-permute-start(f32[2,4,64,128]{3,2,1,0:T(8,128)S(1)} %get-tuple-element.16), channel_id=1, source_target_pairs={{0,1},{1,2},{2,3},{3,4},{4,5},{5,6},{6,7},{7,8},{8,9},{9,10},{10,1... | collective-permute-start | bytes 786440 | tf_op jit(solution)/shard_map/ppermute | solution.py:19
  165.8 2.5 fusion.230
  169.3 2.4 scatter_fusion.14
  171.8 4.8 %fusion.288 = f32[16,64,128]{2,1,0:T(8,128)} fusion(f32[16,64,128]{2,1,0:T(8,128)} %bitcast.148, f32[16,64,128]{2,1,0:T(8,128)} %bitcast.142, f32[16,64,128]{2,1,0:T(8,128)S(1)} %bitcast.135, f32[16,64,128]{2,1,0:T(8,128)} %bitcast.175, f32[16,64,128]{2,1,0:T(8,128)} %bitcast.190, f32[16,64,128]{2,1,0:T(8,128)} %bitcast.181, ...), kind=kLoop, calls=%fused_computation.527 | loop fusion | flops 5111808 | bytes 9961472 | tf_op jit(solution)/shard_map/add | solution.py:78
  176.6 2.2 pad_maximum_fusion.16
  182.0 146.8 %all-reduce.10.cloned.1.call-done = f32[16,64,128]{2,1,0:T(8,128)} async-done(((f32[16,64,128]{2,1,0:T(8,128)}), f32[16,64,128]{2,1,0:T(8,128)}) %all-reduce.10.cloned.1.call-update) | async-done | bytes 524304 | tf_op jit(solution)/shard_map/psum | solution.py:80
  (113 shorter events, 50.1 us)
Async XLA Ops:
  7.2 36.9 %copy-start.20 = (s32[1,256]{1,0:T(1,128)S(1)}, s32[1,256]{1,0:T(1,128)}, u32[]{:S(2)}) copy-start(s32[1,256]{1,0:T(1,128)} %param.12) | copy-start | bytes 3076
  7.2 36.9 %copy-start.21 = (s32[1,2]{1,0:T(1,128)S(1)}, s32[1,2]{1,0:T(1,128)}, u32[]{:S(2)}) copy-start(s32[1,2]{1,0:T(1,128)} %param.10) | copy-start | bytes 28
  7.2 36.9 %copy-start.18 = (f32[1,8,2]{1,2,0:T(2,128)S(1)}, f32[1,8,2]{1,2,0:T(2,128)}, u32[]{:S(2)}) copy-start(f32[1,8,2]{1,2,0:T(2,128)} %param.11) | copy-start | bytes 196
  7.2 321.6 %all-reduce.10.cloned.1.call-start = ((), (), s32[]{:S(2)}) async-start(), calls=%async_computation | async-start | bytes 1048576 | tf_op jit(solution)/shard_map/psum | solution.py:80
  8.3 36.8 %collective-permute-start = (f32[2,4,64,128]{3,2,1,0:T(8,128)S(1)}, f32[2,4,64,128]{3,2,1,0:T(8,128)S(1)}, u32[]{:S(2)}, u32[]{:S(2)}) collective-permute-start(f32[2,4,64,128]{3,2,1,0:T(8,128)S(1)} %get-tuple-element.55), channel_id=1, source_target_pairs={{1,0},{2,1},{3,2},{4,3},{5,4},{6,5},{7,6},{8,7},{9,8},{10,9},{11,1... | collective-permute-start | bytes 786440 | tf_op jit(solution)/shard_map/ppermute | solution.py:20
  9.6 35.5 %collective-permute-start.1 = (f32[2,4,64,128]{3,2,1,0:T(8,128)S(1)}, f32[2,4,64,128]{3,2,1,0:T(8,128)S(1)}, u32[]{:S(2)}, u32[]{:S(2)}) collective-permute-start(f32[2,4,64,128]{3,2,1,0:T(8,128)S(1)} %get-tuple-element.56), channel_id=1, source_target_pairs={{0,1},{1,2},{2,3},{3,4},{4,5},{5,6},{6,7},{7,8},{8,9},{9,10},{10,1... | collective-permute-start | bytes 786440 | tf_op jit(solution)/shard_map/ppermute | solution.py:19
  51.8 28.0 %copy-start.2 = (f32[131072]{0:T(1024)}, f32[131072]{0:T(1024)S(1)}, u32[]{:S(2)}) copy-start(f32[131072]{0:T(1024)S(1)} %scatter_fusion.1) | copy-start | bytes 1572868
  52.6 27.2 %copy-start.3 = (f32[131072]{0:T(1024)}, f32[131072]{0:T(1024)S(1)}, u32[]{:S(2)}) copy-start(f32[131072]{0:T(1024)S(1)} %scatter_fusion) | copy-start | bytes 1572868
  52.7 9.7 %collective-permute-start.2 = (f32[2,4,64,128]{3,2,1,0:T(8,128)S(1)}, f32[2,4,64,128]{3,2,1,0:T(8,128)S(1)}, u32[]{:S(2)}, u32[]{:S(2)}) collective-permute-start(f32[2,4,64,128]{3,2,1,0:T(8,128)S(1)} %get-tuple-element.51), channel_id=1, source_target_pairs={{1,0},{2,1},{3,2},{4,3},{5,4},{6,5},{7,6},{8,7},{9,8},{10,9},{11,1... | collective-permute-start | bytes 786440 | tf_op jit(solution)/shard_map/ppermute | solution.py:20
  54.0 9.2 %collective-permute-start.3 = (f32[2,4,64,128]{3,2,1,0:T(8,128)S(1)}, f32[2,4,64,128]{3,2,1,0:T(8,128)S(1)}, u32[]{:S(2)}, u32[]{:S(2)}) collective-permute-start(f32[2,4,64,128]{3,2,1,0:T(8,128)S(1)} %get-tuple-element.52), channel_id=1, source_target_pairs={{0,1},{1,2},{2,3},{3,4},{4,5},{5,6},{6,7},{7,8},{8,9},{9,10},{10,1... | collective-permute-start | bytes 786440 | tf_op jit(solution)/shard_map/ppermute | solution.py:19
  66.9 28.2 %copy-start.4 = (f32[131072]{0:T(1024)}, f32[131072]{0:T(1024)S(1)}, u32[]{:S(2)}) copy-start(f32[131072]{0:T(1024)S(1)} %scatter_fusion.2) | copy-start | bytes 1572868
  69.2 9.4 %collective-permute-start.4 = (f32[2,4,64,128]{3,2,1,0:T(8,128)S(1)}, f32[2,4,64,128]{3,2,1,0:T(8,128)S(1)}, u32[]{:S(2)}, u32[]{:S(2)}) collective-permute-start(f32[2,4,64,128]{3,2,1,0:T(8,128)S(1)} %get-tuple-element.45), channel_id=1, source_target_pairs={{1,0},{2,1},{3,2},{4,3},{5,4},{6,5},{7,6},{8,7},{9,8},{10,9},{11,1... | collective-permute-start | bytes 786440 | tf_op jit(solution)/shard_map/ppermute | solution.py:20
  70.5 9.0 %collective-permute-start.5 = (f32[2,4,64,128]{3,2,1,0:T(8,128)S(1)}, f32[2,4,64,128]{3,2,1,0:T(8,128)S(1)}, u32[]{:S(2)}, u32[]{:S(2)}) collective-permute-start(f32[2,4,64,128]{3,2,1,0:T(8,128)S(1)} %get-tuple-element.46), channel_id=1, source_target_pairs={{0,1},{1,2},{2,3},{3,4},{4,5},{5,6},{6,7},{7,8},{8,9},{9,10},{10,1... | collective-permute-start | bytes 786440 | tf_op jit(solution)/shard_map/ppermute | solution.py:19
  83.2 27.2 %copy-start.5 = (f32[131072]{0:T(1024)}, f32[131072]{0:T(1024)S(1)}, u32[]{:S(2)}) copy-start(f32[131072]{0:T(1024)S(1)} %scatter_fusion.4) | copy-start | bytes 1572868
  85.4 8.5 %collective-permute-start.6 = (f32[2,4,64,128]{3,2,1,0:T(8,128)S(1)}, f32[2,4,64,128]{3,2,1,0:T(8,128)S(1)}, u32[]{:S(2)}, u32[]{:S(2)}) collective-permute-start(f32[2,4,64,128]{3,2,1,0:T(8,128)S(1)} %get-tuple-element.39), channel_id=1, source_target_pairs={{1,0},{2,1},{3,2},{4,3},{5,4},{6,5},{7,6},{8,7},{9,8},{10,9},{11,1... | collective-permute-start | bytes 786440 | tf_op jit(solution)/shard_map/ppermute | solution.py:20
  86.7 8.0 %collective-permute-start.7 = (f32[2,4,64,128]{3,2,1,0:T(8,128)S(1)}, f32[2,4,64,128]{3,2,1,0:T(8,128)S(1)}, u32[]{:S(2)}, u32[]{:S(2)}) collective-permute-start(f32[2,4,64,128]{3,2,1,0:T(8,128)S(1)} %get-tuple-element.40), channel_id=1, source_target_pairs={{0,1},{1,2},{2,3},{3,4},{4,5},{5,6},{6,7},{7,8},{8,9},{9,10},{10,1... | collective-permute-start | bytes 786440 | tf_op jit(solution)/shard_map/ppermute | solution.py:19
  98.5 11.7 %copy-start.6 = (f32[131072]{0:T(1024)}, f32[131072]{0:T(1024)S(1)}, u32[]{:S(2)}) copy-start(f32[131072]{0:T(1024)S(1)} %scatter_fusion.6) | copy-start | bytes 1572868
  100.7 7.9 %collective-permute-start.8 = (f32[2,4,64,128]{3,2,1,0:T(8,128)S(1)}, f32[2,4,64,128]{3,2,1,0:T(8,128)S(1)}, u32[]{:S(2)}, u32[]{:S(2)}) collective-permute-start(f32[2,4,64,128]{3,2,1,0:T(8,128)S(1)} %get-tuple-element.33), channel_id=1, source_target_pairs={{1,0},{2,1},{3,2},{4,3},{5,4},{6,5},{7,6},{8,7},{9,8},{10,9},{11,1... | collective-permute-start | bytes 786440 | tf_op jit(solution)/shard_map/ppermute | solution.py:20
  102.0 8.1 %collective-permute-start.9 = (f32[2,4,64,128]{3,2,1,0:T(8,128)S(1)}, f32[2,4,64,128]{3,2,1,0:T(8,128)S(1)}, u32[]{:S(2)}, u32[]{:S(2)}) collective-permute-start(f32[2,4,64,128]{3,2,1,0:T(8,128)S(1)} %get-tuple-element.34), channel_id=1, source_target_pairs={{0,1},{1,2},{2,3},{3,4},{4,5},{5,6},{6,7},{7,8},{8,9},{9,10},{10,1... | collective-permute-start | bytes 786440 | tf_op jit(solution)/shard_map/ppermute | solution.py:19
  113.9 8.3 %copy-start.8 = (f32[131072]{0:T(1024)}, f32[131072]{0:T(1024)S(1)}, u32[]{:S(2)}) copy-start(f32[131072]{0:T(1024)S(1)} %scatter_fusion.8) | copy-start | bytes 1572868
  116.1 7.9 %collective-permute-start.10 = (f32[2,4,64,128]{3,2,1,0:T(8,128)S(1)}, f32[2,4,64,128]{3,2,1,0:T(8,128)S(1)}, u32[]{:S(2)}, u32[]{:S(2)}) collective-permute-start(f32[2,4,64,128]{3,2,1,0:T(8,128)S(1)} %get-tuple-element.27), channel_id=1, source_target_pairs={{1,0},{2,1},{3,2},{4,3},{5,4},{6,5},{7,6},{8,7},{9,8},{10,9},{11,1... | collective-permute-start | bytes 786440 | tf_op jit(solution)/shard_map/ppermute | solution.py:20
  117.4 8.0 %collective-permute-start.11 = (f32[2,4,64,128]{3,2,1,0:T(8,128)S(1)}, f32[2,4,64,128]{3,2,1,0:T(8,128)S(1)}, u32[]{:S(2)}, u32[]{:S(2)}) collective-permute-start(f32[2,4,64,128]{3,2,1,0:T(8,128)S(1)} %get-tuple-element.28), channel_id=1, source_target_pairs={{0,1},{1,2},{2,3},{3,4},{4,5},{5,6},{6,7},{7,8},{8,9},{9,10},{10,1... | collective-permute-start | bytes 786440 | tf_op jit(solution)/shard_map/ppermute | solution.py:19
  122.2 4.7 %copy-start.7 = (f32[131072]{0:T(1024)S(1)}, f32[131072]{0:T(1024)}, u32[]{:S(2)}) copy-start(f32[131072]{0:T(1024)} %copy-done.6) | copy-start | bytes 1572868
  134.8 7.1 %copy-start.10 = (f32[131072]{0:T(1024)S(1)}, f32[131072]{0:T(1024)}, u32[]{:S(2)}) copy-start(f32[131072]{0:T(1024)} %scatter_fusion.10) | copy-start | bytes 1572868
  135.9 7.9 %collective-permute-start.12 = (f32[2,4,64,128]{3,2,1,0:T(8,128)S(1)}, f32[2,4,64,128]{3,2,1,0:T(8,128)S(1)}, u32[]{:S(2)}, u32[]{:S(2)}) collective-permute-start(f32[2,4,64,128]{3,2,1,0:T(8,128)S(1)} %get-tuple-element.21), channel_id=1, source_target_pairs={{1,0},{2,1},{3,2},{4,3},{5,4},{6,5},{7,6},{8,7},{9,8},{10,9},{11,1... | collective-permute-start | bytes 786440 | tf_op jit(solution)/shard_map/ppermute | solution.py:20
  137.2 8.0 %collective-permute-start.13 = (f32[2,4,64,128]{3,2,1,0:T(8,128)S(1)}, f32[2,4,64,128]{3,2,1,0:T(8,128)S(1)}, u32[]{:S(2)}, u32[]{:S(2)}) collective-permute-start(f32[2,4,64,128]{3,2,1,0:T(8,128)S(1)} %get-tuple-element.22), channel_id=1, source_target_pairs={{0,1},{1,2},{2,3},{3,4},{4,5},{5,6},{6,7},{7,8},{8,9},{9,10},{10,1... | collective-permute-start | bytes 786440 | tf_op jit(solution)/shard_map/ppermute | solution.py:19
  142.1 3.5 %copy-start.9 = (f32[131072]{0:T(1024)S(1)}, f32[131072]{0:T(1024)}, u32[]{:S(2)}) copy-start(f32[131072]{0:T(1024)} %copy-done.8) | copy-start | bytes 1572868
  155.2 7.0 %copy-start = (f32[131072]{0:T(1024)S(1)}, f32[131072]{0:T(1024)}, u32[]{:S(2)}) copy-start(f32[131072]{0:T(1024)} %scatter_fusion.13) | copy-start | bytes 1572868
  155.2 7.0 %copy-start.12 = (f32[131072]{0:T(1024)S(1)}, f32[131072]{0:T(1024)}, u32[]{:S(2)}) copy-start(f32[131072]{0:T(1024)} %scatter_fusion.12) | copy-start | bytes 1572868
  156.4 7.6 %collective-permute-start.14 = (f32[2,4,64,128]{3,2,1,0:T(8,128)S(1)}, f32[2,4,64,128]{3,2,1,0:T(8,128)S(1)}, u32[]{:S(2)}, u32[]{:S(2)}) collective-permute-start(f32[2,4,64,128]{3,2,1,0:T(8,128)S(1)} %get-tuple-element.15), channel_id=1, source_target_pairs={{1,0},{2,1},{3,2},{4,3},{5,4},{6,5},{7,6},{8,7},{9,8},{10,9},{11,1... | collective-permute-start | bytes 786440 | tf_op jit(solution)/shard_map/ppermute | solution.py:20
  157.7 7.7 %collective-permute-start.15 = (f32[2,4,64,128]{3,2,1,0:T(8,128)S(1)}, f32[2,4,64,128]{3,2,1,0:T(8,128)S(1)}, u32[]{:S(2)}, u32[]{:S(2)}) collective-permute-start(f32[2,4,64,128]{3,2,1,0:T(8,128)S(1)} %get-tuple-element.16), channel_id=1, source_target_pairs={{0,1},{1,2},{2,3},{3,4},{4,5},{5,6},{6,7},{7,8},{8,9},{9,10},{10,1... | collective-permute-start | bytes 786440 | tf_op jit(solution)/shard_map/ppermute | solution.py:19
  180.9 147.9 %copy-start.17 = (f32[16,4,128]{2,1,0:T(4,128)S(1)}, f32[16,4,128]{2,1,0:T(4,128)}, u32[]{:S(2)}) copy-start(f32[16,4,128]{2,1,0:T(4,128)} %param.7) | copy-start | bytes 98308
  (7 other events, 14.8 us)
Sparse Core Ops, SparseCore 0:
  176.7 152.0 all-reduce.9
where the time goes:
time: 338 us; the launch traced here: 337 us
  waiting for transfers between devices  172 us (51%)
  other arithmetic  66.9 us (20%)
  starting transfers between devices  47.9 us (14%)
  blocking collectives  28.7 us (8%)
  between operations  14.8 us (4%)
  local copies, waits for them, and re-layouts  6.99 us (2%)
    psum x1, waiting for transfers between devices, body(): summed = lax.psum(imaging, 'shot')  147 us
    ppermute x8, starting transfers between devices, extended_2(): before = lax.ppermute(last, axis, up)  37.5 us
    all_gather x1, blocking collectives, body(): courant = lax.all_gather(velocity, 'shot', axis=1, tiled=True)  28.7 us
    add x8, other arithmetic, body(): 2.0 * present_mid - earlier_mid + courant * courant * laplacian(extended)  20.7 us
    scatter-add x8, other arithmetic, inject(): adjoint_row = flattened[1].at[receiver_index].add(receiver_amps)  18.9 us
    ppermute x8, waiting for transfers between devices, extended_2(): after = lax.ppermute(first, axis, down)  16.6 us
    scatter-add x8, other arithmetic, inject(): source_row = flattened[0].at[source_index].add(source_amps)  11.4 us
    ppermute x8, starting transfers between devices, extended_2(): after = lax.ppermute(first, axis, down)  10.3 us
  transfers between devices with their start and end apart: 17, of which 15 were waited for; matrix products, arithmetic and copies ran while one was open for 2% of the time, Pallas kernels for 0%

commit v1 on v0

v1 whole, which is shorter than its diff:
```python
import functools

import jax
import jax.numpy as jnp
from jax import lax
from jax.experimental import pallas as pl
from jax.experimental.pallas import tpu as pltpu
from jax.sharding import PartitionSpec as P

STEPS = 8
PLANES = 16
NX = 64
NY = 128
SCALE = 5040.0
TAPS = (8064.0, -1008.0, 128.0, -9.0)
CENTRE = 3.0 * -14350.0
F32 = jnp.float32
BF16 = jnp.bfloat16
VMEM_LIMIT = 24 * 1024 * 1024


def y_matrix():
    row = lax.broadcasted_iota(jnp.int32, (2 * NY, NY), 0)
    col = lax.broadcasted_iota(jnp.int32, (2 * NY, NY), 1)
    apart = jnp.abs((row & (NY - 1)) - col)
    out = jnp.zeros((2 * NY, NY), F32)
    for reach, tap in enumerate(TAPS, 1):
        out = jnp.where(apart == reach, tap, out)
    return out.astype(BF16)


def lateral(src, first, count, mat_ref, dest):
    for field in range(2):
        rows = src[field, pl.ds(first, count)].reshape(count * NX, NY)
        high = rows.astype(BF16)
        low = (rows - high.astype(F32)).astype(BF16)
        both = jnp.concatenate([high, low], axis=1)
        dest[field, pl.ds(0, count)] = jnp.dot(
            both, mat_ref[...], preferred_element_type=F32
        ).reshape(count, 8, 8, NY)


def advance(src, first, prev, prev_first, dest, dest_first, vel, vel_first, count, mat_ref, part,
            image=None, image_first=0, inj=None, inj_first=0, unroll=2):
    lateral(src, first, count, mat_ref, part)
    sub = lax.broadcasted_iota(jnp.int32, (8, NY), 0)
    top, bottom = sub == 0, sub == 7

    def plane(p, carry):
        tiles = []
        for field in range(2):
            own = [src[field, first + p, j] for j in range(8)]
            left = [jnp.where(top, 0.0, pltpu.roll(own[j], 1, 0)) for j in range(4, 8)]
            right = [jnp.where(bottom, 0.0, pltpu.roll(own[j], 7, 0)) for j in range(4)]
            tiles.append(left + own + right)
        for j in range(8):
            speed = vel[vel_first + p, j]
            for field in range(2):
                line = tiles[field]
                here = line[j + 4]
                total = CENTRE * here + part[field, p, j]
                for reach, tap in enumerate(TAPS, 1):
                    pair = (line[j + 4 + reach] + line[j + 4 - reach]) + (
                        src[field, first + p + reach, j] + src[field, first + p - reach, j]
                    )
                    total = total + tap * pair
                change = speed * total
                if field == 1 and inj is not None:
                    change = change + inj[inj_first + p, j]
                dest[field, dest_first + p, j] = (here + here) - prev[field, prev_first + p, j] + change
                if field == 0 and image is not None:
                    image[image_first + p, j] += change * tiles[1][j + 4]
        return carry

    lax.fori_loop(0, count, plane, 0, unroll=unroll)


def add_sources(cells, amps, step, dest, dest_first, image, factor, factor_first):
    sub = lax.broadcasted_iota(jnp.int32, (8, NY), 0)
    lane = lax.broadcasted_iota(jnp.int32, (8, NY), 1)
    for n in range(cells.shape[1]):
        cell = cells[0, n]
        z, x, y = cell >> 13, (cell >> 7) & (NX - 1), cell & (NY - 1)
        j, s = x & 7, x >> 3
        amount = jnp.where((sub == s) & (lane == y), amps[0, step, n], 0.0)
        dest[0, dest_first + z, j] += amount
        image[z, j] += amount * factor[1, factor_first + z, j]


def two_steps(step, now, prev, vel, mid, last, last_first, image, inj, cells, amps, mat_ref, part):
    run = functools.partial(advance, mat_ref=mat_ref, part=part)
    for chunk in range(6):
        lo = 4 * chunk
        run(now, lo + 4, prev, lo, mid, lo, vel, lo, 4,
            image=image if 1 <= chunk <= 4 else None, image_first=lo - 4,
            inj=inj.at[0] if 2 <= chunk <= 3 else None, inj_first=lo - 8)
    add_sources(cells, amps, step, mid, 4, image, now, 8)
    for chunk in range(4):
        lo = 4 * chunk
        run(mid, lo + 4, now, lo + 8, last, last_first + lo, vel, lo + 4, 4,
            image=image, image_first=lo,
            inj=inj.at[1] if 1 <= chunk <= 2 else None, inj_first=lo - 4)
    add_sources(cells, amps, step + 1, last, last_first, image, mid, 4)


def to_tiles(src, base, dest_tile):
    for j in range(8):
        dest_tile(j, src[pl.ds(base + j, 8, stride=8), :])


def inject_kernel(cells, amps, out):
    count = cells.shape[1]
    cell = cells[...]
    z, x, y = cell >> 13, (cell >> 7) & (NX - 1), cell & (NY - 1)
    row = (z - 4) * NX + (x & 7) * 8 + (x >> 3)
    hit = (lax.broadcasted_iota(jnp.int32, (8 * NX, count), 0) == row).astype(F32).astype(BF16)
    hits = jnp.concatenate([hit, hit, hit], axis=1)
    lane = lax.broadcasted_iota(jnp.int32, (NY, count), 0) == y
    for pair in range(STEPS // 2):
        sides = []
        for step in (2 * pair, 2 * pair + 1):
            amount = amps[0, pl.ds(step, 1), :]
            high = amount.astype(BF16).astype(F32)
            rest = amount - high
            middle = rest.astype(BF16).astype(F32)
            low = rest - middle
            sides.append(jnp.concatenate(
                [jnp.where(lane, part, 0.0).astype(BF16) for part in (high, middle, low)], axis=1))
        both = jnp.concatenate(sides, axis=0)
        dense = lax.dot_general(hits, both, (((1,), (1,)), ((), ())), preferred_element_type=F32)
        for side in range(2):
            out[2 * pair + side] = dense[:, side * NY:(side + 1) * NY].reshape(8, 8, 8, NY)


def first_kernel(cells, amps, gathered, low_msg, high_msg, prev_in, now_in, inj,
                 low_out, high_out, mid, vel, image, mat_ref, part, now, prev, last):
    mat_ref[...] = y_matrix()
    image[...] = jnp.zeros_like(image)

    def vel_plane(p, carry):
        for j in range(8):
            line = gathered[pl.ds((j // 4) * 96 + p * 4 + j % 4, 8, stride=192), :]
            vel[p, j] = line * line * (1.0 / SCALE)
        return carry

    lax.fori_loop(0, 24, vel_plane, 0, unroll=2)

    def convert(src, count, src_first, per_field, dest, dest_first):
        def plane(p, carry):
            for field in range(2):
                base = (field * per_field + src_first + p) * NX
                for j in range(8):
                    dest[field, dest_first + p, j] = src[pl.ds(base + j, 8, stride=8), :]
            return carry

        lax.fori_loop(0, count, plane, 0, unroll=2)

    convert(low_msg, 8, 0, 12, now, 0)
    convert(now_in, 16, 0, 16, now, 8)
    convert(high_msg, 8, 0, 12, now, 24)
    convert(low_msg, 4, 8, 12, prev, 0)
    convert(prev_in, 16, 0, 16, prev, 4)
    convert(high_msg, 4, 8, 12, prev, 20)
    two_steps(0, now, prev, vel, mid, last, 0, image, inj, cells, amps, mat_ref, part)
    low_out[...] = last[:, 0:8]
    high_out[...] = last[:, 8:16]


def gather_now(below, low, high, above, now):
    def plane(p, carry):
        for field in range(2):
            for n, src in enumerate((below, low, high, above)):
                now[field, 8 * n + p] = src[field, p]
        return carry

    lax.fori_loop(0, 8, plane, 0, unroll=2)


def middle_kernel(step, cells, amps, below, low, high, above, prev, vel, image_in, inj,
                  low_out, high_out, mid, image, mat_ref, part, now, last):
    mat_ref[...] = y_matrix()
    image[...] = image_in[...]
    gather_now(below, low, high, above, now)
    two_steps(step, now, prev, vel, mid, last, 0, image, inj, cells, amps, mat_ref, part)
    low_out[...] = last[:, 0:8]
    high_out[...] = last[:, 8:16]


def last_kernel(step, cells, amps, below, low, high, above, prev, vel, image_in, inj,
                before, after, image_out, mat_ref, part, now, mid, last, image):
    mat_ref[...] = y_matrix()
    image[...] = image_in[...]
    gather_now(below, low, high, above, now)
    two_steps(step, now, prev, vel, mid, last, 0, image, inj, cells, amps, mat_ref, part)

    def plane(p, carry):
        for j in range(8):
            image_out[pl.ds((j // 4) * 64 + p * 4 + j % 4, 8, stride=128), :] = image[p, j]
            for field in range(2):
                base = (field * 16 + p) * NX + j
                before[pl.ds(base, 8, stride=8), :] = mid[field, 4 + p, j]
                after[pl.ds(base, 8, stride=8), :] = last[field, p, j]
        return carry

    lax.fori_loop(0, PLANES, plane, 0, unroll=2)


def tiles(*lead):
    return jax.ShapeDtypeStruct((*lead, 8, 8, NY), F32)


def call(kernel, smem, args, outs, scratch, flops):
    whole = pl.BlockSpec(memory_space=pltpu.VMEM)
    return pl.pallas_call(
        kernel,
        in_specs=[pl.BlockSpec(memory_space=pltpu.SMEM)] * smem + [whole] * (len(args) - smem),
        out_specs=jax.tree.map(lambda _: whole, outs),
        out_shape=outs,
        scratch_shapes=scratch,
        compiler_params=pltpu.CompilerParams(vmem_limit_bytes=VMEM_LIMIT),
        cost_estimate=pl.CostEstimate(flops=flops, bytes_accessed=4 << 20, transcendentals=0),
    )(*args)


def body(
    velocity, fields_prev, fields_now, source_cells, source_traces, receiver_cells, receiver_traces
):
    slabs, shots = lax.axis_size("slab"), lax.axis_size("shot")
    up = [(i, i + 1) for i in range(slabs - 1)]
    down = [(j, i) for i, j in up]

    vel_below = lax.ppermute(velocity[12:], "slab", up)
    vel_above = lax.ppermute(velocity[:4], "slab", down)
    now, prev = fields_now[0], fields_prev[0]
    low_msg = lax.ppermute(jnp.concatenate([now[:, 8:], prev[:, 12:]], axis=1), "slab", up)
    high_msg = lax.ppermute(jnp.concatenate([now[:, :8], prev[:, :4]], axis=1), "slab", down)
    own = jnp.concatenate([vel_below, velocity, vel_above], axis=0).reshape(1, 96, NY)
    gathered = lax.all_to_all(jnp.broadcast_to(own, (shots, 96, NY)), "shot", 0, 0, tiled=True)

    whole = pl.BlockSpec(memory_space=pltpu.VMEM)
    inj = pl.pallas_call(
        inject_kernel,
        in_specs=[whole, whole],
        out_specs=whole,
        out_shape=tiles(STEPS, 8),
        compiler_params=pltpu.CompilerParams(vmem_limit_bytes=VMEM_LIMIT),
        cost_estimate=pl.CostEstimate(flops=1 << 30, bytes_accessed=2 << 20, transcendentals=0),
    )(receiver_cells, receiver_traces)

    half, ext = tiles(2, 8), tiles(2, 24)
    vm = lambda s: pltpu.VMEM(s.shape, s.dtype)
    common = [pltpu.VMEM((2 * NY, NY), BF16), vm(tiles(2, 4)), vm(tiles(2, 32))]
    flops = 1 << 27
    low, high, mid, vel, image = call(
        first_kernel, 2,
        (source_cells, source_traces, gathered.reshape(shots * 96, NY), low_msg.reshape(-1, NY),
         high_msg.reshape(-1, NY), prev.reshape(-1, NY), now.reshape(-1, NY), inj[0:2]),
        (half, half, ext, tiles(24), tiles(16)),
        [*common, vm(ext), vm(tiles(2, 16))], flops)
    for step in range(2, STEPS, 2):
        below = lax.ppermute(high, "slab", up)
        above = lax.ppermute(low, "slab", down)
        args = (source_cells, source_traces, below, low, high, above, mid, vel, image, inj[step:step + 2])
        if step < STEPS - 2:
            low, high, mid, image = call(
                functools.partial(middle_kernel, step), 2, args, (half, half, ext, tiles(16)),
                [*common, vm(tiles(2, 16))], flops)
        else:
            rows = jax.ShapeDtypeStruct((2 * PLANES * NX, NY), F32)
            before, after, terms = call(
                functools.partial(last_kernel, step), 2, args,
                (rows, rows, jax.ShapeDtypeStruct((16 * 64, NY), F32)),
                [*common, vm(ext), vm(tiles(2, 16)), vm(tiles(16))], flops)
    terms = lax.all_to_all(terms.reshape(shots, 64, NY), "shot", 0, 0, tiled=True)
    summed = jnp.sum(terms, axis=0).reshape(velocity.shape)
    gradient = (-2.0 / (shots * STEPS)) * summed / (velocity * velocity * velocity)
    shape = fields_now.shape
    return gradient, before.reshape(shape), after.reshape(shape)


def solution(mesh):
    return jax.shard_map(
        body,
        mesh=mesh,
        in_specs=(
            P("slab", "shot", None),
            P("shot", None, "slab", None, None),
            P("shot", None, "slab", None, None),
            P("shot", "slab"),
            P("shot", None, "slab"),
            P("shot", "slab"),
            P("shot", None, "slab"),
        ),
        out_specs=(
            P("slab", "shot", None),
            P("shot", None, "slab", None, None),
            P("shot", None, "slab", None, None),
        ),
        check_vma=False,
    )
```

time: 338 us -> 148 us (0.44)
  the two profiles are of different devices: /device:TPU:1 before, /device:TPU:100 now
where the time goes in v1:
time: 148 us; the launch traced here: 147 us
  waiting for transfers between devices  59.3 us (40%)
  starting transfers between devices  38.3 us (26%)
  Pallas kernels  27.6 us (19%)
  blocking collectives  13.5 us (9%)
  local copies, waits for them, and re-layouts  5.25 us (4%)
  other arithmetic  2.62 us (2%)
    pallas_call x4, Pallas kernels, call(): pl.pallas_call(kernel, in_specs=[pl.BlockSpec(memory_space=pltpu.SMEM)] *...  26.6 us
    ppermute x3, waiting for transfers between devices, body(): below = lax.ppermute(high, 'slab', up)  25.3 us
    ppermute x3, waiting for transfers between devices, body(): above = lax.ppermute(low, 'slab', down)  22.5 us
    all_to_all x1, blocking collectives, body(): lax.all_to_all(terms.reshape(shots, 64, NY), 'shot', 0, 0, tiled=True)  13.5 us
    all_to_all x1, waiting for transfers between devices, body(): lax.all_to_all(jnp.broadcast_to(own, (shots, 96, NY)), 'shot', 0, 0, tile...  11.4 us
    ppermute x3, starting transfers between devices, body(): below = lax.ppermute(high, 'slab', up)  10.7 us
    ppermute x3, starting transfers between devices, body(): above = lax.ppermute(low, 'slab', down)  8.21 us
    all_to_all x1, starting transfers between devices, body(): lax.all_to_all(jnp.broadcast_to(own, (shots, 96, NY)), 'shot', 0, 0, tile...  5.21 us
  transfers between devices with their start and end apart: 11, of which 7 were waited for; matrix products, arithmetic and copies ran while one was open for 4% of the time, Pallas kernels for 1%

profile of v1, /device:TPU:100, one launch (start us, length us, event | category | flops | bytes accessed | tf_op | source)
XLA Modules:
  0.0 147.4 jit_solution(3801037806347307595)
XLA Ops:
  0.6 0.8 fusion.4
  1.4 5.0 %collective-permute-start = (f32[4,4,128]{2,1,0:T(4,128)S(1)}, f32[4,4,128]{2,1,0:T(4,128)S(1)}, u32[]{:S(2)}, u32[]{:S(2)}) collective-permute-start(f32[4,4,128]{2,1,0:T(4,128)S(1)} %get-tuple-element.43), channel_id=1, source_target_pairs={{0,1},{1,2},{2,3},{3,4},{4,5},{5,6},{6,7},{7,8},{8,9},{9,10},{10,1... | collective-permute-start | bytes 24584 | tf_op jit(solution)/shard_map/ppermute | solution.py:232
  6.5 1.9 %collective-permute-start.1 = (f32[4,4,128]{2,1,0:T(4,128)S(1)}, f32[4,4,128]{2,1,0:T(4,128)S(1)}, u32[]{:S(2)}, u32[]{:S(2)}) collective-permute-start(f32[4,4,128]{2,1,0:T(4,128)S(1)} %get-tuple-element.44), channel_id=1, source_target_pairs={{1,0},{2,1},{3,2},{4,3},{5,4},{6,5},{7,6},{8,7},{9,8},{10,9},{11,1... | collective-permute-start | bytes 24584 | tf_op jit(solution)/shard_map/ppermute | solution.py:233
  8.4 1.1 fusion.3
  9.6 1.0 pad_maximum_fusion
  10.6 5.1 %collective-permute-start.2 = (f32[2,12,64,128]{3,2,1,0:T(8,128)}, f32[2,12,64,128]{3,2,1,0:T(8,128)}, u32[]{:S(2)}, u32[]{:S(2)}) collective-permute-start(f32[2,12,64,128]{3,2,1,0:T(8,128)} %pad_maximum_fusion), channel_id=1, source_target_pairs={{0,1},{1,2},{2,3},{3,4},{4,5},{5,6},{6,7},{7,8},{8,9},{9,10},{10,1... | collective-permute-start | bytes 2359304 | tf_op jit(solution)/shard_map/ppermute | solution.py:235
  15.7 1.0 pad_maximum_fusion.1
  16.7 2.0 %collective-permute-start.3 = (f32[2,12,64,128]{3,2,1,0:T(8,128)}, f32[2,12,64,128]{3,2,1,0:T(8,128)}, u32[]{:S(2)}, u32[]{:S(2)}) collective-permute-start(f32[2,12,64,128]{3,2,1,0:T(8,128)} %pad_maximum_fusion.1), channel_id=1, source_target_pairs={{1,0},{2,1},{3,2},{4,3},{5,4},{6,5},{7,6},{8,7},{9,8},{10,9},{11,1... | collective-permute-start | bytes 2359304 | tf_op jit(solution)/shard_map/ppermute | solution.py:236
  18.8 1.0 broadcast_in_dim.8
  19.7 5.2 %all-to-all-start = ((f32[16,96,128]{2,1,0:T(8,128)}), f32[16,96,128]{2,1,0:T(8,128)S(1)}, u32[]{:S(2)}, u32[]{:S(2)}) async-start(f32[16,96,128]{2,1,0:T(8,128)} %broadcast_in_dim.8), calls=%async_computation | async-start | bytes 1572864 | tf_op jit(solution)/shard_map/all_to_all | solution.py:238
  25.0 1.0 shard_map.94
  26.1 1.2 fusion.1
  27.3 11.4 %all-to-all-done = f32[16,96,128]{2,1,0:T(8,128)S(1)} async-done(((f32[16,96,128]{2,1,0:T(8,128)}), f32[16,96,128]{2,1,0:T(8,128)S(1)}, u32[]{:S(2)}, u32[]{:S(2)}) %all-to-all-start) | async-done | bytes 786464 | tf_op jit(solution)/shard_map/all_to_all | solution.py:238
  38.7 1.0 copy-done.4
  39.8 7.7 %shard_map.95 = (f32[2,8,8,8,128]{4,3,2,1,0:T(8,128)S(1)}, f32[2,8,8,8,128]{4,3,2,1,0:T(8,128)S(1)}, f32[2,24,8,8,128]{4,3,2,1,0:T(8,128)S(1)}, f32[24,8,8,128]{3,2,1,0:T(8,128)S(1)}, f32[16,8,8,128]{3,2,1,0:T(8,128)S(1)}) custom-call(s32[1,2]{1,0:T(1,128)S(1)} %copy-done.5, f32[1,8,2]{2,1,0:T(8,128)S(1)} %copy.13.amps, f32[1536,128]{1,0:T(8,128)S(1)} %bitcast.17, ...), custom_call_target="tpu_custom_call" | custom-call | flops 134217728 | bytes 4194304 | tf_op jit(solution)/shard_map/pallas_call | solution.py:214
  47.4 5.2 %collective-permute-start.4 = (f32[2,8,8,8,128]{4,3,2,1,0:T(8,128)S(1)}, f32[2,8,8,8,128]{4,3,2,1,0:T(8,128)S(1)}, u32[]{:S(2)}, u32[]{:S(2)}) collective-permute-start(f32[2,8,8,8,128]{4,3,2,1,0:T(8,128)S(1)} %get-tuple-element.19.high), channel_id=1, source_target_pairs={{0,1},{1,2},{2,3},{3,4},{4,5},{5,6},{6,7},{7,8},{8,9},{9,10},{10,1... | collective-permute-start | bytes 1572872 | tf_op jit(solution)/shard_map/ppermute | solution.py:261
  52.6 1.9 %collective-permute-start.5 = (f32[2,8,8,8,128]{4,3,2,1,0:T(8,128)S(1)}, f32[2,8,8,8,128]{4,3,2,1,0:T(8,128)S(1)}, u32[]{:S(2)}, u32[]{:S(2)}) collective-permute-start(f32[2,8,8,8,128]{4,3,2,1,0:T(8,128)S(1)} %get-tuple-element.20.low), channel_id=1, source_target_pairs={{1,0},{2,1},{3,2},{4,3},{5,4},{6,5},{7,6},{8,7},{9,8},{10,9},{11,1... | collective-permute-start | bytes 1572872 | tf_op jit(solution)/shard_map/ppermute | solution.py:262
  54.5 9.0 %collective-permute-done.4.below = f32[2,8,8,8,128]{4,3,2,1,0:T(8,128)S(1)} collective-permute-done((f32[2,8,8,8,128]{4,3,2,1,0:T(8,128)S(1)}, f32[2,8,8,8,128]{4,3,2,1,0:T(8,128)S(1)}, u32[]{:S(2)}, u32[]{:S(2)}) %collective-permute-start.4) | collective-permute-done | bytes 524320 | tf_op jit(solution)/shard_map/ppermute | solution.py:261
  63.6 5.3 %collective-permute-done.5.above = f32[2,8,8,8,128]{4,3,2,1,0:T(8,128)S(1)} collective-permute-done((f32[2,8,8,8,128]{4,3,2,1,0:T(8,128)S(1)}, f32[2,8,8,8,128]{4,3,2,1,0:T(8,128)S(1)}, u32[]{:S(2)}, u32[]{:S(2)}) %collective-permute-start.5) | collective-permute-done | bytes 524320 | tf_op jit(solution)/shard_map/ppermute | solution.py:262
  68.9 5.7 %shard_map.96 = (f32[2,8,8,8,128]{4,3,2,1,0:T(8,128)S(1)}, f32[2,8,8,8,128]{4,3,2,1,0:T(8,128)S(1)}, f32[2,24,8,8,128]{4,3,2,1,0:T(8,128)S(1)}, f32[16,8,8,128]{3,2,1,0:T(8,128)S(1)}) custom-call(s32[1,2]{1,0:T(1,128)S(1)} %copy-done.5, f32[1,8,2]{2,1,0:T(8,128)S(1)} %copy.13.amps, f32[2,8,8,8,128]{4,3,2,1,0:T(8,128)S(1)} %collective-permute-done.4.below, ...), custom_call_target="tpu_custom_call" | custom-call | flops 134217728 | bytes 4194304 | tf_op jit(solution)/shard_map/pallas_call | solution.py:214
  74.6 1.9 %collective-permute-start.6 = (f32[2,8,8,8,128]{4,3,2,1,0:T(8,128)S(1)}, f32[2,8,8,8,128]{4,3,2,1,0:T(8,128)S(1)}, u32[]{:S(2)}, u32[]{:S(2)}) collective-permute-start(f32[2,8,8,8,128]{4,3,2,1,0:T(8,128)S(1)} %get-tuple-element.24.high), channel_id=1, source_target_pairs={{0,1},{1,2},{2,3},{3,4},{4,5},{5,6},{6,7},{7,8},{8,9},{9,10},{10,1... | collective-permute-start | bytes 1572872 | tf_op jit(solution)/shard_map/ppermute | solution.py:261
  76.5 3.9 %collective-permute-start.7 = (f32[2,8,8,8,128]{4,3,2,1,0:T(8,128)S(1)}, f32[2,8,8,8,128]{4,3,2,1,0:T(8,128)S(1)}, u32[]{:S(2)}, u32[]{:S(2)}) collective-permute-start(f32[2,8,8,8,128]{4,3,2,1,0:T(8,128)S(1)} %get-tuple-element.25.low), channel_id=1, source_target_pairs={{1,0},{2,1},{3,2},{4,3},{5,4},{6,5},{7,6},{8,7},{9,8},{10,9},{11,1... | collective-permute-start | bytes 1572872 | tf_op jit(solution)/shard_map/ppermute | solution.py:262
  80.4 8.3 %collective-permute-done.6.below = f32[2,8,8,8,128]{4,3,2,1,0:T(8,128)S(1)} collective-permute-done((f32[2,8,8,8,128]{4,3,2,1,0:T(8,128)S(1)}, f32[2,8,8,8,128]{4,3,2,1,0:T(8,128)S(1)}, u32[]{:S(2)}, u32[]{:S(2)}) %collective-permute-start.6) | collective-permute-done | bytes 524320 | tf_op jit(solution)/shard_map/ppermute | solution.py:261
  88.7 12.9 %collective-permute-done.7.above = f32[2,8,8,8,128]{4,3,2,1,0:T(8,128)S(1)} collective-permute-done((f32[2,8,8,8,128]{4,3,2,1,0:T(8,128)S(1)}, f32[2,8,8,8,128]{4,3,2,1,0:T(8,128)S(1)}, u32[]{:S(2)}, u32[]{:S(2)}) %collective-permute-start.7) | collective-permute-done | bytes 524320 | tf_op jit(solution)/shard_map/ppermute | solution.py:262
  101.6 5.7 %shard_map.97 = (f32[2,8,8,8,128]{4,3,2,1,0:T(8,128)S(1)}, f32[2,8,8,8,128]{4,3,2,1,0:T(8,128)S(1)}, f32[2,24,8,8,128]{4,3,2,1,0:T(8,128)S(1)}, f32[16,8,8,128]{3,2,1,0:T(8,128)S(1)}) custom-call(s32[1,2]{1,0:T(1,128)S(1)} %copy-done.5, f32[1,8,2]{2,1,0:T(8,128)S(1)} %copy.13.amps, f32[2,8,8,8,128]{4,3,2,1,0:T(8,128)S(1)} %collective-permute-done.6.below, ...), custom_call_target="tpu_custom_call" | custom-call | flops 134217728 | bytes 4194304 | tf_op jit(solution)/shard_map/pallas_call | solution.py:214
  107.3 3.7 %collective-permute-start.8 = (f32[2,8,8,8,128]{4,3,2,1,0:T(8,128)S(1)}, f32[2,8,8,8,128]{4,3,2,1,0:T(8,128)S(1)}, u32[]{:S(2)}, u32[]{:S(2)}) collective-permute-start(f32[2,8,8,8,128]{4,3,2,1,0:T(8,128)S(1)} %get-tuple-element.28.high), channel_id=1, source_target_pairs={{0,1},{1,2},{2,3},{3,4},{4,5},{5,6},{6,7},{7,8},{8,9},{9,10},{10,1... | collective-permute-start | bytes 1572872 | tf_op jit(solution)/shard_map/ppermute | solution.py:261
  111.0 2.4 %collective-permute-start.9 = (f32[2,8,8,8,128]{4,3,2,1,0:T(8,128)S(1)}, f32[2,8,8,8,128]{4,3,2,1,0:T(8,128)S(1)}, u32[]{:S(2)}, u32[]{:S(2)}) collective-permute-start(f32[2,8,8,8,128]{4,3,2,1,0:T(8,128)S(1)} %get-tuple-element.29.low), channel_id=1, source_target_pairs={{1,0},{2,1},{3,2},{4,3},{5,4},{6,5},{7,6},{8,7},{9,8},{10,9},{11,1... | collective-permute-start | bytes 1572872 | tf_op jit(solution)/shard_map/ppermute | solution.py:262
  113.4 8.0 %collective-permute-done.8.below = f32[2,8,8,8,128]{4,3,2,1,0:T(8,128)S(1)} collective-permute-done((f32[2,8,8,8,128]{4,3,2,1,0:T(8,128)S(1)}, f32[2,8,8,8,128]{4,3,2,1,0:T(8,128)S(1)}, u32[]{:S(2)}, u32[]{:S(2)}) %collective-permute-start.8) | collective-permute-done | bytes 524320 | tf_op jit(solution)/shard_map/ppermute | solution.py:261
  121.3 4.3 %collective-permute-done.9.above = f32[2,8,8,8,128]{4,3,2,1,0:T(8,128)S(1)} collective-permute-done((f32[2,8,8,8,128]{4,3,2,1,0:T(8,128)S(1)}, f32[2,8,8,8,128]{4,3,2,1,0:T(8,128)S(1)}, u32[]{:S(2)}, u32[]{:S(2)}) %collective-permute-start.9) | collective-permute-done | bytes 524320 | tf_op jit(solution)/shard_map/ppermute | solution.py:262
  125.6 7.6 %shard_map.98 = (f32[2048,128]{1,0:T(8,128)}, f32[2048,128]{1,0:T(8,128)}, f32[1024,128]{1,0:T(8,128)S(1)}) custom-call(s32[1,2]{1,0:T(1,128)S(1)} %copy-done.5, f32[1,8,2]{2,1,0:T(8,128)S(1)} %copy.13.amps, f32[2,8,8,8,128]{4,3,2,1,0:T(8,128)S(1)} %collective-permute-done.8.below, f32[2,8,8,8,128]{4,3,2,1,0:T(8,128)S(1)} %get-tuple-element.29.low, ...), custom_call_target="tpu_custom_call" | custom-call | flops 134217728 | bytes 4194304 | tf_op jit(solution)/shard_map/pallas_call | solution.py:214
  133.2 13.5 %all_to_all.10 = f32[16,64,128]{2,1,0:T(8,128)S(1)} all-to-all(f32[16,64,128]{2,1,0:T(8,128)S(1)} %bitcast.20), channel_id=1, replica_groups=mesh['shot'=16,'slab'=16] {'shot'}, dimensions={0} | all-to-all | bytes 1048576 | tf_op jit(solution)/shard_map/all_to_all | solution.py:274
  146.7 0.6 fusion
  (28 shorter events, 0.3 us)
Async XLA Ops:
  0.6 8.9 %copy-start = (f32[1,2,16,64,128]{4,3,2,1,0:T(8,128)S(1)}, f32[1,2,16,64,128]{4,3,2,1,0:T(8,128)}, u32[]{:S(2)}) copy-start(f32[1,2,16,64,128]{4,3,2,1,0:T(8,128)} %param.9) | copy-start | bytes 3145732
  1.4 17.3 %collective-permute-start = (f32[4,4,128]{2,1,0:T(4,128)S(1)}, f32[4,4,128]{2,1,0:T(4,128)S(1)}, u32[]{:S(2)}, u32[]{:S(2)}) collective-permute-start(f32[4,4,128]{2,1,0:T(4,128)S(1)} %get-tuple-element.43), channel_id=1, source_target_pairs={{0,1},{1,2},{2,3},{3,4},{4,5},{5,6},{6,7},{7,8},{8,9},{9,10},{10,1... | collective-permute-start | bytes 24584 | tf_op jit(solution)/shard_map/ppermute | solution.py:232
  6.5 12.2 %collective-permute-start.1 = (f32[4,4,128]{2,1,0:T(4,128)S(1)}, f32[4,4,128]{2,1,0:T(4,128)S(1)}, u32[]{:S(2)}, u32[]{:S(2)}) collective-permute-start(f32[4,4,128]{2,1,0:T(4,128)S(1)} %get-tuple-element.44), channel_id=1, source_target_pairs={{1,0},{2,1},{3,2},{4,3},{5,4},{6,5},{7,6},{8,7},{9,8},{10,9},{11,1... | collective-permute-start | bytes 24584 | tf_op jit(solution)/shard_map/ppermute | solution.py:233
  9.6 9.2 %copy-start.8 = (f32[16,4,128]{2,1,0:T(4,128)S(1)}, f32[16,4,128]{2,1,0:T(4,128)}, u32[]{:S(2)}) copy-start(f32[16,4,128]{2,1,0:T(4,128)} %param.7) | copy-start | bytes 98308
  10.6 28.1 %collective-permute-start.2 = (f32[2,12,64,128]{3,2,1,0:T(8,128)}, f32[2,12,64,128]{3,2,1,0:T(8,128)}, u32[]{:S(2)}, u32[]{:S(2)}) collective-permute-start(f32[2,12,64,128]{3,2,1,0:T(8,128)} %pad_maximum_fusion), channel_id=1, source_target_pairs={{0,1},{1,2},{2,3},{3,4},{4,5},{5,6},{6,7},{7,8},{8,9},{9,10},{10,1... | collective-permute-start | bytes 2359304 | tf_op jit(solution)/shard_map/ppermute | solution.py:235
  16.7 8.3 %copy-start.9 = (f32[1,8,2]{1,2,0:T(2,128)S(1)}, f32[1,8,2]{1,2,0:T(2,128)}, u32[]{:S(2)}) copy-start(f32[1,8,2]{1,2,0:T(2,128)} %param.11) | copy-start | bytes 196
  16.7 8.4 %copy-start.6 = (f32[1,8,256]{2,1,0:T(8,128)S(1)}, f32[1,8,256]{2,1,0:T(8,128)}, u32[]{:S(2)}) copy-start(f32[1,8,256]{2,1,0:T(8,128)} %amps.5) | copy-start | bytes 24580
  16.7 8.4 %copy-start.7 = (s32[1,256]{1,0:T(1,128)S(1)}, s32[1,256]{1,0:T(1,128)}, u32[]{:S(2)}) copy-start(s32[1,256]{1,0:T(1,128)} %cells.5) | copy-start | bytes 3076
  16.7 22.0 %collective-permute-start.3 = (f32[2,12,64,128]{3,2,1,0:T(8,128)}, f32[2,12,64,128]{3,2,1,0:T(8,128)}, u32[]{:S(2)}, u32[]{:S(2)}) collective-permute-start(f32[2,12,64,128]{3,2,1,0:T(8,128)} %pad_maximum_fusion.1), channel_id=1, source_target_pairs={{1,0},{2,1},{3,2},{4,3},{5,4},{6,5},{7,6},{8,7},{9,8},{10,9},{11,1... | collective-permute-start | bytes 2359304 | tf_op jit(solution)/shard_map/ppermute | solution.py:236
  19.7 19.0 %all-to-all-start = ((f32[16,96,128]{2,1,0:T(8,128)}), f32[16,96,128]{2,1,0:T(8,128)S(1)}, u32[]{:S(2)}, u32[]{:S(2)}) async-start(f32[16,96,128]{2,1,0:T(8,128)} %broadcast_in_dim.8), calls=%async_computation | async-start | bytes 1572864 | tf_op jit(solution)/shard_map/all_to_all | solution.py:238
  26.1 12.7 %copy-start.1 = (f32[1,2,16,64,128]{4,3,2,1,0:T(8,128)S(1)}, f32[1,2,16,64,128]{4,3,2,1,0:T(8,128)}, u32[]{:S(2)}) copy-start(f32[1,2,16,64,128]{4,3,2,1,0:T(8,128)} %param.8) | copy-start | bytes 3145732
  26.1 12.6 %copy-start.5 = (s32[1,2]{1,0:T(1,128)S(1)}, s32[1,2]{1,0:T(1,128)}, u32[]{:S(2)}) copy-start(s32[1,2]{1,0:T(1,128)} %cells.9) | copy-start | bytes 28
  38.7 1.0 copy-start.4
  39.8 29.1 %copy-start.3 = (f32[2,8,8,8,128]{4,3,2,1,0:T(8,128)S(1)}, f32[2,8,8,8,128]{4,3,2,1,0:T(8,128)}, u32[]{:S(2)}) copy-start(f32[2,8,8,8,128]{4,3,2,1,0:T(8,128)} %get-tuple-element.37.inj) | copy-start | bytes 1572868
  47.4 16.1 %collective-permute-start.4 = (f32[2,8,8,8,128]{4,3,2,1,0:T(8,128)S(1)}, f32[2,8,8,8,128]{4,3,2,1,0:T(8,128)S(1)}, u32[]{:S(2)}, u32[]{:S(2)}) collective-permute-start(f32[2,8,8,8,128]{4,3,2,1,0:T(8,128)S(1)} %get-tuple-element.19.high), channel_id=1, source_target_pairs={{0,1},{1,2},{2,3},{3,4},{4,5},{5,6},{6,7},{7,8},{8,9},{9,10},{10,1... | collective-permute-start | bytes 1572872 | tf_op jit(solution)/shard_map/ppermute | solution.py:261
  52.6 16.3 %collective-permute-start.5 = (f32[2,8,8,8,128]{4,3,2,1,0:T(8,128)S(1)}, f32[2,8,8,8,128]{4,3,2,1,0:T(8,128)S(1)}, u32[]{:S(2)}, u32[]{:S(2)}) collective-permute-start(f32[2,8,8,8,128]{4,3,2,1,0:T(8,128)S(1)} %get-tuple-element.20.low), channel_id=1, source_target_pairs={{1,0},{2,1},{3,2},{4,3},{5,4},{6,5},{7,6},{8,7},{9,8},{10,9},{11,1... | collective-permute-start | bytes 1572872 | tf_op jit(solution)/shard_map/ppermute | solution.py:262
  68.9 32.7 %copy-start.2 = (f32[2,8,8,8,128]{4,3,2,1,0:T(8,128)S(1)}, f32[2,8,8,8,128]{4,3,2,1,0:T(8,128)}, u32[]{:S(2)}) copy-start(f32[2,8,8,8,128]{4,3,2,1,0:T(8,128)} %get-tuple-element.36.inj) | copy-start | bytes 1572868
  74.6 14.2 %collective-permute-start.6 = (f32[2,8,8,8,128]{4,3,2,1,0:T(8,128)S(1)}, f32[2,8,8,8,128]{4,3,2,1,0:T(8,128)S(1)}, u32[]{:S(2)}, u32[]{:S(2)}) collective-permute-start(f32[2,8,8,8,128]{4,3,2,1,0:T(8,128)S(1)} %get-tuple-element.24.high), channel_id=1, source_target_pairs={{0,1},{1,2},{2,3},{3,4},{4,5},{5,6},{6,7},{7,8},{8,9},{9,10},{10,1... | collective-permute-start | bytes 1572872 | tf_op jit(solution)/shard_map/ppermute | solution.py:261
  76.5 25.1 %collective-permute-start.7 = (f32[2,8,8,8,128]{4,3,2,1,0:T(8,128)S(1)}, f32[2,8,8,8,128]{4,3,2,1,0:T(8,128)S(1)}, u32[]{:S(2)}, u32[]{:S(2)}) collective-permute-start(f32[2,8,8,8,128]{4,3,2,1,0:T(8,128)S(1)} %get-tuple-element.25.low), channel_id=1, source_target_pairs={{1,0},{2,1},{3,2},{4,3},{5,4},{6,5},{7,6},{8,7},{9,8},{10,9},{11,1... | collective-permute-start | bytes 1572872 | tf_op jit(solution)/shard_map/ppermute | solution.py:262
  107.3 14.0 %collective-permute-start.8 = (f32[2,8,8,8,128]{4,3,2,1,0:T(8,128)S(1)}, f32[2,8,8,8,128]{4,3,2,1,0:T(8,128)S(1)}, u32[]{:S(2)}, u32[]{:S(2)}) collective-permute-start(f32[2,8,8,8,128]{4,3,2,1,0:T(8,128)S(1)} %get-tuple-element.28.high), channel_id=1, source_target_pairs={{0,1},{1,2},{2,3},{3,4},{4,5},{5,6},{6,7},{7,8},{8,9},{9,10},{10,1... | collective-permute-start | bytes 1572872 | tf_op jit(solution)/shard_map/ppermute | solution.py:261
  111.0 14.6 %collective-permute-start.9 = (f32[2,8,8,8,128]{4,3,2,1,0:T(8,128)S(1)}, f32[2,8,8,8,128]{4,3,2,1,0:T(8,128)S(1)}, u32[]{:S(2)}, u32[]{:S(2)}) collective-permute-start(f32[2,8,8,8,128]{4,3,2,1,0:T(8,128)S(1)} %get-tuple-element.29.low), channel_id=1, source_target_pairs={{1,0},{2,1},{3,2},{4,3},{5,4},{6,5},{7,6},{8,7},{9,8},{10,9},{11,1... | collective-permute-start | bytes 1572872 | tf_op jit(solution)/shard_map/ppermute | solution.py:262

commit v2 on v1

v2 whole, which is shorter than its diff:
```python
import functools

import jax
import jax.numpy as jnp
from jax import lax
from jax.experimental import pallas as pl
from jax.experimental.pallas import tpu as pltpu
from jax.sharding import PartitionSpec as P

STEPS = 8
PLANES = 16
NX = 64
NY = 128
SCALE = 5040.0
TAPS = (8064.0, -1008.0, 128.0, -9.0)
CENTRE = 3.0 * -14350.0
F32 = jnp.float32
BF16 = jnp.bfloat16
VMEM_LIMIT = 20 * 1024 * 1024


def fill_matrix(mat_ref):
    row = lax.broadcasted_iota(jnp.int32, (2 * NY, NY), 0)
    col = lax.broadcasted_iota(jnp.int32, (2 * NY, NY), 1)
    apart = jnp.abs((row & (NY - 1)) - col)
    out = jnp.zeros((2 * NY, NY), F32)
    for reach, tap in enumerate(TAPS, 1):
        out = jnp.where(apart == reach, tap, out)
    mat_ref[...] = out.astype(BF16)


class Rows:
    def __init__(self, *parts):
        self.parts = parts

    def find(self, plane):
        for ref, first, count in self.parts:
            if first <= plane < first + count:
                return ref, plane - first
        raise ValueError(plane)

    def tile(self, field, plane, j):
        ref, at = self.find(plane)
        return ref[field, at, j]

    def chunk(self, field, plane, count):
        ref, at = self.find(plane)
        return ref[field, pl.ds(at, count)]

    def put(self, field, plane, j, value):
        ref, at = self.find(plane)
        ref[field, at, j] = value


def advance(src, prev, dest, vel, first, mat_ref, part, image, inj):
    for field in range(2):
        rows = src.chunk(field, first, 4).reshape(4 * NX, NY)
        high = rows.astype(BF16)
        low = (rows - high.astype(F32)).astype(BF16)
        both = jnp.concatenate([high, low], axis=1)
        part[field] = jnp.dot(both, mat_ref[...], preferred_element_type=F32).reshape(4, 8, 8, NY)
    sub = lax.broadcasted_iota(jnp.int32, (8, NY), 0)
    top, bottom = sub == 0, sub == 7
    for p in range(4):
        plane = first + p
        imaged = 0 <= plane < PLANES
        tiles = []
        for field in range(2):
            own = [src.tile(field, plane, j) for j in range(8)]
            left = [jnp.where(top, 0.0, pltpu.roll(own[j], 1, 0)) for j in range(4, 8)]
            right = [jnp.where(bottom, 0.0, pltpu.roll(own[j], 7, 0)) for j in range(4)]
            tiles.append(left + own + right)
        for j in range(8):
            speed = vel[plane + 4, j]
            for field in range(2):
                line = tiles[field]
                here = line[j + 4]
                total = CENTRE * here + part[field, p, j]
                for reach, tap in enumerate(TAPS, 1):
                    pair = (line[j + 4 + reach] + line[j + 4 - reach]) + (
                        src.tile(field, plane + reach, j) + src.tile(field, plane - reach, j)
                    )
                    total = total + tap * pair
                change = speed * total
                if field == 1 and 4 <= plane < 12:
                    change = change + inj[plane - 4, j]
                dest.put(field, plane, j, (here + here) - prev.tile(field, plane, j) + change)
                if field == 0 and imaged:
                    image[plane, j] += change * tiles[1][j + 4]


def add_sources(cells, amps, step, dest, dest_plane, image, factors, planes):
    sub = lax.broadcasted_iota(jnp.int32, (8, NY), 0)
    lane = lax.broadcasted_iota(jnp.int32, (8, NY), 1)
    for n in range(cells.shape[1]):
        cell = cells[0, n]
        z, x, y = cell >> 13, (cell >> 7) & (NX - 1), cell & (NY - 1)
        j, s = x & 7, x >> 3
        for ref, ref_plane, lo, hi in factors:
            lo, hi = max(lo, planes[0]), min(hi, planes[1])

            @pl.when((z >= lo) & (z <= hi))
            def _():
                zc = jnp.clip(z, lo, hi)
                amount = jnp.where((sub == s) & (lane == y), amps[0, step, n], 0.0)
                dest[0, zc - dest_plane, j] += amount
                image[zc, j] += amount * ref[1, zc - ref_plane, j]


def half_block(side, first_half, step, now_parts, prev_parts, mids, outs, vel, image, inj, cells, amps, mat_ref, part):
    now, prev = Rows(*now_parts), Rows(*prev_parts)
    mid = Rows(*mids)
    run = functools.partial(advance, vel=vel, mat_ref=mat_ref, image=image)
    if side == 0:
        chunks = (-4, 0, 4, 8) if first_half else (-4, 0)
    else:
        chunks = (4, 8, 12, 16) if first_half else (12, 16)
    for n, lo in enumerate(chunks):
        run(now, prev, mid, first=lo, part=part.at[n % 2], inj=inj.at[0])
    own_mid, own_first, _ = mids[side] if len(mids) == 2 else mids[0]
    if first_half:
        factors = [(ref, first, first, first + count - 1) for ref, first, count in now_parts if 0 <= first < 16]
        add_sources(cells, amps, step, own_mid, own_first, image, factors, (4, 11))
    base = 8 * side
    out = Rows((outs, base, 8))
    for n, lo in enumerate((base, base + 4)):
        run(mid, now, out, first=lo, part=part.at[n % 2], inj=inj.at[1])
    factors = [(ref, first, first, first + count - 1) for ref, first, count in mids]
    planes = (4, 7) if side == 0 else (8, 11)
    factors = [f for f in factors if max(f[2], planes[0]) <= min(f[3], planes[1])]
    add_sources(cells, amps, step + 1, outs, base, image, factors, planes)


def first_half_kernel(side, step, zero_end, cells, amps, beyond, low, high, prev_lo, prev_hi, vel, image_in, inj, mat_ref,
                      out, mid, image, beyond_out, part, *, prev_split):
    del beyond, image_in

    @pl.when(zero_end[0] == 1)
    def _():
        beyond_out[...] = jnp.zeros_like(beyond_out)

    if side == 0:
        now = ((beyond_out, -8, 8), (low, 0, 8), (high, 8, 8))
        mids = ((mid, -4, 16),)
    else:
        now = ((low, 0, 8), (high, 8, 8), (beyond_out, 16, 8))
        mids = ((mid, 4, 16),)
    prev = ((prev_lo, -4, prev_split), (prev_hi, prev_split - 4, 24 - prev_split))
    half_block(side, True, step, now, prev, mids, out, vel, image, inj, cells, amps, mat_ref, part)


def second_half_kernel(side, step, zero_end, cells, amps, beyond, low, high, prev_lo, prev_hi, other_mid, vel, image_in, inj,
                       mat_ref, out, mid, image, beyond_out, part, *, prev_split):
    del beyond, image_in

    @pl.when(zero_end[0] == 1)
    def _():
        beyond_out[...] = jnp.zeros_like(beyond_out)

    if side == 0:
        now = ((beyond_out, -8, 8), (low, 0, 8), (high, 8, 8))
        mids = ((mid, -4, 8), (other_mid, 4, 16))
    else:
        now = ((low, 0, 8), (high, 8, 8), (beyond_out, 16, 8))
        mids = ((other_mid, -4, 16), (mid, 12, 8))
    prev = ((prev_lo, -4, prev_split), (prev_hi, prev_split - 4, 24 - prev_split))
    half_block(side, False, step, now, prev, mids, out, vel, image, inj, cells, amps, mat_ref, part)


def pack_kernel(prev_in, now_in, up_msg, down_msg, low, high, prev, mat_ref):
    fill_matrix(mat_ref)

    def plane(src, field, p, *dests):
        for j in range(8):
            tile = src[pl.ds((field * PLANES + p) * NX + j, 8, stride=8), :]
            for ref, at in dests:
                ref[field, at, j] = tile

    for field in range(2):
        for p in range(8):
            plane(now_in, field, p, (low, p), (down_msg, p))
        for p in range(8):
            plane(now_in, field, 8 + p, (high, p), (up_msg, p))
        for p in range(PLANES):
            more = ((down_msg, 8 + p),) if p < 4 else ((up_msg, p - 4),) if p >= 12 else ()
            plane(prev_in, field, p, (prev, p), *more)


def spread_kernel(below, own, above, out):
    rows = jnp.concatenate([below[...], own[...], above[...]], axis=0)
    for shot in range(16):
        out[pl.ds(shot * 96, 96), :] = rows


def inject_kernel(cells, amps, out):
    count = cells.shape[1]
    cell = cells[...]
    z, x, y = cell >> 13, (cell >> 7) & (NX - 1), cell & (NY - 1)
    row = (z - 4) * NX + (x & 7) * 8 + (x >> 3)
    hit = (lax.broadcasted_iota(jnp.int32, (8 * NX, count), 0) == row).astype(F32).astype(BF16)
    hits = jnp.concatenate([hit, hit, hit], axis=1)
    lane = lax.broadcasted_iota(jnp.int32, (NY, count), 0) == y
    for pair in range(STEPS // 2):
        sides = []
        for step in (2 * pair, 2 * pair + 1):
            amount = amps[0, pl.ds(step, 1), :]
            high = amount.astype(BF16).astype(F32)
            rest = amount - high
            middle = rest.astype(BF16).astype(F32)
            low = rest - middle
            sides.append(jnp.concatenate(
                [jnp.where(lane, part, 0.0).astype(BF16) for part in (high, middle, low)], axis=1))
        both = jnp.concatenate(sides, axis=0)
        dense = lax.dot_general(hits, both, (((1,), (1,)), ((), ())), preferred_element_type=F32)
        for side in range(2):
            out[2 * pair + side] = dense[:, side * NY:(side + 1) * NY].reshape(8, 8, 8, NY)


def open_kernel(ends, gathered, below_msg, above_msg, prev, vel, image, below, above, prev_lo, prev_hi):
    image[...] = jnp.zeros_like(image)
    at_start, at_end = ends[0] == 1, ends[1] == 1

    for p in range(24):
        for j in range(8):
            line = gathered[pl.ds((j // 4) * 96 + p * 4 + j % 4, 8, stride=192), :]
            vel[p, j] = line * line * (1.0 / SCALE)
    below[...] = below_msg[:, :8]
    above[...] = above_msg[:, :8]
    prev_lo[:, 0:4] = below_msg[:, 8:]
    prev_lo[:, 4:12] = prev[:, :8]
    prev_hi[:, 0:8] = prev[:, 8:]
    prev_hi[:, 8:12] = above_msg[:, 8:]

    @pl.when(at_start)
    def _():
        vel[0:4] = jnp.zeros((4, 8, 8, NY), F32)
        prev_lo[:, 0:4] = jnp.zeros((2, 4, 8, 8, NY), F32)

    @pl.when(at_end)
    def _():
        vel[20:24] = jnp.zeros((4, 8, 8, NY), F32)
        prev_hi[:, 8:12] = jnp.zeros((2, 4, 8, 8, NY), F32)


def terms_kernel(image, out):
    for p in range(PLANES):
        for j in range(8):
            out[pl.ds((j // 4) * 64 + p * 4 + j % 4, 8, stride=128), :] = image[p, j]


def close_kernel(mid_lo, mid_hi, low, high, before, after, *, split):
    mid = Rows((mid_lo, -4, split), (mid_hi, split - 4, 24 - split))
    last = Rows((low, 0, 8), (high, 8, 8))
    for field in range(2):
        for p in range(PLANES):
            for j in range(8):
                rows = pl.ds((field * PLANES + p) * NX + j, 8, stride=8)
                before[rows, :] = mid.tile(field, p, j)
                after[rows, :] = last.tile(field, p, j)


def tiles(*lead):
    return jax.ShapeDtypeStruct((*lead, 8, 8, NY), F32)


def rows_of(count):
    return jax.ShapeDtypeStruct((count, NY), F32)


def call(kernel, args, outs, flops, smem=0, scratch=(), aliases=None):
    whole = pl.BlockSpec(memory_space=pltpu.VMEM)
    return pl.pallas_call(
        kernel,
        in_specs=[pl.BlockSpec(memory_space=pltpu.SMEM)] * smem + [whole] * (len(args) - smem),
        out_specs=jax.tree.map(lambda _: whole, outs),
        out_shape=outs,
        scratch_shapes=list(scratch),
        input_output_aliases=aliases or {},
        compiler_params=pltpu.CompilerParams(vmem_limit_bytes=VMEM_LIMIT),
        cost_estimate=pl.CostEstimate(flops=flops, bytes_accessed=1 << 20, transcendentals=0),
    )(*args)


def body(
    velocity, fields_prev, fields_now, source_cells, source_traces, receiver_cells, receiver_traces
):
    slabs, shots = lax.axis_size("slab"), lax.axis_size("shot")
    up = [(i, (i + 1) % slabs) for i in range(slabs)]
    down = [(j, i) for i, j in up]
    slab = lax.axis_index("slab")
    at_start = (slab == 0).astype(jnp.int32).reshape(1)
    at_end = (slab == slabs - 1).astype(jnp.int32).reshape(1)

    vel_rows = velocity.reshape(PLANES * 4, NY)
    vel_below = lax.ppermute(vel_rows[48:], "slab", up)
    vel_above = lax.ppermute(vel_rows[:16], "slab", down)
    half, ext = tiles(2, 8), tiles(2, 24)
    mat = jax.ShapeDtypeStruct((2 * NY, NY), BF16)
    up_msg, down_msg, low, high, prev, mat = call(
        pack_kernel, (fields_prev.reshape(-1, NY), fields_now.reshape(-1, NY)),
        (tiles(2, 12), tiles(2, 12), half, half, tiles(2, 16), mat), 1 << 22)
    below_msg = lax.ppermute(up_msg, "slab", up)
    above_msg = lax.ppermute(down_msg, "slab", down)
    spread = call(spread_kernel, (vel_below, vel_rows, vel_above), rows_of(shots * 96), 1 << 20)
    gathered = lax.all_to_all(spread.reshape(shots, 96, NY), "shot", 0, 0, tiled=True)
    inj = call(inject_kernel, (receiver_cells, receiver_traces), tiles(STEPS, 8), 1 << 27)
    vel, image, below, above, prev_lo, prev_hi = call(
        open_kernel, (jnp.concatenate([at_start, at_end]), gathered.reshape(shots * 96, NY), below_msg, above_msg, prev),
        (tiles(24), tiles(16), half, half, tiles(2, 12), tiles(2, 12)), 1 << 22, smem=1)

    split = 12
    part = [pltpu.VMEM((2, 2, 4, 8, 8, NY), F32)]
    for step in range(0, STEPS, 2):
        order = (1, 0) if step % 4 == 0 else (0, 1)
        news, mids = {}, {}
        for n, side in enumerate(order):
            beyond, flag = (below, at_start) if side == 0 else (above, at_end)
            args = [flag, source_cells, source_traces, beyond, low, high, prev_lo, prev_hi]
            if n == 1:
                args.append(mids[order[0]])
            at = len(args)
            args += [vel, image, inj[step:step + 2], mat]
            kernel = first_half_kernel if n == 0 else second_half_kernel
            news[side], mids[side], image, _ = call(
                functools.partial(kernel, side, step, prev_split=split), args,
                (half, tiles(2, 16 if n == 0 else 8), tiles(16), half), 1 << 26,
                smem=3, scratch=part, aliases={3: 3, at + 1: 2})
            if step < STEPS - 2:
                if side == 1:
                    next_below = lax.ppermute(news[1], "slab", up)
                else:
                    next_above = lax.ppermute(news[0], "slab", down)
        low, high = news[0], news[1]
        prev_lo, prev_hi = mids[0], mids[1]
        split = 16 if order[0] == 0 else 8
        below, above = next_below, next_above

    terms = call(terms_kernel, (image,), rows_of(shots * 64), 1 << 20)
    terms = lax.all_to_all(terms.reshape(shots, 64, NY), "shot", 0, 0, tiled=True)
    before, after = call(
        functools.partial(close_kernel, split=split), (prev_lo, prev_hi, low, high),
        (rows_of(2 * PLANES * NX), rows_of(2 * PLANES * NX)), 1 << 22)
    summed = jnp.sum(terms, axis=0).reshape(velocity.shape)
    gradient = (-2.0 / (shots * STEPS)) * summed / (velocity * velocity * velocity)
    shape = fields_now.shape
    return gradient, before.reshape(shape), after.reshape(shape)


def solution(mesh):
    return jax.shard_map(
        body,
        mesh=mesh,
        in_specs=(
            P("slab", "shot", None),
            P("shot", None, "slab", None, None),
            P("shot", None, "slab", None, None),
            P("shot", "slab"),
            P("shot", None, "slab"),
            P("shot", "slab"),
            P("shot", None, "slab"),
        ),
        out_specs=(
            P("slab", "shot", None),
            P("shot", None, "slab", None, None),
            P("shot", None, "slab", None, None),
        ),
        check_vma=False,
    )
```

time: 148 us -> 132 us (0.89)
  the two profiles are of different devices: /device:TPU:100 before, /device:TPU:1 now
where the time goes in v2:
time: 132 us
  waiting for transfers between devices  59.8 us (45%)
  starting transfers between devices  35.7 us (27%)
  Pallas kernels  28.7 us (22%)
  local copies, waits for them, and re-layouts  6.08 us (5%)
    pallas_call x14, Pallas kernels, call(): pl.pallas_call(kernel, in_specs=[pl.BlockSpec(memory_space=pltpu.SMEM)] *...  28.7 us
    ppermute x3, waiting for transfers between devices, body(): next_below = lax.ppermute(news[1], 'slab', up)  19.9 us
    ppermute x1, waiting for transfers between devices, body(): vel_below = lax.ppermute(vel_rows[48:], 'slab', up)  12.7 us
    all_to_all x1, waiting for transfers between devices, body(): lax.all_to_all(spread.reshape(shots, 96, NY), 'shot', 0, 0, tiled=True)  11.6 us
    ppermute x3, starting transfers between devices, body(): next_above = lax.ppermute(news[0], 'slab', down)  8.91 us
    ppermute x3, waiting for transfers between devices, body(): next_above = lax.ppermute(news[0], 'slab', down)  8.41 us
    all_to_all x1, waiting for transfers between devices, body(): lax.all_to_all(terms.reshape(shots, 64, NY), 'shot', 0, 0, tiled=True)  7.21 us
    all_to_all x1, starting transfers between devices, body(): lax.all_to_all(terms.reshape(shots, 64, NY), 'shot', 0, 0, tiled=True)  6.66 us
  transfers between devices with their start and end apart: 12, of which 7 were waited for; matrix products, arithmetic and copies ran while one was open for 0% of the time, Pallas kernels for 14%

profile of v2, /device:TPU:1, one launch (start us, length us, event | category | flops | bytes accessed | tf_op | source)
XLA Modules:
  0.0 131.9 jit_solution(16565827603956383251)
XLA Ops:
  0.6 1.2 copy-done.2
  1.9 1.2 copy-done.3
  3.1 1.5 %shard_map.95 = (f32[2,12,8,8,128]{4,3,2,1,0:T(8,128)}, f32[2,12,8,8,128]{4,3,2,1,0:T(8,128)}, f32[2,8,8,8,128]{4,3,2,1,0:T(8,128)S(1)}, f32[2,8,8,8,128]{4,3,2,...) custom-call(f32[2048,128]{1,0:T(8,128)S(1)} %bitcast.17, f32[2048,128]{1,0:T(8,128)S(1)} %bitcast.18), custom_call_target="tpu_custom_call" | custom-call | flops 4194304 | bytes 1048576 | tf_op jit(solution)/shard_map/pallas_call | solution.py:272
  5.6 2.5 %collective-permute-start.2 = (f32[2,12,8,8,128]{4,3,2,1,0:T(8,128)}, f32[2,12,8,8,128]{4,3,2,1,0:T(8,128)}, u32[]{:S(2)}, u32[]{:S(2)}) collective-permute-start(f32[2,12,8,8,128]{4,3,2,1,0:T(8,128)} %get-tuple-element.41), channel_id=1, source_target_pairs={{0,1},{1,2},{2,3},{3,4},{4,5},{5,6},{6,7},{7,8},{8,9},{9,10},{10,1... | collective-permute-start | bytes 2359304 | tf_op jit(solution)/shard_map/ppermute | solution.py:302
  8.0 6.4 %collective-permute-start.3 = (f32[2,12,8,8,128]{4,3,2,1,0:T(8,128)}, f32[2,12,8,8,128]{4,3,2,1,0:T(8,128)}, u32[]{:S(2)}, u32[]{:S(2)}) collective-permute-start(f32[2,12,8,8,128]{4,3,2,1,0:T(8,128)} %get-tuple-element.42), channel_id=1, source_target_pairs={{1,0},{2,1},{3,2},{4,3},{5,4},{6,5},{7,6},{8,7},{9,8},{10,9},{11,1... | collective-permute-start | bytes 2359304 | tf_op jit(solution)/shard_map/ppermute | solution.py:303
  14.4 5.1 %collective-permute-start.1 = (f32[16,128]{1,0:T(8,128)S(1)}, f32[16,128]{1,0:T(8,128)S(1)}, u32[]{:S(2)}, u32[]{:S(2)}) collective-permute-start(f32[16,128]{1,0:T(8,128)S(1)} %bitcast.23), channel_id=1, source_target_pairs={{1,0},{2,1},{3,2},{4,3},{5,4},{6,5},{7,6},{8,7},{9,8},{10,9},{11,1... | collective-permute-start | bytes 24584 | tf_op jit(solution)/shard_map/ppermute | solution.py:296
  19.5 12.7 %collective-permute-done.below = f32[16,128]{1,0:T(8,128)S(1)} collective-permute-done((f32[16,128]{1,0:T(8,128)S(1)}, f32[16,128]{1,0:T(8,128)S(1)}, u32[]{:S(2)}, u32[]{:S(2)}) %collective-permute-start) | collective-permute-done | bytes 8224 | tf_op jit(solution)/shard_map/ppermute | solution.py:295
  33.1 5.7 %all-to-all-start = ((f32[16,96,128]{2,1,0:T(8,128)}), f32[16,96,128]{2,1,0:T(8,128)S(1)}, u32[]{:S(2)}, u32[]{:S(2)}) async-start(f32[16,96,128]{2,1,0:T(8,128)} %bitcast.5), calls=%async_computation | async-start | bytes 1572864 | tf_op jit(solution)/shard_map/all_to_all | solution.py:305
  38.9 1.0 shard_map.97
  40.2 11.6 %all-to-all-done = f32[16,96,128]{2,1,0:T(8,128)S(1)} async-done(((f32[16,96,128]{2,1,0:T(8,128)}), f32[16,96,128]{2,1,0:T(8,128)S(1)}, u32[]{:S(2)}, u32[]{:S(2)}) %all-to-all-start) | async-done | bytes 786464 | tf_op jit(solution)/shard_map/all_to_all | solution.py:305
  51.8 1.3 copy-done.5
  53.1 2.1 %shard_map.96 = (f32[24,8,8,128]{3,2,1,0:T(8,128)S(1)}, f32[16,8,8,128]{3,2,1,0:T(8,128)S(1)}, f32[2,8,8,8,128]{4,3,2,1,0:T(8,128)S(1)}, f32[2,8,8,8,128]{4,3,2,...) custom-call(s32[2]{0:T(128)S(1)} %pad_add_fusion.ends, f32[1536,128]{1,0:T(8,128)S(1)} %bitcast.16, ...), custom_call_target="tpu_custom_call" | custom-call | flops 4194304 | bytes 1048576 | tf_op jit(solution)/shard_map/pallas_call | solution.py:272
  55.2 3.0 %shard_map.98 = (f32[2,8,8,8,128]{4,3,2,1,0:T(8,128)S(1)}, f32[2,16,8,8,128]{4,3,2,1,0:T(8,128)S(1)}, f32[16,8,8,128]{3,2,1,0:T(8,128)S(1)}, f32[2,8,8,8,128]{4,3,2,1,0:T(8,128)S(1)}) custom-call(s32[1]{0:T(128)} %bitcast.zero_end, s32[1,2]{1,0:T(1,128)S(1)} %copy-done.9, f32[1,8,2]{2,1,0:T(8,128)S(1)} %copy.33.amps, ...), custom_call_target="tpu_custom_call", output_to_operand_aliasing={{3}: (3, {}), {2}: (9, {})} | custom-call | flops 67108864 | bytes 1048576 | tf_op jit(solution)/shard_map/pallas_call | solution.py:272
  58.3 2.0 %shard_map.99 = (f32[2,8,8,8,128]{4,3,2,1,0:T(8,128)S(1)}, f32[2,8,8,8,128]{4,3,2,1,0:T(8,128)S(1)}, f32[16,8,8,128]{3,2,1,0:T(8,128)S(1)}, f32[2,8,8,8,128]{4,3,2,1,0:T(8,128)S(1)}) custom-call(s32[1]{0:T(128)} %bitcast.1.zero_end, s32[1,2]{1,0:T(1,128)S(1)} %copy-done.9, f32[1,8,2]{2,1,0:T(8,128)S(1)} %copy.33.amps, ...), custom_call_target="tpu_custom_call", output_to_operand_aliasing={{3}: (3, {}), {2}: (10, {})} | custom-call | flops 67108864 | bytes 1048576 | tf_op jit(solution)/shard_map/pallas_call | solution.py:272
  60.3 5.8 %collective-permute-start.4 = (f32[2,8,8,8,128]{4,3,2,1,0:T(8,128)S(1)}, f32[2,8,8,8,128]{4,3,2,1,0:T(8,128)S(1)}, u32[]{:S(2)}, u32[]{:S(2)}) collective-permute-start(f32[2,8,8,8,128]{4,3,2,1,0:T(8,128)S(1)} %get-tuple-element.55.low), channel_id=1, source_target_pairs={{1,0},{2,1},{3,2},{4,3},{5,4},{6,5},{7,6},{8,7},{9,8},{10,9},{11,1... | collective-permute-start | bytes 1572872 | tf_op jit(solution)/shard_map/ppermute | solution.py:332
  66.1 9.3 %collective-permute-done.5.beyond = f32[2,8,8,8,128]{4,3,2,1,0:T(8,128)S(1)} collective-permute-done((f32[2,8,8,8,128]{4,3,2,1,0:T(8,128)S(1)}, f32[2,8,8,8,128]{4,3,2,1,0:T(8,128)S(1)}, u32[]{:S(2)}, u32[]{:S(2)}) %collective-permute-start.5) | collective-permute-done | bytes 524320 | tf_op jit(solution)/shard_map/ppermute | solution.py:330
  75.4 3.1 %shard_map.100 = (f32[2,8,8,8,128]{4,3,2,1,0:T(8,128)S(1)}, f32[2,16,8,8,128]{4,3,2,1,0:T(8,128)S(1)}, f32[16,8,8,128]{3,2,1,0:T(8,128)S(1)}, f32[2,8,8,8,128]{4,3,2,1,0:T(8,128)S(1)}) custom-call(s32[1]{0:T(128)} %bitcast.1.zero_end, s32[1,2]{1,0:T(1,128)S(1)} %copy-done.9, ...), custom_call_target="tpu_custom_call", output_to_operand_aliasing={{3}: (3, {}), {2}: (9, {})} | custom-call | flops 67108864 | bytes 1048576 | tf_op jit(solution)/shard_map/pallas_call | solution.py:272
  78.5 1.2 collective-permute-start.7
  79.7 2.0 %shard_map.101 = (f32[2,8,8,8,128]{4,3,2,1,0:T(8,128)S(1)}, f32[2,8,8,8,128]{4,3,2,1,0:T(8,128)S(1)}, f32[16,8,8,128]{3,2,1,0:T(8,128)S(1)}, f32[2,8,8,8,128]{4,3,2,1,0:T(8,128)S(1)}) custom-call(s32[1]{0:T(128)} %bitcast.zero_end, s32[1,2]{1,0:T(1,128)S(1)} %copy-done.9, f32[1,8,2]{2,1,0:T(8,128)S(1)} %copy.33.amps, ...), custom_call_target="tpu_custom_call", output_to_operand_aliasing={{3}: (3, {}), {2}: (10, {})} | custom-call | flops 67108864 | bytes 1048576 | tf_op jit(solution)/shard_map/pallas_call | solution.py:272
  82.2 8.4 %collective-permute-done.7.beyond = f32[2,8,8,8,128]{4,3,2,1,0:T(8,128)S(1)} collective-permute-done((f32[2,8,8,8,128]{4,3,2,1,0:T(8,128)S(1)}, f32[2,8,8,8,128]{4,3,2,1,0:T(8,128)S(1)}, u32[]{:S(2)}, u32[]{:S(2)}) %collective-permute-start.7) | collective-permute-done | bytes 524320 | tf_op jit(solution)/shard_map/ppermute | solution.py:332
  90.6 3.0 %shard_map.102 = (f32[2,8,8,8,128]{4,3,2,1,0:T(8,128)S(1)}, f32[2,16,8,8,128]{4,3,2,1,0:T(8,128)S(1)}, f32[16,8,8,128]{3,2,1,0:T(8,128)S(1)}, f32[2,8,8,8,128]{4,3,2,1,0:T(8,128)S(1)}) custom-call(s32[1]{0:T(128)} %bitcast.zero_end, s32[1,2]{1,0:T(1,128)S(1)} %copy-done.9, f32[1,8,2]{2,1,0:T(8,128)S(1)} %copy.33.amps, ...), custom_call_target="tpu_custom_call", output_to_operand_aliasing={{3}: (3, {}), {2}: (9, {})} | custom-call | flops 67108864 | bytes 1048576 | tf_op jit(solution)/shard_map/pallas_call | solution.py:272
  93.7 3.2 %collective-permute-done.6.beyond = f32[2,8,8,8,128]{4,3,2,1,0:T(8,128)S(1)} collective-permute-done((f32[2,8,8,8,128]{4,3,2,1,0:T(8,128)S(1)}, f32[2,8,8,8,128]{4,3,2,1,0:T(8,128)S(1)}, u32[]{:S(2)}, u32[]{:S(2)}) %collective-permute-start.6) | collective-permute-done | bytes 524320 | tf_op jit(solution)/shard_map/ppermute | solution.py:330
  96.8 2.0 %shard_map.103 = (f32[2,8,8,8,128]{4,3,2,1,0:T(8,128)S(1)}, f32[2,8,8,8,128]{4,3,2,1,0:T(8,128)S(1)}, f32[16,8,8,128]{3,2,1,0:T(8,128)S(1)}, f32[2,8,8,8,128]{4,3,2,1,0:T(8,128)S(1)}) custom-call(s32[1]{0:T(128)} %bitcast.1.zero_end, s32[1,2]{1,0:T(1,128)S(1)} %copy-done.9, ...), custom_call_target="tpu_custom_call", output_to_operand_aliasing={{3}: (3, {}), {2}: (10, {})} | custom-call | flops 67108864 | bytes 1048576 | tf_op jit(solution)/shard_map/pallas_call | solution.py:272
  98.9 2.0 %collective-permute-start.8 = (f32[2,8,8,8,128]{4,3,2,1,0:T(8,128)S(1)}, f32[2,8,8,8,128]{4,3,2,1,0:T(8,128)S(1)}, u32[]{:S(2)}, u32[]{:S(2)}) collective-permute-start(f32[2,8,8,8,128]{4,3,2,1,0:T(8,128)S(1)} %get-tuple-element.67.low), channel_id=1, source_target_pairs={{1,0},{2,1},{3,2},{4,3},{5,4},{6,5},{7,6},{8,7},{9,8},{10,9},{11,1... | collective-permute-start | bytes 1572872 | tf_op jit(solution)/shard_map/ppermute | solution.py:332
  100.8 7.5 %collective-permute-done.9.beyond = f32[2,8,8,8,128]{4,3,2,1,0:T(8,128)S(1)} collective-permute-done((f32[2,8,8,8,128]{4,3,2,1,0:T(8,128)S(1)}, f32[2,8,8,8,128]{4,3,2,1,0:T(8,128)S(1)}, u32[]{:S(2)}, u32[]{:S(2)}) %collective-permute-start.9) | collective-permute-done | bytes 524320 | tf_op jit(solution)/shard_map/ppermute | solution.py:330
  108.3 3.2 %shard_map.104 = (f32[2,8,8,8,128]{4,3,2,1,0:T(8,128)S(1)}, f32[2,16,8,8,128]{4,3,2,1,0:T(8,128)S(1)}, f32[16,8,8,128]{3,2,1,0:T(8,128)S(1)}, f32[2,8,8,8,128]{4,3,2,1,0:T(8,128)S(1)}) custom-call(s32[1]{0:T(128)} %bitcast.1.zero_end, s32[1,2]{1,0:T(1,128)S(1)} %copy-done.9, ...), custom_call_target="tpu_custom_call", output_to_operand_aliasing={{3}: (3, {}), {2}: (9, {})} | custom-call | flops 67108864 | bytes 1048576 | tf_op jit(solution)/shard_map/pallas_call | solution.py:272
  111.6 2.0 %shard_map.105 = (f32[2,8,8,8,128]{4,3,2,1,0:T(8,128)S(1)}, f32[2,8,8,8,128]{4,3,2,1,0:T(8,128)S(1)}, f32[16,8,8,128]{3,2,1,0:T(8,128)S(1)}, f32[2,8,8,8,128]{4,3,2,1,0:T(8,128)S(1)}) custom-call(s32[1]{0:T(128)} %bitcast.zero_end, s32[1,2]{1,0:T(1,128)S(1)} %copy-done.9, f32[1,8,2]{2,1,0:T(8,128)S(1)} %copy.33.amps, ...), custom_call_target="tpu_custom_call", output_to_operand_aliasing={{3}: (3, {}), {2}: (10, {})} | custom-call | flops 67108864 | bytes 1048576 | tf_op jit(solution)/shard_map/pallas_call | solution.py:272
  113.6 1.1 shard_map.106
  114.7 6.7 %all-to-all-start.1 = ((f32[16,64,128]{2,1,0:T(8,128)}), f32[16,64,128]{2,1,0:T(8,128)S(1)}, u32[]{:S(2)}, u32[]{:S(2)}) async-start(f32[16,64,128]{2,1,0:T(8,128)} %bitcast.9), calls=%async_computation.1 | async-start | bytes 1048576 | tf_op jit(solution)/shard_map/all_to_all | solution.py:339
  121.3 1.0 copy-done.7
  122.4 1.6 %shard_map.107 = (f32[2048,128]{1,0:T(8,128)}, f32[2048,128]{1,0:T(8,128)}) custom-call(f32[2,16,8,8,128]{4,3,2,1,0:T(8,128)S(1)} %get-tuple-element.71.other_mid.mid_lo, f32[2,8,8,8,128]{4,3,2,1,0:T(8,128)S(1)} %copy-done.7, f32[2,8,8,8,128]{4,3,2,1,0:T(8,128)S(1)} %get-tuple-element.75.low, f32[2,8,8,8,128]{4,3,2,1,0:T(8,128)S(1)} %get-tuple-element.76.high), custom_call_target="tpu_custom_call" | custom-call | flops 4194304 | bytes 1048576 | tf_op jit(solution)/shard_map/pallas_call | solution.py:272
  124.0 7.2 %all-to-all-done.1 = f32[16,64,128]{2,1,0:T(8,128)S(1)} async-done(((f32[16,64,128]{2,1,0:T(8,128)}), f32[16,64,128]{2,1,0:T(8,128)S(1)}, u32[]{:S(2)}, u32[]{:S(2)}) %all-to-all-start.1) | async-done | bytes 524320 | tf_op jit(solution)/shard_map/all_to_all | solution.py:339
  (39 shorter events, 3.6 us)
Async XLA Ops:
  0.6 1.2 copy-start.2
  1.9 1.2 copy-start.3
  3.1 11.3 %copy-start.8 = (f32[16,4,128]{2,1,0:T(4,128)S(1)}, f32[16,4,128]{2,1,0:T(4,128)}, u32[]{:S(2)}) copy-start(f32[16,4,128]{2,1,0:T(4,128)} %param.7) | copy-start | bytes 98308
  3.1 35.7 %copy-start.12 = (f32[1,8,2]{1,2,0:T(2,128)S(1)}, f32[1,8,2]{1,2,0:T(2,128)}, u32[]{:S(2)}) copy-start(f32[1,8,2]{1,2,0:T(2,128)} %param.11) | copy-start | bytes 196
  3.1 35.8 %copy-start.10 = (f32[1,8,256]{2,1,0:T(8,128)S(1)}, f32[1,8,256]{2,1,0:T(8,128)}, u32[]{:S(2)}) copy-start(f32[1,8,256]{2,1,0:T(8,128)} %amps.9) | copy-start | bytes 24580
  3.1 35.8 %copy-start.11 = (s32[1,256]{1,0:T(1,128)S(1)}, s32[1,256]{1,0:T(1,128)}, u32[]{:S(2)}) copy-start(s32[1,256]{1,0:T(1,128)} %cells.9) | copy-start | bytes 3076
  4.6 1.0 copy-start.4
  5.6 27.6 %copy-start = (f32[2,8,8,8,128]{4,3,2,1,0:T(8,128)}, f32[2,8,8,8,128]{4,3,2,1,0:T(8,128)S(1)}, u32[]{:S(2)}) copy-start(f32[2,8,8,8,128]{4,3,2,1,0:T(8,128)S(1)} %get-tuple-element.46.high) | copy-start | bytes 1572868
  5.6 46.2 %collective-permute-start.2 = (f32[2,12,8,8,128]{4,3,2,1,0:T(8,128)}, f32[2,12,8,8,128]{4,3,2,1,0:T(8,128)}, u32[]{:S(2)}, u32[]{:S(2)}) collective-permute-start(f32[2,12,8,8,128]{4,3,2,1,0:T(8,128)} %get-tuple-element.41), channel_id=1, source_target_pairs={{0,1},{1,2},{2,3},{3,4},{4,5},{5,6},{6,7},{7,8},{8,9},{9,10},{10,1... | collective-permute-start | bytes 2359304 | tf_op jit(solution)/shard_map/ppermute | solution.py:302
  8.0 43.8 %collective-permute-start.3 = (f32[2,12,8,8,128]{4,3,2,1,0:T(8,128)}, f32[2,12,8,8,128]{4,3,2,1,0:T(8,128)}, u32[]{:S(2)}, u32[]{:S(2)}) collective-permute-start(f32[2,12,8,8,128]{4,3,2,1,0:T(8,128)} %get-tuple-element.42), channel_id=1, source_target_pairs={{1,0},{2,1},{3,2},{4,3},{5,4},{6,5},{7,6},{8,7},{9,8},{10,9},{11,1... | collective-permute-start | bytes 2359304 | tf_op jit(solution)/shard_map/ppermute | solution.py:303
  14.4 17.7 %collective-permute-start = (f32[16,128]{1,0:T(8,128)S(1)}, f32[16,128]{1,0:T(8,128)S(1)}, u32[]{:S(2)}, u32[]{:S(2)}) collective-permute-start(f32[16,128]{1,0:T(8,128)S(1)} %bitcast.24), channel_id=1, source_target_pairs={{0,1},{1,2},{2,3},{3,4},{4,5},{5,6},{6,7},{7,8},{8,9},{9,10},{10,1... | collective-permute-start | bytes 24584 | tf_op jit(solution)/shard_map/ppermute | solution.py:295
  14.4 17.7 %collective-permute-start.1 = (f32[16,128]{1,0:T(8,128)S(1)}, f32[16,128]{1,0:T(8,128)S(1)}, u32[]{:S(2)}, u32[]{:S(2)}) collective-permute-start(f32[16,128]{1,0:T(8,128)S(1)} %bitcast.23), channel_id=1, source_target_pairs={{1,0},{2,1},{3,2},{4,3},{5,4},{6,5},{7,6},{8,7},{9,8},{10,9},{11,1... | collective-permute-start | bytes 24584 | tf_op jit(solution)/shard_map/ppermute | solution.py:296
  33.1 18.6 %all-to-all-start = ((f32[16,96,128]{2,1,0:T(8,128)}), f32[16,96,128]{2,1,0:T(8,128)S(1)}, u32[]{:S(2)}, u32[]{:S(2)}) async-start(f32[16,96,128]{2,1,0:T(8,128)} %bitcast.5), calls=%async_computation | async-start | bytes 1572864 | tf_op jit(solution)/shard_map/all_to_all | solution.py:305
  40.0 15.2 %copy-start.9 = (s32[1,2]{1,0:T(1,128)S(1)}, s32[1,2]{1,0:T(1,128)}, u32[]{:S(2)}) copy-start(s32[1,2]{1,0:T(1,128)} %cells.17) | copy-start | bytes 28
  51.8 3.4 %copy-start.1 = (f32[2,8,8,8,128]{4,3,2,1,0:T(8,128)S(1)}, f32[2,8,8,8,128]{4,3,2,1,0:T(8,128)}, u32[]{:S(2)}) copy-start(f32[2,8,8,8,128]{4,3,2,1,0:T(8,128)} %copy-done) | copy-start | bytes 1572868
  51.8 1.3 copy-start.5
  58.2 17.2 %collective-permute-start.5 = (f32[2,8,8,8,128]{4,3,2,1,0:T(8,128)S(1)}, f32[2,8,8,8,128]{4,3,2,1,0:T(8,128)S(1)}, u32[]{:S(2)}, u32[]{:S(2)}) collective-permute-start(f32[2,8,8,8,128]{4,3,2,1,0:T(8,128)S(1)} %get-tuple-element.56.high), channel_id=1, source_target_pairs={{0,1},{1,2},{2,3},{3,4},{4,5},{5,6},{6,7},{7,8},{8,9},{9,10},{10,1... | collective-permute-start | bytes 1572872 | tf_op jit(solution)/shard_map/ppermute | solution.py:330
  60.3 19.4 %collective-permute-start.4 = (f32[2,8,8,8,128]{4,3,2,1,0:T(8,128)S(1)}, f32[2,8,8,8,128]{4,3,2,1,0:T(8,128)S(1)}, u32[]{:S(2)}, u32[]{:S(2)}) collective-permute-start(f32[2,8,8,8,128]{4,3,2,1,0:T(8,128)S(1)} %get-tuple-element.55.low), channel_id=1, source_target_pairs={{1,0},{2,1},{3,2},{4,3},{5,4},{6,5},{7,6},{8,7},{9,8},{10,9},{11,1... | collective-permute-start | bytes 1572872 | tf_op jit(solution)/shard_map/ppermute | solution.py:332
  78.5 12.0 %collective-permute-start.7 = (f32[2,8,8,8,128]{4,3,2,1,0:T(8,128)S(1)}, f32[2,8,8,8,128]{4,3,2,1,0:T(8,128)S(1)}, u32[]{:S(2)}, u32[]{:S(2)}) collective-permute-start(f32[2,8,8,8,128]{4,3,2,1,0:T(8,128)S(1)} %get-tuple-element.62.low), channel_id=1, source_target_pairs={{1,0},{2,1},{3,2},{4,3},{5,4},{6,5},{7,6},{8,7},{9,8},{10,9},{11,1... | collective-permute-start | bytes 1572872 | tf_op jit(solution)/shard_map/ppermute | solution.py:332
  81.8 15.1 %collective-permute-start.6 = (f32[2,8,8,8,128]{4,3,2,1,0:T(8,128)S(1)}, f32[2,8,8,8,128]{4,3,2,1,0:T(8,128)S(1)}, u32[]{:S(2)}, u32[]{:S(2)}) collective-permute-start(f32[2,8,8,8,128]{4,3,2,1,0:T(8,128)S(1)} %get-tuple-element.61.high), channel_id=1, source_target_pairs={{0,1},{1,2},{2,3},{3,4},{4,5},{5,6},{6,7},{7,8},{8,9},{9,10},{10,1... | collective-permute-start | bytes 1572872 | tf_op jit(solution)/shard_map/ppermute | solution.py:330
  93.6 14.7 %collective-permute-start.9 = (f32[2,8,8,8,128]{4,3,2,1,0:T(8,128)S(1)}, f32[2,8,8,8,128]{4,3,2,1,0:T(8,128)S(1)}, u32[]{:S(2)}, u32[]{:S(2)}) collective-permute-start(f32[2,8,8,8,128]{4,3,2,1,0:T(8,128)S(1)} %get-tuple-element.68.high), channel_id=1, source_target_pairs={{0,1},{1,2},{2,3},{3,4},{4,5},{5,6},{6,7},{7,8},{8,9},{9,10},{10,1... | collective-permute-start | bytes 1572872 | tf_op jit(solution)/shard_map/ppermute | solution.py:330
  98.9 12.7 %collective-permute-start.8 = (f32[2,8,8,8,128]{4,3,2,1,0:T(8,128)S(1)}, f32[2,8,8,8,128]{4,3,2,1,0:T(8,128)S(1)}, u32[]{:S(2)}, u32[]{:S(2)}) collective-permute-start(f32[2,8,8,8,128]{4,3,2,1,0:T(8,128)S(1)} %get-tuple-element.67.low), channel_id=1, source_target_pairs={{1,0},{2,1},{3,2},{4,3},{5,4},{6,5},{7,6},{8,7},{9,8},{10,9},{11,1... | collective-permute-start | bytes 1572872 | tf_op jit(solution)/shard_map/ppermute | solution.py:332
  113.6 1.1 copy-start.6
  114.7 16.5 %all-to-all-start.1 = ((f32[16,64,128]{2,1,0:T(8,128)}), f32[16,64,128]{2,1,0:T(8,128)S(1)}, u32[]{:S(2)}, u32[]{:S(2)}) async-start(f32[16,64,128]{2,1,0:T(8,128)} %bitcast.9), calls=%async_computation.1 | async-start | bytes 1048576 | tf_op jit(solution)/shard_map/all_to_all | solution.py:339
  121.3 1.0 copy-start.7

commit v3 on v0

v3 whole, which is shorter than its diff:
```python
import functools

import jax
import jax.numpy as jnp
from jax import lax
from jax.experimental import pallas as pl
from jax.experimental.pallas import tpu as pltpu
from jax.sharding import PartitionSpec as P

STEPS = 8
PLANES = 16
NX = 64
NY = 128
SCALE = 5040.0
TAPS = (8064.0, -1008.0, 128.0, -9.0)
CENTRE = 3.0 * -14350.0
F32 = jnp.float32
BF16 = jnp.bfloat16
VMEM_LIMIT = 16 * 1024 * 1024


def fill_matrix(mat_ref):
    row = lax.broadcasted_iota(jnp.int32, (2 * NY, NY), 0)
    col = lax.broadcasted_iota(jnp.int32, (2 * NY, NY), 1)
    apart = jnp.abs((row & (NY - 1)) - col)
    out = jnp.zeros((2 * NY, NY), F32)
    for reach, tap in enumerate(TAPS, 1):
        out = jnp.where(apart == reach, tap, out)
    mat_ref[...] = out.astype(BF16)


class Rows:
    def __init__(self, *parts):
        self.parts = parts

    def find(self, plane):
        for ref, first, count in self.parts:
            if first <= plane < first + count:
                return ref, plane - first
        raise ValueError(plane)

    def tile(self, plane, j):
        ref, at = self.find(plane)
        return ref[at, j]

    def chunk(self, plane, count):
        ref, at = self.find(plane)
        return ref[pl.ds(at, count)]

    def put(self, plane, j, value):
        ref, at = self.find(plane)
        ref[at, j] = value


def advance(src, prev, dest, vel, first, mat_ref, part, inj, see):
    rows = src.chunk(first, 4).reshape(4 * NX, NY)
    high = rows.astype(BF16)
    low = (rows - high.astype(F32)).astype(BF16)
    both = jnp.concatenate([high, low], axis=1)
    part[...] = jnp.dot(both, mat_ref[...], preferred_element_type=F32).reshape(4, 8, 8, NY)
    sub = lax.broadcasted_iota(jnp.int32, (8, NY), 0)
    top, bottom = sub == 0, sub == 7
    for p in range(4):
        plane = first + p
        own = [src.tile(plane, j) for j in range(8)]
        left = [jnp.where(top, 0.0, pltpu.roll(own[j], 1, 0)) for j in range(4, 8)]
        right = [jnp.where(bottom, 0.0, pltpu.roll(own[j], 7, 0)) for j in range(4)]
        line = left + own + right
        for j in range(8):
            here = line[j + 4]
            total = CENTRE * here + part[p, j]
            for reach, tap in enumerate(TAPS, 1):
                pair = (line[j + 4 + reach] + line[j + 4 - reach]) + (
                    src.tile(plane + reach, j) + src.tile(plane - reach, j)
                )
                total = total + tap * pair
            change = vel.tile(plane, j) * total
            if 4 <= plane < 12:
                change = change + inj[plane - 4, j]
            dest.put(plane, j, (here + here) - prev.tile(plane, j) + change)
            if 0 <= plane < PLANES:
                see(plane, j, change, here)


class Natural:
    def __init__(self, ref, field):
        self.ref, self.field = ref, field

    def tile(self, plane, j):
        return self.ref[pl.ds((self.field * PLANES + plane) * NX + j, 8, stride=8), :]


def half_kernel(*refs, side, field, now_at, prev_at, vel_at, mid_at, masked, ride, send):
    refs = list(refs)
    take = lambda count: [refs.pop(0) for _ in range(count)]
    rows = lambda some, at: Rows(*[(ref, *where) for ref, where in zip(some, at)])
    keep, mat_ref, inj = take(3)
    vel = rows(take(len(vel_at)), vel_at)
    now_refs = take(len(now_at))
    prev = Natural(take(1)[0], field) if prev_at is None else rows(take(len(prev_at)), prev_at)
    other_mid = take(max(len(mid_at) - 1, 0))
    if field == 1:
        changes, image_in = take(2)
        del image_in
    take(1)
    out, extra = take(2)
    mid = take(1) if mid_at else []
    message = take(1)[0] if send else None
    part, beyond = refs
    if masked:
        beyond = now_refs[0]
    else:
        inside = keep[...] > 0.0
        for p in range(now_at[0][1]):
            for j in range(8):
                beyond[p, j] = jnp.where(inside, now_refs[0][p, j], 0.0)
    now = rows([beyond, *now_refs[1:]], now_at)
    base = 8 * side
    last = Rows((out, base, 8))
    if mid_at:
        mids = rows([*mid, *other_mid], mid_at)
        starts = range(mid_at[0][0], sum(mid_at[0]), 4)
        seen = [p for p in range(mid_at[0][0], sum(mid_at[0])) if 0 <= p < PLANES]

    def see(first):
        def change_out(plane, j, change, here):
            extra[plane - first, j] = change

        def image_out(plane, j, change, here):
            extra[plane, j] += changes[plane - first, j] * here

        return change_out if field == 0 else image_out

    run = functools.partial(advance, vel=vel, mat_ref=mat_ref)
    skip = 0
    if mid_at:
        for n, lo in enumerate(starts):
            run(now, prev, mids, first=lo, part=part.at[n % 2], inj=inj.at[0], see=see(seen[0]))
        now, prev, skip = mids, now, len(seen)
    for n, lo in enumerate((base, base + 4)):
        run(now, prev, last, first=lo, part=part.at[n % 2], inj=inj.at[1 if mid_at else 0], see=see(base - skip))
    border = 12 if side else 0
    for p in range(4):
        for j in range(8):
            if ride:
                out[8 + p, j] = vel.tile(border + p, j)
            if send:
                message[p, j] = out[border - base + p, j]


def edge_kernel(keep, message, out):
    inside = keep[...] > 0.0
    for p in range(4):
        for j in range(8):
            out[p, j] = jnp.where(inside, message[8 + p, j], 0.0)


def pack_kernel(now_in, up_0, down_0, up_1, down_1, low_0, high_0, low_1, high_1, mat_ref):
    fill_matrix(mat_ref)
    for field, (up_msg, down_msg, low, high) in enumerate(((up_0, down_0, low_0, high_0), (up_1, down_1, low_1, high_1))):
        now = Natural(now_in, field)
        for p in range(PLANES):
            for j in range(8):
                tile = now.tile(p, j)
                (high if p >= 8 else low)[p % 8, j] = tile
                if p < 4:
                    down_msg[p, j] = tile
                if p >= 12:
                    up_msg[p - 12, j] = tile


def spread_kernel(own, out):
    for shot in range(16):
        out[pl.ds(shot * 64, 64), :] = own[...]


def dense(cells, amps, step, steps):
    count = cells.shape[1]
    cell = cells[...]
    z, x, y = cell >> 13, (cell >> 7) & (NX - 1), cell & (NY - 1)
    row = (z - 4) * NX + (x & 7) * 8 + (x >> 3)
    hit = (lax.broadcasted_iota(jnp.int32, (8 * NX, count), 0) == row).astype(F32).astype(BF16)
    hits = jnp.concatenate([hit, hit, hit], axis=1)
    lane = lax.broadcasted_iota(jnp.int32, (NY, count), 0) == y
    sides = []
    for at in range(step, step + steps):
        amount = amps[pl.ds(at, 1), :]
        high = amount.astype(BF16).astype(F32)
        rest = amount - high
        middle = rest.astype(BF16).astype(F32)
        low = rest - middle
        sides.append(jnp.concatenate([jnp.where(lane, part, 0.0).astype(BF16) for part in (high, middle, low)], axis=1))
    both = jnp.concatenate(sides, axis=0)
    return lax.dot_general(hits, both, (((1,), (1,)), ((), ())), preferred_element_type=F32)


def inject_kernel(source_cells, source_amps, cells, amps, token, out_0, out_1, *, step, steps):
    del token
    for out, (where, what) in ((out_0, (source_cells, source_amps)), (out_1, (cells, amps))):
        values = dense(where, what, step, steps)
        for side in range(steps):
            out[side] = values[:, side * NY:(side + 1) * NY].reshape(8, 8, 8, NY)


def open_kernel(keep_below, keep_above, gathered, below_0, above_0, below_1, above_1,
                vel, image, below_out_0, above_out_0, below_out_1, above_out_1):
    image[...] = jnp.zeros_like(image)
    for p in range(PLANES):
        for j in range(8):
            line = gathered[pl.ds((j // 4) * 64 + p * 4 + j % 4, 8, stride=128), :]
            vel[p, j] = line * line * (1.0 / SCALE)
    for keep, src, dest in ((keep_below, below_0, below_out_0), (keep_above, above_0, above_out_0),
                            (keep_below, below_1, below_out_1), (keep_above, above_1, above_out_1)):
        inside = keep[...] > 0.0
        for p in range(4):
            for j in range(8):
                dest[p, j] = jnp.where(inside, src[p, j], 0.0)


def terms_kernel(image, velocity, out, factor):
    speed = velocity[...]
    factor[...] = (-2.0 / (16 * STEPS)) / (speed * speed * speed)
    for p in range(PLANES):
        for j in range(8):
            out[pl.ds((j // 4) * 64 + p * 4 + j % 4, 8, stride=128), :] = image[p, j]


def sum_kernel(terms, factor, out):
    total = terms[0:64, :]
    for shot in range(1, 16):
        total = total + terms[pl.ds(64 * shot, 64), :]
    out[...] = total * factor[...]


def close_kernel(before_low_0, before_high_0, low_0, high_0, before_low_1, before_high_1, low_1, high_1, before, after):
    for field, (before_low, before_high, low, high) in enumerate(
            ((before_low_0, before_high_0, low_0, high_0), (before_low_1, before_high_1, low_1, high_1))):
        for p in range(PLANES):
            for j in range(8):
                rows = pl.ds((field * PLANES + p) * NX + j, 8, stride=8)
                before[rows, :] = (before_high if p >= 8 else before_low)[p % 8, j]
                after[rows, :] = (high if p >= 8 else low)[p % 8, j]


def tiles(*lead):
    return jax.ShapeDtypeStruct((*lead, 8, 8, NY), F32)


def rows_of(count):
    return jax.ShapeDtypeStruct((count, NY), F32)


def call(kernel, args, outs, flops, scratch=(), aliases=None):
    whole = pl.BlockSpec(memory_space=pltpu.VMEM)
    return pl.pallas_call(
        kernel,
        in_specs=[whole] * len(args),
        out_specs=jax.tree.map(lambda _: whole, outs),
        out_shape=outs,
        scratch_shapes=list(scratch),
        input_output_aliases=aliases or {},
        compiler_params=pltpu.CompilerParams(vmem_limit_bytes=VMEM_LIMIT),
        cost_estimate=pl.CostEstimate(flops=flops, bytes_accessed=1 << 20, transcendentals=0),
    )(*args)


def body(
    velocity, fields_prev, fields_now, source_cells, source_traces, receiver_cells, receiver_traces
):
    slabs, shots = lax.axis_size("slab"), lax.axis_size("shot")
    up = [(i, (i + 1) % slabs) for i in range(slabs)]
    down = [(j, i) for i, j in up]
    slab = lax.axis_index("slab")
    keep = [jnp.full((8, NY), slab > 0, F32), jnp.full((8, NY), slab < slabs - 1, F32)]

    vel_rows = velocity.reshape(PLANES * 4, NY)
    spread = call(spread_kernel, (vel_rows,), rows_of(shots * 64), 1 << 20)
    gathered = lax.all_to_all(spread.reshape(shots, 64, NY), "shot", 0, 0, tiled=True)
    half, quarter = tiles(8), tiles(4)
    mat = jax.ShapeDtypeStruct((2 * NY, NY), BF16)
    up_0, down_0, up_1, down_1, low_0, high_0, low_1, high_1, mat = call(
        pack_kernel, (fields_now.reshape(-1, NY),), (*[quarter] * 4, *[half] * 4, mat), 1 << 22)
    now = [[low_0, high_0], [low_1, high_1]]
    arrived = [lax.ppermute(a, "slab", way) for a, way in ((up_0, up), (down_0, down), (up_1, up), (down_1, down))]
    few = 128 - source_cells.shape[1]
    marks = (
        jnp.pad(source_cells, ((0, 0), (0, few)), constant_values=4 * NX * NY),
        jnp.pad(source_traces[0], ((0, 0), (0, few))),
        receiver_cells, receiver_traces[0],
    )
    vel, image, *far = call(
        open_kernel, (*keep, gathered.reshape(shots * 64, NY), *arrived), (tiles(16), tiles(16), *[quarter] * 4), 1 << 22)
    beyond = [far[:2], far[2:]]
    vels = [[(vel, (0, 16))], [(vel, (0, 16))]]
    prev_rows = fields_prev.reshape(-1, NY)

    lengths = (1, 2, 2, 2, 1)
    token, step, prev = image, 0, None
    for block, length in enumerate(lengths):
        final = block == len(lengths) - 1
        to_send = 0 if final else 4 * lengths[block + 1]
        order = (1, 0) if block % 2 == 0 else (0, 1)
        news, mids, sent = ([[None, None], [None, None]] for _ in range(3))
        changes = [None, None]
        inj = call(functools.partial(inject_kernel, step=step, steps=length),
                   (*marks, mat if block == 0 else token), (tiles(length, 8), tiles(length, 8)), 1 << 24)
        for field in range(2):
            for n, side in enumerate(order):
                first = block == 0
                if block == 1 and field == 0:
                    edge = call(edge_kernel, (keep[side], beyond[0][side]), quarter, 1 << 16)
                    vels[side] = [(vel, (0, 16)), (edge, (16 if side else -4, 4))]
                reach = 4 * length
                now_list = [(beyond[field][side], (16 if side else -reach, reach)), (now[field][0], (0, 8)), (now[field][1], (8, 8))]
                prev_list = [(prev_rows, None)] if first else prev[field]
                mid_list = []
                if length == 2:
                    mid_at = (4, 16) if side and n == 0 else (-4, 16) if n == 0 else (12, 8) if side else (-4, 8)
                    mid_list = [(None, mid_at)] + ([mids[field][order[0]]] if n == 1 else [])
                args = [keep[side], mat, inj[field]] + [a for a, _ in vels[side]]
                args += [a for a, _ in now_list] + [a for a, _ in prev_list] + [a for a, _ in mid_list[1:]]
                aliases = {}
                if field == 1:
                    args += [changes[side], image]
                    aliases = {len(args) - 1: 1}
                args.append(token)
                seen = (12 if n == 0 else 4) if length == 2 else 0
                ride = first and field == 0
                send = to_send == 4
                outs = [tiles(12) if ride else half, tiles(seen + 8) if field == 0 else tiles(16)]
                if length == 2:
                    outs.append(tiles(mid_at[1]))
                if send:
                    outs.append(quarter)
                out, extra, *rest = call(
                    functools.partial(
                        half_kernel, side=side, field=field, now_at=[at for _, at in now_list],
                        prev_at=None if first else [at for _, at in prev_list], vel_at=[at for _, at in vels[side]],
                        mid_at=[at for _, at in mid_list], masked=first, ride=ride, send=send),
                    args, outs, 1 << 25,
                    scratch=(pltpu.VMEM((2, 4, 8, 8, NY), F32), pltpu.VMEM((8, 8, 8, NY), F32)), aliases=aliases)
                token = out
                news[field][side] = out
                if length == 2:
                    mids[field][side] = (rest[0], mid_at)
                if field == 0:
                    changes[side] = extra
                else:
                    image = extra
                if not final:
                    sent[field][1 - side] = lax.ppermute(rest[-1] if send else out, "slab", up if side else down)
        if first:
            prev = [[(a, (0, 8)), (b, (8, 8)), (beyond[f][0], (-4, 4)), (beyond[f][1], (16, 4))] for f, (a, b) in enumerate(now)]
        else:
            prev = mids
        before_last, now, beyond = now, news, sent
        step += length

    terms, factor = call(terms_kernel, (image, vel_rows), (rows_of(shots * 64), rows_of(64)), 1 << 20)
    terms = lax.all_to_all(terms.reshape(shots, 64, NY), "shot", 0, 0, tiled=True)
    args = []
    for field in range(2):
        args += [*before_last[field], *now[field]]
    before, after = call(close_kernel, args, (rows_of(2 * PLANES * NX), rows_of(2 * PLANES * NX)), 1 << 22)
    gradient = call(sum_kernel, (terms.reshape(shots * 64, NY), factor), rows_of(64), 1 << 18).reshape(velocity.shape)
    shape = fields_now.shape
    return gradient, before.reshape(shape), after.reshape(shape)


def solution(mesh):
    return jax.shard_map(
        body,
        mesh=mesh,
        in_specs=(
            P("slab", "shot", None),
            P("shot", None, "slab", None, None),
            P("shot", None, "slab", None, None),
            P("shot", "slab"),
            P("shot", None, "slab"),
            P("shot", "slab"),
            P("shot", None, "slab"),
        ),
        out_specs=(
            P("slab", "shot", None),
            P("shot", None, "slab", None, None),
            P("shot", None, "slab", None, None),
        ),
        check_vma=False,
    )
```

time: 338 us -> 110 us (0.33)
  waiting for transfers between devices: 172 us -> 20.2 us
  other arithmetic: 66.9 us -> 0 us
  blocking collectives: 28.7 us -> 0 us
  Pallas kernels: 0 us -> 22.8 us
  between operations: 14.8 us -> 0.95 us
  starting transfers between devices: 47.9 us -> 61.2 us
    psum x1 -> x0, waiting for transfers between devices: 147 us -> none  [body(): summed = lax.psum(imaging, 'shot')]
    scatter-add x16 -> x0, other arithmetic: 30.3 us -> none  [the longest x8 18.9 us: inject(): adjoint_row = flattened[1].at[receiver_index].add(receiver_amps)]
    all_gather x1 -> x0, blocking collectives: 28.7 us -> none  [body(): courant = lax.all_gather(velocity, 'shot', axis=1, tiled=True)]
    add x9 -> x0, other arithmetic: 25.5 us -> none  [the longest x8 20.7 us: body(): 2.0 * present_mid - earlier_mid + courant * courant * laplacian(extended)]
    pallas_call x0 -> x33, Pallas kernels: none -> 22.8 us  [call(): pl.pallas_call(kernel, in_specs=[whole] * len(args), out_specs=jax.tree.m...]
    all_to_all x0 -> x2, starting transfers between devices: none -> 18.7 us  [the longest x1 11.8 us: body(): lax.all_to_all(terms.reshape(shots, 64, NY), 'shot', 0, 0, tiled=True)]
    ppermute x16 -> x20, waiting for transfers between devices: 25.1 us -> 12 us  [the longest x16 11.1 us: body(): lax.ppermute(rest[-1] if send else out, 'slab', up if side else down)]
    all_to_all x0 -> x2, waiting for transfers between devices: none -> 8.17 us  [the longest x1 8.17 us: body(): lax.all_to_all(terms.reshape(shots, 64, NY), 'shot', 0, 0, tiled=True)]
  transfers between devices with their start and end apart: 17 -> 22, of which waited for: 15 -> 9; matrix products, arithmetic and copies ran while one was open for 2% -> 0% of each run, Pallas kernels for 0% -> 16%
where the time goes in v3:
time: 110 us
  starting transfers between devices  61.2 us (56%)
  Pallas kernels  22.8 us (21%)
  waiting for transfers between devices  20.2 us (18%)
  local copies, waits for them, and re-layouts  4.41 us (4%)
    ppermute x16, starting transfers between devices, body(): lax.ppermute(rest[-1] if send else out, 'slab', up if side else down)  29.6 us
    pallas_call x33, Pallas kernels, call(): pl.pallas_call(kernel, in_specs=[whole] * len(args), out_specs=jax.tree.m...  22.8 us
    ppermute x4, starting transfers between devices, body(): lax.ppermute(a, 'slab', way)  12.8 us
    all_to_all x1, starting transfers between devices, body(): lax.all_to_all(terms.reshape(shots, 64, NY), 'shot', 0, 0, tiled=True)  11.8 us
    ppermute x16, waiting for transfers between devices, body(): lax.ppermute(rest[-1] if send else out, 'slab', up if side else down)  11.1 us
    all_to_all x1, waiting for transfers between devices, body(): lax.all_to_all(terms.reshape(shots, 64, NY), 'shot', 0, 0, tiled=True)  8.17 us
    all_to_all x1, starting transfers between devices, body(): lax.all_to_all(spread.reshape(shots, 64, NY), 'shot', 0, 0, tiled=True)  6.91 us
    unnamed x16, local copies, waits for them, and re-layouts  4.31 us
  transfers between devices with their start and end apart: 22, of which 9 were waited for; matrix products, arithmetic and copies ran while one was open for 0% of the time, Pallas kernels for 16%

profile of v3, /device:TPU:1, one launch (start us, length us, event | category | flops | bytes accessed | tf_op | source)
XLA Modules:
  0.0 109.5 jit_solution(16034029790403981997)
XLA Ops:
  1.4 0.8 shard_map.96
  2.2 6.9 %all-to-all-start = ((f32[16,64,128]{2,1,0:T(8,128)}), f32[16,64,128]{2,1,0:T(8,128)S(1)}, u32[]{:S(2)}, u32[]{:S(2)}) async-start(f32[16,64,128]{2,1,0:T(8,128)} %bitcast.4), calls=%async_computation | async-start | bytes 1048576 | tf_op jit(solution)/shard_map/all_to_all | solution.py:278
  9.1 1.2 %copy-done.1 = f32[1,2,16,64,128]{4,3,2,1,0:T(8,128)S(1)} copy-done((f32[1,2,16,64,128]{4,3,2,1,0:T(8,128)S(1)}, f32[1,2,16,64,128]{4,3,2,1,0:T(8,128)}, u32[]{:S(2)}) %copy-start.1) | copy-done | bytes 1048600
  10.4 0.9 shard_map.94
  11.2 1.7 %collective-permute-start = (f32[4,8,8,128]{3,2,1,0:T(8,128)}, f32[4,8,8,128]{3,2,1,0:T(8,128)S(1)}, u32[]{:S(2)}, u32[]{:S(2)}) collective-permute-start(f32[4,8,8,128]{3,2,1,0:T(8,128)} %get-tuple-element.90), channel_id=1, source_target_pairs={{0,1},{1,2},{2,3},{3,4},{4,5},{5,6},{6,7},{7,8},{8,9},{9,10},{10,1... | collective-permute-start | bytes 393224 | tf_op jit(solution)/shard_map/ppermute | solution.py:284
  12.9 6.1 %collective-permute-start.1 = (f32[4,8,8,128]{3,2,1,0:T(8,128)}, f32[4,8,8,128]{3,2,1,0:T(8,128)S(1)}, u32[]{:S(2)}, u32[]{:S(2)}) collective-permute-start(f32[4,8,8,128]{3,2,1,0:T(8,128)} %get-tuple-element.91), channel_id=1, source_target_pairs={{1,0},{2,1},{3,2},{4,3},{5,4},{6,5},{7,6},{8,7},{9,8},{10,9},{11,1... | collective-permute-start | bytes 393224 | tf_op jit(solution)/shard_map/ppermute | solution.py:284
  19.0 5.1 %collective-permute-start.3 = (f32[4,8,8,128]{3,2,1,0:T(8,128)}, f32[4,8,8,128]{3,2,1,0:T(8,128)}, u32[]{:S(2)}, u32[]{:S(2)}) collective-permute-start(f32[4,8,8,128]{3,2,1,0:T(8,128)} %get-tuple-element.93), channel_id=1, source_target_pairs={{1,0},{2,1},{3,2},{4,3},{5,4},{6,5},{7,6},{8,7},{9,8},{10,9},{11,1... | collective-permute-start | bytes 393224 | tf_op jit(solution)/shard_map/ppermute | solution.py:284
  26.7 1.0 collective-permute-done.2.below_1
  27.7 1.4 %shard_map.97 = (f32[16,8,8,128]{3,2,1,0:T(8,128)S(1)}, f32[16,8,8,128]{3,2,1,0:T(8,128)S(1)}, f32[4,8,8,128]{3,2,1,0:T(8,128)S(1)}, f32[4,8,8,128]{3,2,1,0:T(8,...) custom-call(f32[8,128]{1,0:T(8,128)S(1)} %broadcast_in_dim.6.keep_below.refs_0_.keep, ...), custom_call_target="tpu_custom_call" | custom-call | flops 4194304 | bytes 1048576 | tf_op jit(solution)/shard_map/pallas_call | solution.py:255
  30.0 5.1 %collective-permute-start.4 = (f32[12,8,8,128]{3,2,1,0:T(8,128)S(1)}, f32[12,8,8,128]{3,2,1,0:T(8,128)S(1)}, u32[]{:S(2)}, u32[]{:S(2)}) collective-permute-start(f32[12,8,8,128]{3,2,1,0:T(8,128)S(1)} %get-tuple-element.108.refs_10_.refs_6_), channel_id=1, source_target_pairs={{1,0},{2,1},{3,2},{4,3},{5,4},{6,5},{7,6},{8,7},{9,8},{10,9},{11,1... | collective-permute-start | bytes 1179656 | tf_op jit(solution)/shard_map/ppermute | solution.py:351
  36.1 5.1 %collective-permute-start.5 = (f32[8,8,8,128]{3,2,1,0:T(8,128)S(1)}, f32[8,8,8,128]{3,2,1,0:T(8,128)S(1)}, u32[]{:S(2)}, u32[]{:S(2)}) collective-permute-start(f32[8,8,8,128]{3,2,1,0:T(8,128)S(1)} %get-tuple-element.111.token.refs_12_.refs_6_), channel_id=1, source_target_pairs={{1,0},{2,1},{3,2},{4,3},{5,4},{6,5},{7,6},{8,7},{9,8},{10,9},{11,1... | collective-permute-start | bytes 786440 | tf_op jit(solution)/shard_map/ppermute | solution.py:351
  41.8 0.8 collective-permute-done.6.message.refs_5_
  42.6 1.0 shard_map.105
  43.6 0.9 collective-permute-start.10
  45.2 0.9 collective-permute-start.11
  46.1 2.1 %collective-permute-done.7.refs_5_ = f32[8,8,8,128]{3,2,1,0:T(8,128)S(1)} collective-permute-done((f32[8,8,8,128]{3,2,1,0:T(8,128)S(1)}, f32[8,8,8,128]{3,2,1,0:T(8,128)S(1)}, u32[]{:S(2)}, u32[]{:S(2)}) %collective-permute-start.7) | collective-permute-done | bytes 262176 | tf_op jit(solution)/shard_map/ppermute | solution.py:351
  48.2 1.0 shard_map.107
  49.3 2.4 %collective-permute-start.9 = (f32[8,8,8,128]{3,2,1,0:T(8,128)S(1)}, f32[8,8,8,128]{3,2,1,0:T(8,128)S(1)}, u32[]{:S(2)}, u32[]{:S(2)}) collective-permute-start(f32[8,8,8,128]{3,2,1,0:T(8,128)S(1)} %get-tuple-element.122.refs_15_.refs_6_), channel_id=1, source_target_pairs={{1,0},{2,1},{3,2},{4,3},{5,4},{6,5},{7,6},{8,7},{9,8},{10,9},{11,1... | collective-permute-start | bytes 786440 | tf_op jit(solution)/shard_map/ppermute | solution.py:351
  53.3 1.0 shard_map.110
  55.1 5.9 %collective-permute-start.15 = (f32[8,8,8,128]{3,2,1,0:T(8,128)S(1)}, f32[8,8,8,128]{3,2,1,0:T(8,128)S(1)}, u32[]{:S(2)}, u32[]{:S(2)}) collective-permute-start(f32[8,8,8,128]{3,2,1,0:T(8,128)S(1)} %get-tuple-element.132.refs_12_.refs_6_), channel_id=1, source_target_pairs={{1,0},{2,1},{3,2},{4,3},{5,4},{6,5},{7,6},{8,7},{9,8},{10,9},{11,1... | collective-permute-start | bytes 786440 | tf_op jit(solution)/shard_map/ppermute | solution.py:351
  61.0 1.0 shard_map.112
  63.0 5.0 %collective-permute-start.12 = (f32[8,8,8,128]{3,2,1,0:T(8,128)S(1)}, f32[8,8,8,128]{3,2,1,0:T(8,128)S(1)}, u32[]{:S(2)}, u32[]{:S(2)}) collective-permute-start(f32[8,8,8,128]{3,2,1,0:T(8,128)S(1)} %get-tuple-element.137.token.refs_10_.refs_6_), channel_id=1, source_target_pairs={{1,0},{2,1},{3,2},{4,3},{5,4},{6,5},{7,6},{8,7},{9,8},{10,9},{11,1... | collective-permute-start | bytes 786440 | tf_op jit(solution)/shard_map/ppermute | solution.py:351
  68.6 1.0 shard_map.115
  70.6 1.5 %collective-permute-start.17 = (f32[4,8,8,128]{3,2,1,0:T(8,128)S(1)}, f32[4,8,8,128]{3,2,1,0:T(8,128)S(1)}, u32[]{:S(2)}, u32[]{:S(2)}) collective-permute-start(f32[4,8,8,128]{3,2,1,0:T(8,128)S(1)} %get-tuple-element.156), channel_id=1, source_target_pairs={{0,1},{1,2},{2,3},{3,4},{4,5},{5,6},{6,7},{7,8},{8,9},{9,10},{10,1... | collective-permute-start | bytes 393224 | tf_op jit(solution)/shard_map/ppermute | solution.py:351
  72.1 1.7 %collective-permute-done.13.refs_5_ = f32[8,8,8,128]{3,2,1,0:T(8,128)S(1)} collective-permute-done((f32[8,8,8,128]{3,2,1,0:T(8,128)S(1)}, f32[8,8,8,128]{3,2,1,0:T(8,128)S(1)}, u32[]{:S(2)}, u32[]{:S(2)}) %collective-permute-start.13) | collective-permute-done | bytes 262176 | tf_op jit(solution)/shard_map/ppermute | solution.py:351
  73.8 1.0 shard_map.117
  74.9 2.0 %collective-permute-start.19 = (f32[4,8,8,128]{3,2,1,0:T(8,128)S(1)}, f32[4,8,8,128]{3,2,1,0:T(8,128)S(1)}, u32[]{:S(2)}, u32[]{:S(2)}) collective-permute-start(f32[4,8,8,128]{3,2,1,0:T(8,128)S(1)} %get-tuple-element.161), channel_id=1, source_target_pairs={{1,0},{2,1},{3,2},{4,3},{5,4},{6,5},{7,6},{8,7},{9,8},{10,9},{11,1... | collective-permute-start | bytes 393224 | tf_op jit(solution)/shard_map/ppermute | solution.py:351
  80.2 5.3 %collective-permute-done.16.refs_5_ = f32[4,8,8,128]{3,2,1,0:T(8,128)S(1)} collective-permute-done((f32[4,8,8,128]{3,2,1,0:T(8,128)S(1)}, f32[4,8,8,128]{3,2,1,0:T(8,128)S(1)}, u32[]{:S(2)}, u32[]{:S(2)}) %collective-permute-start.16) | collective-permute-done | bytes 131104 | tf_op jit(solution)/shard_map/ppermute | solution.py:351
  86.2 1.1 %shard_map.124 = (f32[1024,128]{1,0:T(8,128)}, f32[64,128]{1,0:T(8,128)S(1)}) custom-call(f32[16,8,8,128]{3,2,1,0:T(8,128)S(1)} %get-tuple-element.167.image, f32[64,128]{1,0:T(8,128)S(1)} %bitcast.25), custom_call_target="tpu_custom_call" | custom-call | flops 1048576 | bytes 1048576 | tf_op jit(solution)/shard_map/pallas_call | solution.py:255
  87.3 11.8 %all-to-all-start.1 = ((f32[16,64,128]{2,1,0:T(8,128)}), f32[16,64,128]{2,1,0:T(8,128)S(1)}, u32[]{:S(2)}, u32[]{:S(2)}) async-start(f32[16,64,128]{2,1,0:T(8,128)} %bitcast.7), calls=%async_computation.1 | async-start | bytes 1048576 | tf_op jit(solution)/shard_map/all_to_all | solution.py:360
  99.1 1.6 %shard_map.126 = (f32[2048,128]{1,0:T(8,128)}, f32[2048,128]{1,0:T(8,128)}) custom-call(f32[8,8,8,128]{3,2,1,0:T(8,128)S(1)} %get-tuple-element.145.refs_11_.refs_6_.before_low_0, f32[8,8,8,128]{3,2,1,0:T(8,128)S(1)} %get-tuple-element.146.refs_12_.refs_7_.before_high_0, f32[8,8,8,128]{3,2,1,0:T(8,128)S(1)} %get-tuple-element.164.refs_12_.low_0, ...), custom_call_target="tpu_custom_call" | custom-call | flops 4194304 | bytes 1048576 | tf_op jit(solution)/shard_map/pallas_call | solution.py:255
  100.7 8.2 %all-to-all-done.1 = f32[16,64,128]{2,1,0:T(8,128)S(1)} async-done(((f32[16,64,128]{2,1,0:T(8,128)}), f32[16,64,128]{2,1,0:T(8,128)S(1)}, u32[]{:S(2)}, u32[]{:S(2)}) %all-to-all-start.1) | async-done | bytes 524320 | tf_op jit(solution)/shard_map/all_to_all | solution.py:360
  (66 shorter events, 16.1 us)
Async XLA Ops:
  0.6 0.8 copy-start.3
  2.2 25.4 %all-to-all-start = ((f32[16,64,128]{2,1,0:T(8,128)}), f32[16,64,128]{2,1,0:T(8,128)S(1)}, u32[]{:S(2)}, u32[]{:S(2)}) async-start(f32[16,64,128]{2,1,0:T(8,128)} %bitcast.4), calls=%async_computation | async-start | bytes 1048576 | tf_op jit(solution)/shard_map/all_to_all | solution.py:278
  9.1 1.2 %copy-start.1 = (f32[1,2,16,64,128]{4,3,2,1,0:T(8,128)S(1)}, f32[1,2,16,64,128]{4,3,2,1,0:T(8,128)}, u32[]{:S(2)}) copy-start(f32[1,2,16,64,128]{4,3,2,1,0:T(8,128)} %param.9) | copy-start | bytes 3145732
  10.4 18.7 %copy-start = (f32[1,2,16,64,128]{4,3,2,1,0:T(8,128)S(1)}, f32[1,2,16,64,128]{4,3,2,1,0:T(8,128)}, u32[]{:S(2)}) copy-start(f32[1,2,16,64,128]{4,3,2,1,0:T(8,128)} %param.8) | copy-start | bytes 3145732
  11.2 15.4 %collective-permute-start = (f32[4,8,8,128]{3,2,1,0:T(8,128)}, f32[4,8,8,128]{3,2,1,0:T(8,128)S(1)}, u32[]{:S(2)}, u32[]{:S(2)}) collective-permute-start(f32[4,8,8,128]{3,2,1,0:T(8,128)} %get-tuple-element.90), channel_id=1, source_target_pairs={{0,1},{1,2},{2,3},{3,4},{4,5},{5,6},{6,7},{7,8},{8,9},{9,10},{10,1... | collective-permute-start | bytes 393224 | tf_op jit(solution)/shard_map/ppermute | solution.py:284
  12.9 13.8 %collective-permute-start.1 = (f32[4,8,8,128]{3,2,1,0:T(8,128)}, f32[4,8,8,128]{3,2,1,0:T(8,128)S(1)}, u32[]{:S(2)}, u32[]{:S(2)}) collective-permute-start(f32[4,8,8,128]{3,2,1,0:T(8,128)} %get-tuple-element.91), channel_id=1, source_target_pairs={{1,0},{2,1},{3,2},{4,3},{5,4},{6,5},{7,6},{8,7},{9,8},{10,9},{11,1... | collective-permute-start | bytes 393224 | tf_op jit(solution)/shard_map/ppermute | solution.py:284
  19.0 8.7 %collective-permute-start.2 = (f32[4,8,8,128]{3,2,1,0:T(8,128)}, f32[4,8,8,128]{3,2,1,0:T(8,128)}, u32[]{:S(2)}, u32[]{:S(2)}) collective-permute-start(f32[4,8,8,128]{3,2,1,0:T(8,128)} %get-tuple-element.92), channel_id=1, source_target_pairs={{0,1},{1,2},{2,3},{3,4},{4,5},{5,6},{6,7},{7,8},{8,9},{9,10},{10,1... | collective-permute-start | bytes 393224 | tf_op jit(solution)/shard_map/ppermute | solution.py:284
  19.0 8.7 %collective-permute-start.3 = (f32[4,8,8,128]{3,2,1,0:T(8,128)}, f32[4,8,8,128]{3,2,1,0:T(8,128)}, u32[]{:S(2)}, u32[]{:S(2)}) collective-permute-start(f32[4,8,8,128]{3,2,1,0:T(8,128)} %get-tuple-element.93), channel_id=1, source_target_pairs={{1,0},{2,1},{3,2},{4,3},{5,4},{6,5},{7,6},{8,7},{9,8},{10,9},{11,1... | collective-permute-start | bytes 393224 | tf_op jit(solution)/shard_map/ppermute | solution.py:284
  24.1 0.7 copy-start.6
  24.8 0.7 copy-start.7
  24.9 0.7 copy-start.2
  25.5 0.7 copy-start.5
  29.5 13.1 %collective-permute-start.6 = (f32[12,8,8,128]{3,2,1,0:T(8,128)S(1)}, f32[12,8,8,128]{3,2,1,0:T(8,128)S(1)}, u32[]{:S(2)}, u32[]{:S(2)}) collective-permute-start(f32[12,8,8,128]{3,2,1,0:T(8,128)S(1)} %get-tuple-element.104.refs_8_.refs_7_), channel_id=1, source_target_pairs={{0,1},{1,2},{2,3},{3,4},{4,5},{5,6},{6,7},{7,8},{8,9},{9,10},{10,1... | collective-permute-start | bytes 1179656 | tf_op jit(solution)/shard_map/ppermute | solution.py:351
  30.0 14.5 %collective-permute-start.4 = (f32[12,8,8,128]{3,2,1,0:T(8,128)S(1)}, f32[12,8,8,128]{3,2,1,0:T(8,128)S(1)}, u32[]{:S(2)}, u32[]{:S(2)}) collective-permute-start(f32[12,8,8,128]{3,2,1,0:T(8,128)S(1)} %get-tuple-element.108.refs_10_.refs_6_), channel_id=1, source_target_pairs={{1,0},{2,1},{3,2},{4,3},{5,4},{6,5},{7,6},{8,7},{9,8},{10,9},{11,1... | collective-permute-start | bytes 1179656 | tf_op jit(solution)/shard_map/ppermute | solution.py:351
  35.6 12.6 %collective-permute-start.7 = (f32[8,8,8,128]{3,2,1,0:T(8,128)S(1)}, f32[8,8,8,128]{3,2,1,0:T(8,128)S(1)}, u32[]{:S(2)}, u32[]{:S(2)}) collective-permute-start(f32[8,8,8,128]{3,2,1,0:T(8,128)S(1)} %get-tuple-element.110.refs_10_.refs_7_), channel_id=1, source_target_pairs={{0,1},{1,2},{2,3},{3,4},{4,5},{5,6},{6,7},{7,8},{8,9},{9,10},{10,1... | collective-permute-start | bytes 786440 | tf_op jit(solution)/shard_map/ppermute | solution.py:351
  36.1 15.6 %collective-permute-start.5 = (f32[8,8,8,128]{3,2,1,0:T(8,128)S(1)}, f32[8,8,8,128]{3,2,1,0:T(8,128)S(1)}, u32[]{:S(2)}, u32[]{:S(2)}) collective-permute-start(f32[8,8,8,128]{3,2,1,0:T(8,128)S(1)} %get-tuple-element.111.token.refs_12_.refs_6_), channel_id=1, source_target_pairs={{1,0},{2,1},{3,2},{4,3},{5,4},{6,5},{7,6},{8,7},{9,8},{10,9},{11,1... | collective-permute-start | bytes 786440 | tf_op jit(solution)/shard_map/ppermute | solution.py:351
  43.6 9.7 %collective-permute-start.10 = (f32[8,8,8,128]{3,2,1,0:T(8,128)S(1)}, f32[8,8,8,128]{3,2,1,0:T(8,128)S(1)}, u32[]{:S(2)}, u32[]{:S(2)}) collective-permute-start(f32[8,8,8,128]{3,2,1,0:T(8,128)S(1)} %get-tuple-element.117.refs_13_.refs_6_), channel_id=1, source_target_pairs={{1,0},{2,1},{3,2},{4,3},{5,4},{6,5},{7,6},{8,7},{9,8},{10,9},{11,1... | collective-permute-start | bytes 786440 | tf_op jit(solution)/shard_map/ppermute | solution.py:351
  45.2 9.2 %collective-permute-start.11 = (f32[8,8,8,128]{3,2,1,0:T(8,128)S(1)}, f32[8,8,8,128]{3,2,1,0:T(8,128)S(1)}, u32[]{:S(2)}, u32[]{:S(2)}) collective-permute-start(f32[8,8,8,128]{3,2,1,0:T(8,128)S(1)} %get-tuple-element.118.refs_14_.refs_7_), channel_id=1, source_target_pairs={{0,1},{1,2},{2,3},{3,4},{4,5},{5,6},{6,7},{7,8},{8,9},{9,10},{10,1... | collective-permute-start | bytes 786440 | tf_op jit(solution)/shard_map/ppermute | solution.py:351
  49.3 11.7 %collective-permute-start.9 = (f32[8,8,8,128]{3,2,1,0:T(8,128)S(1)}, f32[8,8,8,128]{3,2,1,0:T(8,128)S(1)}, u32[]{:S(2)}, u32[]{:S(2)}) collective-permute-start(f32[8,8,8,128]{3,2,1,0:T(8,128)S(1)} %get-tuple-element.122.refs_15_.refs_6_), channel_id=1, source_target_pairs={{1,0},{2,1},{3,2},{4,3},{5,4},{6,5},{7,6},{8,7},{9,8},{10,9},{11,1... | collective-permute-start | bytes 786440 | tf_op jit(solution)/shard_map/ppermute | solution.py:351
  52.4 9.9 %collective-permute-start.8 = (f32[8,8,8,128]{3,2,1,0:T(8,128)S(1)}, f32[8,8,8,128]{3,2,1,0:T(8,128)S(1)}, u32[]{:S(2)}, u32[]{:S(2)}) collective-permute-start(f32[8,8,8,128]{3,2,1,0:T(8,128)S(1)} %get-tuple-element.123.token.refs_10_.refs_7_), channel_id=1, source_target_pairs={{0,1},{1,2},{2,3},{3,4},{4,5},{5,6},{6,7},{7,8},{8,9},{9,10},{10,1... | collective-permute-start | bytes 786440 | tf_op jit(solution)/shard_map/ppermute | solution.py:351
  54.3 14.2 %collective-permute-start.14 = (f32[8,8,8,128]{3,2,1,0:T(8,128)S(1)}, f32[8,8,8,128]{3,2,1,0:T(8,128)S(1)}, u32[]{:S(2)}, u32[]{:S(2)}) collective-permute-start(f32[8,8,8,128]{3,2,1,0:T(8,128)S(1)} %get-tuple-element.131.refs_11_.refs_7_), channel_id=1, source_target_pairs={{0,1},{1,2},{2,3},{3,4},{4,5},{5,6},{6,7},{7,8},{8,9},{9,10},{10,1... | collective-permute-start | bytes 786440 | tf_op jit(solution)/shard_map/ppermute | solution.py:351
  55.1 14.8 %collective-permute-start.15 = (f32[8,8,8,128]{3,2,1,0:T(8,128)S(1)}, f32[8,8,8,128]{3,2,1,0:T(8,128)S(1)}, u32[]{:S(2)}, u32[]{:S(2)}) collective-permute-start(f32[8,8,8,128]{3,2,1,0:T(8,128)S(1)} %get-tuple-element.132.refs_12_.refs_6_), channel_id=1, source_target_pairs={{1,0},{2,1},{3,2},{4,3},{5,4},{6,5},{7,6},{8,7},{9,8},{10,9},{11,1... | collective-permute-start | bytes 786440 | tf_op jit(solution)/shard_map/ppermute | solution.py:351
  62.0 11.8 %collective-permute-start.13 = (f32[8,8,8,128]{3,2,1,0:T(8,128)S(1)}, f32[8,8,8,128]{3,2,1,0:T(8,128)S(1)}, u32[]{:S(2)}, u32[]{:S(2)}) collective-permute-start(f32[8,8,8,128]{3,2,1,0:T(8,128)S(1)} %get-tuple-element.136.refs_13_.refs_7_), channel_id=1, source_target_pairs={{0,1},{1,2},{2,3},{3,4},{4,5},{5,6},{6,7},{7,8},{8,9},{9,10},{10,1... | collective-permute-start | bytes 786440 | tf_op jit(solution)/shard_map/ppermute | solution.py:351
  63.0 13.8 %collective-permute-start.12 = (f32[8,8,8,128]{3,2,1,0:T(8,128)S(1)}, f32[8,8,8,128]{3,2,1,0:T(8,128)S(1)}, u32[]{:S(2)}, u32[]{:S(2)}) collective-permute-start(f32[8,8,8,128]{3,2,1,0:T(8,128)S(1)} %get-tuple-element.137.token.refs_10_.refs_6_), channel_id=1, source_target_pairs={{1,0},{2,1},{3,2},{4,3},{5,4},{6,5},{7,6},{8,7},{9,8},{10,9},{11,1... | collective-permute-start | bytes 786440 | tf_op jit(solution)/shard_map/ppermute | solution.py:351
  69.6 8.6 %collective-permute-start.18 = (f32[4,8,8,128]{3,2,1,0:T(8,128)S(1)}, f32[4,8,8,128]{3,2,1,0:T(8,128)S(1)}, u32[]{:S(2)}, u32[]{:S(2)}) collective-permute-start(f32[4,8,8,128]{3,2,1,0:T(8,128)S(1)} %get-tuple-element.158), channel_id=1, source_target_pairs={{1,0},{2,1},{3,2},{4,3},{5,4},{6,5},{7,6},{8,7},{9,8},{10,9},{11,1... | collective-permute-start | bytes 393224 | tf_op jit(solution)/shard_map/ppermute | solution.py:351
  70.6 8.0 %collective-permute-start.17 = (f32[4,8,8,128]{3,2,1,0:T(8,128)S(1)}, f32[4,8,8,128]{3,2,1,0:T(8,128)S(1)}, u32[]{:S(2)}, u32[]{:S(2)}) collective-permute-start(f32[4,8,8,128]{3,2,1,0:T(8,128)S(1)} %get-tuple-element.156), channel_id=1, source_target_pairs={{0,1},{1,2},{2,3},{3,4},{4,5},{5,6},{6,7},{7,8},{8,9},{9,10},{10,1... | collective-permute-start | bytes 393224 | tf_op jit(solution)/shard_map/ppermute | solution.py:351
  74.9 4.8 %collective-permute-start.19 = (f32[4,8,8,128]{3,2,1,0:T(8,128)S(1)}, f32[4,8,8,128]{3,2,1,0:T(8,128)S(1)}, u32[]{:S(2)}, u32[]{:S(2)}) collective-permute-start(f32[4,8,8,128]{3,2,1,0:T(8,128)S(1)} %get-tuple-element.161), channel_id=1, source_target_pairs={{1,0},{2,1},{3,2},{4,3},{5,4},{6,5},{7,6},{8,7},{9,8},{10,9},{11,1... | collective-permute-start | bytes 393224 | tf_op jit(solution)/shard_map/ppermute | solution.py:351
  77.6 7.8 %collective-permute-start.16 = (f32[4,8,8,128]{3,2,1,0:T(8,128)S(1)}, f32[4,8,8,128]{3,2,1,0:T(8,128)S(1)}, u32[]{:S(2)}, u32[]{:S(2)}) collective-permute-start(f32[4,8,8,128]{3,2,1,0:T(8,128)S(1)} %get-tuple-element.153), channel_id=1, source_target_pairs={{0,1},{1,2},{2,3},{3,4},{4,5},{5,6},{6,7},{7,8},{8,9},{9,10},{10,1... | collective-permute-start | bytes 393224 | tf_op jit(solution)/shard_map/ppermute | solution.py:351
  85.4 0.8 copy-start.4
  87.3 21.6 %all-to-all-start.1 = ((f32[16,64,128]{2,1,0:T(8,128)}), f32[16,64,128]{2,1,0:T(8,128)S(1)}, u32[]{:S(2)}, u32[]{:S(2)}) async-start(f32[16,64,128]{2,1,0:T(8,128)} %bitcast.7), calls=%async_computation.1 | async-start | bytes 1048576 | tf_op jit(solution)/shard_map/all_to_all | solution.py:360

commit v4 on v3

--- a/solution.py
+++ b/solution.py
@@ -13,10 +13,22 @@
 NY = 128
 SCALE = 5040.0
 TAPS = (8064.0, -1008.0, 128.0, -9.0)
-CENTRE = 3.0 * -14350.0
+CENTRE = (-43008.0, -42.0)
 F32 = jnp.float32
 BF16 = jnp.bfloat16
 VMEM_LIMIT = 16 * 1024 * 1024
+
+
+def fill_x_matrix(mat_ref):
+    row = lax.broadcasted_iota(jnp.int32, (NX, 4 * NX), 0)
+    col = lax.broadcasted_iota(jnp.int32, (NX, 4 * NX), 1)
+    place = lambda n: (n & 7) * 8 + ((n & (NX - 1)) >> 3)
+    apart = jnp.abs(place(row) - place(col))
+    first = jnp.where(apart == 0, CENTRE[0], 0.0)
+    for reach, tap in enumerate(TAPS, 1):
+        first = jnp.where(apart == reach, tap, first)
+    second = jnp.where(apart == 0, CENTRE[1], 0.0)
+    mat_ref[...] = jnp.where(col < 2 * NX, first, second).astype(BF16)
 
 
 def fill_matrix(mat_ref):
@@ -52,28 +64,27 @@
         ref[at, j] = value
 
 
-def advance(src, prev, dest, vel, first, mat_ref, part, inj, see):
+def advance(src, prev, dest, vel, first, mat_ref, x_ref, part, inj, see):
     rows = src.chunk(first, 4).reshape(4 * NX, NY)
     high = rows.astype(BF16)
     low = (rows - high.astype(F32)).astype(BF16)
     both = jnp.concatenate([high, low], axis=1)
-    part[...] = jnp.dot(both, mat_ref[...], preferred_element_type=F32).reshape(4, 8, 8, NY)
-    sub = lax.broadcasted_iota(jnp.int32, (8, NY), 0)
-    top, bottom = sub == 0, sub == 7
+    along_y = jnp.dot(both, mat_ref[...], preferred_element_type=F32)
+    for p in (0, 2):
+        sides = []
+        for at in (p * NX, (p + 1) * NX):
+            sides.append(jnp.concatenate([high[at:at + NX], low[at:at + NX]] * 2, axis=0))
+        along_x = jnp.dot(x_ref[...], jnp.concatenate(sides, axis=1), preferred_element_type=F32)
+        for q in range(2):
+            at = (p + q) * NX
+            part[p + q] = (along_y[at:at + NX] + along_x[:, q * NY:(q + 1) * NY]).reshape(8, 8, NY)
     for p in range(4):
         plane = first + p
-        own = [src.tile(plane, j) for j in range(8)]
-        left = [jnp.where(top, 0.0, pltpu.roll(own[j], 1, 0)) for j in range(4, 8)]
-        right = [jnp.where(bottom, 0.0, pltpu.roll(own[j], 7, 0)) for j in range(4)]
-        line = left + own + right
-        for j in range(8):
-            here = line[j + 4]
-            total = CENTRE * here + part[p, j]
+        for j in range(8):
+            here = src.tile(plane, j)
+            total = part[p, j]
             for reach, tap in enumerate(TAPS, 1):
-                pair = (line[j + 4 + reach] + line[j + 4 - reach]) + (
-                    src.tile(plane + reach, j) + src.tile(plane - reach, j)
-                )
-                total = total + tap * pair
+                total = total + tap * (src.tile(plane + reach, j) + src.tile(plane - reach, j))
             change = vel.tile(plane, j) * total
             if 4 <= plane < 12:
                 change = change + inj[plane - 4, j]
@@ -94,7 +105,7 @@
     refs = list(refs)
     take = lambda count: [refs.pop(0) for _ in range(count)]
     rows = lambda some, at: Rows(*[(ref, *where) for ref, where in zip(some, at)])
-    keep, mat_ref, inj = take(3)
+    keep, mat_ref, x_ref, inj = take(4)
     vel = rows(take(len(vel_at)), vel_at)
     now_refs = take(len(now_at))
     prev = Natural(take(1)[0], field) if prev_at is None else rows(take(len(prev_at)), prev_at)
@@ -131,7 +142,7 @@
 
         return change_out if field == 0 else image_out
 
-    run = functools.partial(advance, vel=vel, mat_ref=mat_ref)
+    run = functools.partial(advance, vel=vel, mat_ref=mat_ref, x_ref=x_ref)
     skip = 0
     if mid_at:
         for n, lo in enumerate(starts):
@@ -155,21 +166,24 @@
             out[p, j] = jnp.where(inside, message[8 + p, j], 0.0)
 
 
-def pack_kernel(now_in, up_0, down_0, up_1, down_1, low_0, high_0, low_1, high_1, mat_ref):
+def pack_kernel(now_in, up_msg, down_msg, low_0, high_0, low_1, high_1, mat_ref, x_ref):
     fill_matrix(mat_ref)
-    for field, (up_msg, down_msg, low, high) in enumerate(((up_0, down_0, low_0, high_0), (up_1, down_1, low_1, high_1))):
+    fill_x_matrix(x_ref)
+    for field, (low, high) in enumerate(((low_0, high_0), (low_1, high_1))):
         now = Natural(now_in, field)
         for p in range(PLANES):
             for j in range(8):
                 tile = now.tile(p, j)
                 (high if p >= 8 else low)[p % 8, j] = tile
                 if p < 4:
-                    down_msg[p, j] = tile
+                    down_msg[field, p, j] = tile
                 if p >= 12:
-                    up_msg[p - 12, j] = tile
-
-
-def spread_kernel(own, out):
+                    up_msg[field, p - 12, j] = tile
+
+
+def spread_kernel(own, out, factor):
+    speed = own[...]
+    factor[...] = (-2.0 / (16 * STEPS)) / (speed * speed * speed)
     for shot in range(16):
         out[pl.ds(shot * 64, 64), :] = own[...]
 
@@ -196,30 +210,51 @@
 
 def inject_kernel(source_cells, source_amps, cells, amps, token, out_0, out_1, *, step, steps):
     del token
-    for out, (where, what) in ((out_0, (source_cells, source_amps)), (out_1, (cells, amps))):
-        values = dense(where, what, step, steps)
-        for side in range(steps):
-            out[side] = values[:, side * NY:(side + 1) * NY].reshape(8, 8, 8, NY)
-
-
-def open_kernel(keep_below, keep_above, gathered, below_0, above_0, below_1, above_1,
+    values = dense(cells, amps, step, steps)
+    for at in range(steps):
+        out_1[at] = values[:, at * NY:(at + 1) * NY].reshape(8, 8, 8, NY)
+
+    def pick(array, row, column):
+        spot = (lax.broadcasted_iota(jnp.int32, array.shape, 0) == row) & (lax.broadcasted_iota(jnp.int32, array.shape, 1) == column)
+        return jnp.sum(jnp.where(spot, array, 0.0), keepdims=True)
+
+    sub = lax.broadcasted_iota(jnp.int32, (8, NY), 0)
+    lane = lax.broadcasted_iota(jnp.int32, (8, NY), 1)
+    places = source_cells[...].astype(F32)
+    count = source_cells.shape[1]
+    rows, columns, amounts = [], [], []
+    for n in range(count):
+        cell = pick(places, 0, n).astype(jnp.int32)
+        z, x, y = cell >> 13, (cell >> 7) & (NX - 1), cell & (NY - 1)
+        rows.append(sub - ((z - 4) * NX + (x & 7) * 8 + (x >> 3)))
+        columns.append(lane == y)
+        amounts.append([pick(source_amps[...], n, step + at) for at in range(steps)])
+    for p in range(8):
+        for j in range(8):
+            hits = [(row == -(p * NX + j * 8)) & column for row, column in zip(rows, columns)]
+            for at in range(steps):
+                total = jnp.zeros((8, NY), F32)
+                for hit, amount in zip(hits, amounts):
+                    total = total + jnp.where(hit, amount[at], 0.0)
+                out_0[at, p, j] = total
+
+
+def open_kernel(keep_below, keep_above, gathered, below, above,
                 vel, image, below_out_0, above_out_0, below_out_1, above_out_1):
     image[...] = jnp.zeros_like(image)
     for p in range(PLANES):
         for j in range(8):
             line = gathered[pl.ds((j // 4) * 64 + p * 4 + j % 4, 8, stride=128), :]
             vel[p, j] = line * line * (1.0 / SCALE)
-    for keep, src, dest in ((keep_below, below_0, below_out_0), (keep_above, above_0, above_out_0),
-                            (keep_below, below_1, below_out_1), (keep_above, above_1, above_out_1)):
+    for keep, src, dests in ((keep_below, below, (below_out_0, below_out_1)), (keep_above, above, (above_out_0, above_out_1))):
         inside = keep[...] > 0.0
-        for p in range(4):
-            for j in range(8):
-                dest[p, j] = jnp.where(inside, src[p, j], 0.0)
-
-
-def terms_kernel(image, velocity, out, factor):
-    speed = velocity[...]
-    factor[...] = (-2.0 / (16 * STEPS)) / (speed * speed * speed)
+        for field, dest in enumerate(dests):
+            for p in range(4):
+                for j in range(8):
+                    dest[p, j] = jnp.where(inside, src[field, p, j], 0.0)
+
+
+def terms_kernel(image, out):
     for p in range(PLANES):
         for j in range(8):
             out[pl.ds((j // 4) * 64 + p * 4 + j % 4, 8, stride=128), :] = image[p, j]
@@ -274,20 +309,15 @@
     keep = [jnp.full((8, NY), slab > 0, F32), jnp.full((8, NY), slab < slabs - 1, F32)]
 
     vel_rows = velocity.reshape(PLANES * 4, NY)
-    spread = call(spread_kernel, (vel_rows,), rows_of(shots * 64), 1 << 20)
+    spread, factor = call(spread_kernel, (vel_rows,), (rows_of(shots * 64), rows_of(64)), 1 << 20)
     gathered = lax.all_to_all(spread.reshape(shots, 64, NY), "shot", 0, 0, tiled=True)
     half, quarter = tiles(8), tiles(4)
-    mat = jax.ShapeDtypeStruct((2 * NY, NY), BF16)
-    up_0, down_0, up_1, down_1, low_0, high_0, low_1, high_1, mat = call(
-        pack_kernel, (fields_now.reshape(-1, NY),), (*[quarter] * 4, *[half] * 4, mat), 1 << 22)
+    mat, mat_x = jax.ShapeDtypeStruct((2 * NY, NY), BF16), jax.ShapeDtypeStruct((NX, 4 * NX), BF16)
+    up_msg, down_msg, low_0, high_0, low_1, high_1, mat, mat_x = call(
+        pack_kernel, (fields_now.reshape(-1, NY),), (*[tiles(2, 4)] * 2, *[half] * 4, mat, mat_x), 1 << 22)
     now = [[low_0, high_0], [low_1, high_1]]
-    arrived = [lax.ppermute(a, "slab", way) for a, way in ((up_0, up), (down_0, down), (up_1, up), (down_1, down))]
-    few = 128 - source_cells.shape[1]
-    marks = (
-        jnp.pad(source_cells, ((0, 0), (0, few)), constant_values=4 * NX * NY),
-        jnp.pad(source_traces[0], ((0, 0), (0, few))),
-        receiver_cells, receiver_traces[0],
-    )
+    arrived = [lax.ppermute(up_msg, "slab", up), lax.ppermute(down_msg, "slab", down)]
+    marks = (source_cells, source_traces[0].T, receiver_cells, receiver_traces[0])
     vel, image, *far = call(
         open_kernel, (*keep, gathered.reshape(shots * 64, NY), *arrived), (tiles(16), tiles(16), *[quarter] * 4), 1 << 22)
     beyond = [far[:2], far[2:]]
@@ -300,13 +330,13 @@
         final = block == len(lengths) - 1
         to_send = 0 if final else 4 * lengths[block + 1]
         order = (1, 0) if block % 2 == 0 else (0, 1)
+        first = block == 0
         news, mids, sent = ([[None, None], [None, None]] for _ in range(3))
         changes = [None, None]
         inj = call(functools.partial(inject_kernel, step=step, steps=length),
                    (*marks, mat if block == 0 else token), (tiles(length, 8), tiles(length, 8)), 1 << 24)
         for field in range(2):
             for n, side in enumerate(order):
-                first = block == 0
                 if block == 1 and field == 0:
                     edge = call(edge_kernel, (keep[side], beyond[0][side]), quarter, 1 << 16)
                     vels[side] = [(vel, (0, 16)), (edge, (16 if side else -4, 4))]
@@ -317,7 +347,7 @@
                 if length == 2:
                     mid_at = (4, 16) if side and n == 0 else (-4, 16) if n == 0 else (12, 8) if side else (-4, 8)
                     mid_list = [(None, mid_at)] + ([mids[field][order[0]]] if n == 1 else [])
-                args = [keep[side], mat, inj[field]] + [a for a, _ in vels[side]]
+                args = [keep[side], mat, mat_x, inj[field]] + [a for a, _ in vels[side]]
                 args += [a for a, _ in now_list] + [a for a, _ in prev_list] + [a for a, _ in mid_list[1:]]
                 aliases = {}
                 if field == 1:
@@ -356,7 +386,7 @@
         before_last, now, beyond = now, news, sent
         step += length
 
-    terms, factor = call(terms_kernel, (image, vel_rows), (rows_of(shots * 64), rows_of(64)), 1 << 20)
+    terms = call(terms_kernel, (image,), rows_of(shots * 64), 1 << 20)
     terms = lax.all_to_all(terms.reshape(shots, 64, NY), "shot", 0, 0, tiled=True)
     args = []
     for field in range(2):

time: 110 us -> 106 us (0.964)
  starting transfers between devices: 61.2 us -> 52.5 us
  waiting for transfers between devices: 20.2 us -> 28.9 us
  Pallas kernels: 22.8 us -> 20.8 us
  local copies, waits for them, and re-layouts: 4.41 us -> 2.68 us
    ppermute x4 -> x2, starting transfers between devices: 12.8 us -> 7.77 us  [the longest x1 6.11 us: body(): lax.ppermute(down_msg, 'slab', down)]
    ppermute x4 -> x2, waiting for transfers between devices: 0.97 us -> 5.68 us  [the longest x1 5.68 us: body(): lax.ppermute(up_msg, 'slab', up)]
    ppermute x16, waiting for transfers between devices: 11.1 us -> 15 us  [body(): lax.ppermute(rest[-1] if send else out, 'slab', up if side else down)]
    ppermute x16, starting transfers between devices: 29.6 us -> 27.4 us  [body(): lax.ppermute(rest[-1] if send else out, 'slab', up if side else down)]
    pallas_call x33, Pallas kernels: 22.8 us -> 20.8 us  [call(): pl.pallas_call(kernel, in_specs=[whole] * len(args), out_specs=jax.tree.m...]
    unnamed x16, local copies, waits for them, and re-layouts: 4.31 us -> 2.68 us
    all_to_all x1, starting transfers between devices: 11.8 us -> 10.4 us  [body(): lax.all_to_all(terms.reshape(shots, 64, NY), 'shot', 0, 0, tiled=True)]
  transfers between devices with their start and end apart: 22 -> 20, of which waited for: 9 -> 9; matrix products, arithmetic and copies ran while one was open for 0% -> 0% of each run, Pallas kernels for 16% -> 15%
where the time goes in v4:
time: 106 us
  starting transfers between devices  52.5 us (50%)
  waiting for transfers between devices  28.9 us (27%)
  Pallas kernels  20.8 us (20%)
  local copies, waits for them, and re-layouts  2.68 us (3%)
    ppermute x16, starting transfers between devices, body(): lax.ppermute(rest[-1] if send else out, 'slab', up if side else down)  27.4 us
    pallas_call x33, Pallas kernels, call(): pl.pallas_call(kernel, in_specs=[whole] * len(args), out_specs=jax.tree.m...  20.8 us
    ppermute x16, waiting for transfers between devices, body(): lax.ppermute(rest[-1] if send else out, 'slab', up if side else down)  15 us
    all_to_all x1, starting transfers between devices, body(): lax.all_to_all(terms.reshape(shots, 64, NY), 'shot', 0, 0, tiled=True)  10.4 us
    all_to_all x1, waiting for transfers between devices, body(): lax.all_to_all(terms.reshape(shots, 64, NY), 'shot', 0, 0, tiled=True)  8.25 us
    all_to_all x1, starting transfers between devices, body(): lax.all_to_all(spread.reshape(shots, 64, NY), 'shot', 0, 0, tiled=True)  6.91 us
    ppermute x1, starting transfers between devices, body(): lax.ppermute(down_msg, 'slab', down)  6.11 us
    ppermute x1, waiting for transfers between devices, body(): lax.ppermute(up_msg, 'slab', up)  5.68 us
  transfers between devices with their start and end apart: 20, of which 9 were waited for; matrix products, arithmetic and copies ran while one was open for 0% of the time, Pallas kernels for 15%

profile of v4, /device:TPU:1, one launch (start us, length us, event | category | flops | bytes accessed | tf_op | source)
XLA Modules:
  0.0 105.9 jit_solution(12420553801198184486)
XLA Ops:
  0.6 0.7 copy-done.3
  1.4 0.8 shard_map.96
  2.2 6.9 %all-to-all-start = ((f32[16,64,128]{2,1,0:T(8,128)}), f32[16,64,128]{2,1,0:T(8,128)S(1)}, u32[]{:S(2)}, u32[]{:S(2)}) async-start(f32[16,64,128]{2,1,0:T(8,128)} %bitcast.6), calls=%async_computation | async-start | bytes 1048576 | tf_op jit(solution)/shard_map/all_to_all | solution.py:313
  9.1 1.2 %copy-done.1 = f32[1,2,16,64,128]{4,3,2,1,0:T(8,128)S(1)} copy-done((f32[1,2,16,64,128]{4,3,2,1,0:T(8,128)S(1)}, f32[1,2,16,64,128]{4,3,2,1,0:T(8,128)}, u32[]{:S(2)}) %copy-start.1) | copy-done | bytes 1048600
  10.4 0.9 shard_map.94
  11.2 1.7 %collective-permute-start = (f32[2,4,8,8,128]{4,3,2,1,0:T(8,128)}, f32[2,4,8,8,128]{4,3,2,1,0:T(8,128)S(1)}, u32[]{:S(2)}, u32[]{:S(2)}) collective-permute-start(f32[2,4,8,8,128]{4,3,2,1,0:T(8,128)} %get-tuple-element.91), channel_id=1, source_target_pairs={{0,1},{1,2},{2,3},{3,4},{4,5},{5,6},{6,7},{7,8},{8,9},{9,10},{10,1... | collective-permute-start | bytes 786440 | tf_op jit(solution)/shard_map/ppermute | solution.py:319
  12.9 6.1 %collective-permute-start.1 = (f32[2,4,8,8,128]{4,3,2,1,0:T(8,128)}, f32[2,4,8,8,128]{4,3,2,1,0:T(8,128)}, u32[]{:S(2)}, u32[]{:S(2)}) collective-permute-start(f32[2,4,8,8,128]{4,3,2,1,0:T(8,128)} %get-tuple-element.92), channel_id=1, source_target_pairs={{1,0},{2,1},{3,2},{4,3},{5,4},{6,5},{7,6},{8,7},{9,8},{10,9},{11,1... | collective-permute-start | bytes 786440 | tf_op jit(solution)/shard_map/ppermute | solution.py:319
  20.1 5.7 %collective-permute-done.below = f32[2,4,8,8,128]{4,3,2,1,0:T(8,128)S(1)} collective-permute-done((f32[2,4,8,8,128]{4,3,2,1,0:T(8,128)}, f32[2,4,8,8,128]{4,3,2,1,0:T(8,128)S(1)}, u32[]{:S(2)}, u32[]{:S(2)}) %collective-permute-start) | collective-permute-done | bytes 262176 | tf_op jit(solution)/shard_map/ppermute | solution.py:319
  25.8 1.3 %shard_map.97 = (f32[16,8,8,128]{3,2,1,0:T(8,128)S(1)}, f32[16,8,8,128]{3,2,1,0:T(8,128)S(1)}, f32[4,8,8,128]{3,2,1,0:T(8,128)S(1)}, f32[4,8,8,128]{3,2,1,0:T(8,...) custom-call(f32[8,128]{1,0:T(8,128)S(1)} %broadcast_in_dim.6.keep_below.refs_0_.keep, ...), custom_call_target="tpu_custom_call" | custom-call | flops 4194304 | bytes 1048576 | tf_op jit(solution)/shard_map/pallas_call | solution.py:290
  28.0 5.1 %collective-permute-start.2 = (f32[12,8,8,128]{3,2,1,0:T(8,128)S(1)}, f32[12,8,8,128]{3,2,1,0:T(8,128)S(1)}, u32[]{:S(2)}, u32[]{:S(2)}) collective-permute-start(f32[12,8,8,128]{3,2,1,0:T(8,128)S(1)} %get-tuple-element.107.refs_11_.refs_7_), channel_id=1, source_target_pairs={{1,0},{2,1},{3,2},{4,3},{5,4},{6,5},{7,6},{8,7},{9,8},{10,9},{11,1... | collective-permute-start | bytes 1179656 | tf_op jit(solution)/shard_map/ppermute | solution.py:381
  34.1 5.1 %collective-permute-start.3 = (f32[8,8,8,128]{3,2,1,0:T(8,128)S(1)}, f32[8,8,8,128]{3,2,1,0:T(8,128)S(1)}, u32[]{:S(2)}, u32[]{:S(2)}) collective-permute-start(f32[8,8,8,128]{3,2,1,0:T(8,128)S(1)} %get-tuple-element.110.token.refs_13_.refs_7_), channel_id=1, source_target_pairs={{1,0},{2,1},{3,2},{4,3},{5,4},{6,5},{7,6},{8,7},{9,8},{10,9},{11,1... | collective-permute-start | bytes 786440 | tf_op jit(solution)/shard_map/ppermute | solution.py:381
  39.7 0.9 shard_map.105
  40.6 0.9 collective-permute-start.8
  42.9 2.8 %collective-permute-done.5.refs_6_ = f32[8,8,8,128]{3,2,1,0:T(8,128)S(1)} collective-permute-done((f32[8,8,8,128]{3,2,1,0:T(8,128)S(1)}, f32[8,8,8,128]{3,2,1,0:T(8,128)S(1)}, u32[]{:S(2)}, u32[]{:S(2)}) %collective-permute-start.5) | collective-permute-done | bytes 262176 | tf_op jit(solution)/shard_map/ppermute | solution.py:381
  45.6 0.9 shard_map.107
  46.5 1.9 %collective-permute-start.7 = (f32[8,8,8,128]{3,2,1,0:T(8,128)S(1)}, f32[8,8,8,128]{3,2,1,0:T(8,128)S(1)}, u32[]{:S(2)}, u32[]{:S(2)}) collective-permute-start(f32[8,8,8,128]{3,2,1,0:T(8,128)S(1)} %get-tuple-element.121.refs_16_.refs_7_), channel_id=1, source_target_pairs={{1,0},{2,1},{3,2},{4,3},{5,4},{6,5},{7,6},{8,7},{9,8},{10,9},{11,1... | collective-permute-start | bytes 786440 | tf_op jit(solution)/shard_map/ppermute | solution.py:381
  49.6 1.4 %collective-permute-done.8.refs_6_ = f32[8,8,8,128]{3,2,1,0:T(8,128)S(1)} collective-permute-done((f32[8,8,8,128]{3,2,1,0:T(8,128)S(1)}, f32[8,8,8,128]{3,2,1,0:T(8,128)S(1)}, u32[]{:S(2)}, u32[]{:S(2)}) %collective-permute-start.8) | collective-permute-done | bytes 262176 | tf_op jit(solution)/shard_map/ppermute | solution.py:381
  51.0 0.8 shard_map.110
  52.6 5.9 %collective-permute-start.13 = (f32[8,8,8,128]{3,2,1,0:T(8,128)S(1)}, f32[8,8,8,128]{3,2,1,0:T(8,128)S(1)}, u32[]{:S(2)}, u32[]{:S(2)}) collective-permute-start(f32[8,8,8,128]{3,2,1,0:T(8,128)S(1)} %get-tuple-element.131.refs_13_.refs_7_), channel_id=1, source_target_pairs={{1,0},{2,1},{3,2},{4,3},{5,4},{6,5},{7,6},{8,7},{9,8},{10,9},{11,1... | collective-permute-start | bytes 786440 | tf_op jit(solution)/shard_map/ppermute | solution.py:381
  58.5 0.9 shard_map.112
  59.5 1.3 %collective-permute-done.6.refs_6_ = f32[8,8,8,128]{3,2,1,0:T(8,128)S(1)} collective-permute-done((f32[8,8,8,128]{3,2,1,0:T(8,128)S(1)}, f32[8,8,8,128]{3,2,1,0:T(8,128)S(1)}, u32[]{:S(2)}, u32[]{:S(2)}) %collective-permute-start.6) | collective-permute-done | bytes 262176 | tf_op jit(solution)/shard_map/ppermute | solution.py:381
  61.6 3.8 %collective-permute-start.10 = (f32[8,8,8,128]{3,2,1,0:T(8,128)S(1)}, f32[8,8,8,128]{3,2,1,0:T(8,128)S(1)}, u32[]{:S(2)}, u32[]{:S(2)}) collective-permute-start(f32[8,8,8,128]{3,2,1,0:T(8,128)S(1)} %get-tuple-element.136.token.refs_11_.refs_7_), channel_id=1, source_target_pairs={{1,0},{2,1},{3,2},{4,3},{5,4},{6,5},{7,6},{8,7},{9,8},{10,9},{11,1... | collective-permute-start | bytes 786440 | tf_op jit(solution)/shard_map/ppermute | solution.py:381
  65.9 0.9 shard_map.115
  67.5 1.5 %collective-permute-start.15 = (f32[4,8,8,128]{3,2,1,0:T(8,128)S(1)}, f32[4,8,8,128]{3,2,1,0:T(8,128)S(1)}, u32[]{:S(2)}, u32[]{:S(2)}) collective-permute-start(f32[4,8,8,128]{3,2,1,0:T(8,128)S(1)} %get-tuple-element.155), channel_id=1, source_target_pairs={{0,1},{1,2},{2,3},{3,4},{4,5},{5,6},{6,7},{7,8},{8,9},{9,10},{10,1... | collective-permute-start | bytes 393224 | tf_op jit(solution)/shard_map/ppermute | solution.py:381
  69.0 2.5 %collective-permute-done.11.refs_6_ = f32[8,8,8,128]{3,2,1,0:T(8,128)S(1)} collective-permute-done((f32[8,8,8,128]{3,2,1,0:T(8,128)S(1)}, f32[8,8,8,128]{3,2,1,0:T(8,128)S(1)}, u32[]{:S(2)}, u32[]{:S(2)}) %collective-permute-start.11) | collective-permute-done | bytes 262176 | tf_op jit(solution)/shard_map/ppermute | solution.py:381
  71.5 0.9 shard_map.117
  72.4 1.4 %collective-permute-start.17 = (f32[4,8,8,128]{3,2,1,0:T(8,128)S(1)}, f32[4,8,8,128]{3,2,1,0:T(8,128)S(1)}, u32[]{:S(2)}, u32[]{:S(2)}) collective-permute-start(f32[4,8,8,128]{3,2,1,0:T(8,128)S(1)} %get-tuple-element.160), channel_id=1, source_target_pairs={{1,0},{2,1},{3,2},{4,3},{5,4},{6,5},{7,6},{8,7},{9,8},{10,9},{11,1... | collective-permute-start | bytes 393224 | tf_op jit(solution)/shard_map/ppermute | solution.py:381
  77.6 5.7 %collective-permute-done.14.refs_6_ = f32[4,8,8,128]{3,2,1,0:T(8,128)S(1)} collective-permute-done((f32[4,8,8,128]{3,2,1,0:T(8,128)S(1)}, f32[4,8,8,128]{3,2,1,0:T(8,128)S(1)}, u32[]{:S(2)}, u32[]{:S(2)}) %collective-permute-start.14) | collective-permute-done | bytes 131104 | tf_op jit(solution)/shard_map/ppermute | solution.py:381
  83.8 1.1 %shard_map.124 = f32[1024,128]{1,0:T(8,128)} custom-call(f32[16,8,8,128]{3,2,1,0:T(8,128)S(1)} %get-tuple-element.166.image), custom_call_target="tpu_custom_call" | custom-call | flops 1048576 | bytes 1048576 | tf_op jit(solution)/shard_map/pallas_call | solution.py:290
  84.9 10.4 %all-to-all-start.1 = ((f32[16,64,128]{2,1,0:T(8,128)}), f32[16,64,128]{2,1,0:T(8,128)S(1)}, u32[]{:S(2)}, u32[]{:S(2)}) async-start(f32[16,64,128]{2,1,0:T(8,128)} %bitcast.9), calls=%async_computation.1 | async-start | bytes 1048576 | tf_op jit(solution)/shard_map/all_to_all | solution.py:390
  95.3 1.6 %shard_map.126 = (f32[2048,128]{1,0:T(8,128)}, f32[2048,128]{1,0:T(8,128)}) custom-call(f32[8,8,8,128]{3,2,1,0:T(8,128)S(1)} %get-tuple-element.144.refs_12_.refs_7_.before_low_0, f32[8,8,8,128]{3,2,1,0:T(8,128)S(1)} %get-tuple-element.145.refs_13_.refs_8_.before_high_0, f32[8,8,8,128]{3,2,1,0:T(8,128)S(1)} %get-tuple-element.163.refs_13_.low_0, ...), custom_call_target="tpu_custom_call" | custom-call | flops 4194304 | bytes 1048576 | tf_op jit(solution)/shard_map/pallas_call | solution.py:290
  97.0 8.3 %all-to-all-done.1 = f32[16,64,128]{2,1,0:T(8,128)S(1)} async-done(((f32[16,64,128]{2,1,0:T(8,128)}), f32[16,64,128]{2,1,0:T(8,128)S(1)}, u32[]{:S(2)}, u32[]{:S(2)}) %all-to-all-start.1) | async-done | bytes 524320 | tf_op jit(solution)/shard_map/all_to_all | solution.py:390
  (59 shorter events, 13.4 us)
Async XLA Ops:
  0.6 0.8 copy-start.3
  2.2 23.6 %all-to-all-start = ((f32[16,64,128]{2,1,0:T(8,128)}), f32[16,64,128]{2,1,0:T(8,128)S(1)}, u32[]{:S(2)}, u32[]{:S(2)}) async-start(f32[16,64,128]{2,1,0:T(8,128)} %bitcast.6), calls=%async_computation | async-start | bytes 1048576 | tf_op jit(solution)/shard_map/all_to_all | solution.py:313
  9.1 1.2 %copy-start.1 = (f32[1,2,16,64,128]{4,3,2,1,0:T(8,128)S(1)}, f32[1,2,16,64,128]{4,3,2,1,0:T(8,128)}, u32[]{:S(2)}) copy-start(f32[1,2,16,64,128]{4,3,2,1,0:T(8,128)} %param.9) | copy-start | bytes 3145732
  10.4 8.7 %copy-start.5 = (s32[1,256]{1,0:T(1,128)S(1)}, s32[1,256]{1,0:T(1,128)}, u32[]{:S(2)}) copy-start(s32[1,256]{1,0:T(1,128)} %cells.9) | copy-start | bytes 3076
  10.4 16.8 %copy-start = (f32[1,2,16,64,128]{4,3,2,1,0:T(8,128)S(1)}, f32[1,2,16,64,128]{4,3,2,1,0:T(8,128)}, u32[]{:S(2)}) copy-start(f32[1,2,16,64,128]{4,3,2,1,0:T(8,128)} %param.8) | copy-start | bytes 3145732
  11.2 14.5 %collective-permute-start = (f32[2,4,8,8,128]{4,3,2,1,0:T(8,128)}, f32[2,4,8,8,128]{4,3,2,1,0:T(8,128)S(1)}, u32[]{:S(2)}, u32[]{:S(2)}) collective-permute-start(f32[2,4,8,8,128]{4,3,2,1,0:T(8,128)} %get-tuple-element.91), channel_id=1, source_target_pairs={{0,1},{1,2},{2,3},{3,4},{4,5},{5,6},{6,7},{7,8},{8,9},{9,10},{10,1... | collective-permute-start | bytes 786440 | tf_op jit(solution)/shard_map/ppermute | solution.py:319
  12.9 12.9 %collective-permute-start.1 = (f32[2,4,8,8,128]{4,3,2,1,0:T(8,128)}, f32[2,4,8,8,128]{4,3,2,1,0:T(8,128)}, u32[]{:S(2)}, u32[]{:S(2)}) collective-permute-start(f32[2,4,8,8,128]{4,3,2,1,0:T(8,128)} %get-tuple-element.92), channel_id=1, source_target_pairs={{1,0},{2,1},{3,2},{4,3},{5,4},{6,5},{7,6},{8,7},{9,8},{10,9},{11,1... | collective-permute-start | bytes 786440 | tf_op jit(solution)/shard_map/ppermute | solution.py:319
  19.0 0.7 copy-start.2
  19.0 0.7 copy-start.4
  19.0 0.7 copy-start.6
  27.5 12.2 %collective-permute-start.4 = (f32[12,8,8,128]{3,2,1,0:T(8,128)S(1)}, f32[12,8,8,128]{3,2,1,0:T(8,128)S(1)}, u32[]{:S(2)}, u32[]{:S(2)}) collective-permute-start(f32[12,8,8,128]{3,2,1,0:T(8,128)S(1)} %get-tuple-element.103.refs_9_.refs_8_), channel_id=1, source_target_pairs={{0,1},{1,2},{2,3},{3,4},{4,5},{5,6},{6,7},{7,8},{8,9},{9,10},{10,1... | collective-permute-start | bytes 1179656 | tf_op jit(solution)/shard_map/ppermute | solution.py:381
  28.0 13.5 %collective-permute-start.2 = (f32[12,8,8,128]{3,2,1,0:T(8,128)S(1)}, f32[12,8,8,128]{3,2,1,0:T(8,128)S(1)}, u32[]{:S(2)}, u32[]{:S(2)}) collective-permute-start(f32[12,8,8,128]{3,2,1,0:T(8,128)S(1)} %get-tuple-element.107.refs_11_.refs_7_), channel_id=1, source_target_pairs={{1,0},{2,1},{3,2},{4,3},{5,4},{6,5},{7,6},{8,7},{9,8},{10,9},{11,1... | collective-permute-start | bytes 1179656 | tf_op jit(solution)/shard_map/ppermute | solution.py:381
  33.6 12.1 %collective-permute-start.5 = (f32[8,8,8,128]{3,2,1,0:T(8,128)S(1)}, f32[8,8,8,128]{3,2,1,0:T(8,128)S(1)}, u32[]{:S(2)}, u32[]{:S(2)}) collective-permute-start(f32[8,8,8,128]{3,2,1,0:T(8,128)S(1)} %get-tuple-element.109.refs_11_.refs_8_), channel_id=1, source_target_pairs={{0,1},{1,2},{2,3},{3,4},{4,5},{5,6},{6,7},{7,8},{8,9},{9,10},{10,1... | collective-permute-start | bytes 786440 | tf_op jit(solution)/shard_map/ppermute | solution.py:381
  34.1 5.2 %copy-start.7 = (s32[1,2]{1,0:T(1,128)S(1)}, s32[1,2]{1,0:T(1,128)}, u32[]{:S(2)}) copy-start(s32[1,2]{1,0:T(1,128)} %source_cells.9) | copy-start | bytes 28
  34.1 14.4 %collective-permute-start.3 = (f32[8,8,8,128]{3,2,1,0:T(8,128)S(1)}, f32[8,8,8,128]{3,2,1,0:T(8,128)S(1)}, u32[]{:S(2)}, u32[]{:S(2)}) collective-permute-start(f32[8,8,8,128]{3,2,1,0:T(8,128)S(1)} %get-tuple-element.110.token.refs_13_.refs_7_), channel_id=1, source_target_pairs={{1,0},{2,1},{3,2},{4,3},{5,4},{6,5},{7,6},{8,7},{9,8},{10,9},{11,1... | collective-permute-start | bytes 786440 | tf_op jit(solution)/shard_map/ppermute | solution.py:381
  40.6 10.4 %collective-permute-start.8 = (f32[8,8,8,128]{3,2,1,0:T(8,128)S(1)}, f32[8,8,8,128]{3,2,1,0:T(8,128)S(1)}, u32[]{:S(2)}, u32[]{:S(2)}) collective-permute-start(f32[8,8,8,128]{3,2,1,0:T(8,128)S(1)} %get-tuple-element.116.refs_14_.refs_7_), channel_id=1, source_target_pairs={{1,0},{2,1},{3,2},{4,3},{5,4},{6,5},{7,6},{8,7},{9,8},{10,9},{11,1... | collective-permute-start | bytes 786440 | tf_op jit(solution)/shard_map/ppermute | solution.py:381
  42.2 9.8 %collective-permute-start.9 = (f32[8,8,8,128]{3,2,1,0:T(8,128)S(1)}, f32[8,8,8,128]{3,2,1,0:T(8,128)S(1)}, u32[]{:S(2)}, u32[]{:S(2)}) collective-permute-start(f32[8,8,8,128]{3,2,1,0:T(8,128)S(1)} %get-tuple-element.117.refs_15_.refs_8_), channel_id=1, source_target_pairs={{0,1},{1,2},{2,3},{3,4},{4,5},{5,6},{6,7},{7,8},{8,9},{9,10},{10,1... | collective-permute-start | bytes 786440 | tf_op jit(solution)/shard_map/ppermute | solution.py:381
  46.5 12.0 %collective-permute-start.7 = (f32[8,8,8,128]{3,2,1,0:T(8,128)S(1)}, f32[8,8,8,128]{3,2,1,0:T(8,128)S(1)}, u32[]{:S(2)}, u32[]{:S(2)}) collective-permute-start(f32[8,8,8,128]{3,2,1,0:T(8,128)S(1)} %get-tuple-element.121.refs_16_.refs_7_), channel_id=1, source_target_pairs={{1,0},{2,1},{3,2},{4,3},{5,4},{6,5},{7,6},{8,7},{9,8},{10,9},{11,1... | collective-permute-start | bytes 786440 | tf_op jit(solution)/shard_map/ppermute | solution.py:381
  49.1 11.8 %collective-permute-start.6 = (f32[8,8,8,128]{3,2,1,0:T(8,128)S(1)}, f32[8,8,8,128]{3,2,1,0:T(8,128)S(1)}, u32[]{:S(2)}, u32[]{:S(2)}) collective-permute-start(f32[8,8,8,128]{3,2,1,0:T(8,128)S(1)} %get-tuple-element.122.token.refs_11_.refs_8_), channel_id=1, source_target_pairs={{0,1},{1,2},{2,3},{3,4},{4,5},{5,6},{6,7},{7,8},{8,9},{9,10},{10,1... | collective-permute-start | bytes 786440 | tf_op jit(solution)/shard_map/ppermute | solution.py:381
  51.8 14.1 %collective-permute-start.12 = (f32[8,8,8,128]{3,2,1,0:T(8,128)S(1)}, f32[8,8,8,128]{3,2,1,0:T(8,128)S(1)}, u32[]{:S(2)}, u32[]{:S(2)}) collective-permute-start(f32[8,8,8,128]{3,2,1,0:T(8,128)S(1)} %get-tuple-element.130.refs_12_.refs_8_), channel_id=1, source_target_pairs={{0,1},{1,2},{2,3},{3,4},{4,5},{5,6},{6,7},{7,8},{8,9},{9,10},{10,1... | collective-permute-start | bytes 786440 | tf_op jit(solution)/shard_map/ppermute | solution.py:381
  52.6 14.3 %collective-permute-start.13 = (f32[8,8,8,128]{3,2,1,0:T(8,128)S(1)}, f32[8,8,8,128]{3,2,1,0:T(8,128)S(1)}, u32[]{:S(2)}, u32[]{:S(2)}) collective-permute-start(f32[8,8,8,128]{3,2,1,0:T(8,128)S(1)} %get-tuple-element.131.refs_13_.refs_7_), channel_id=1, source_target_pairs={{1,0},{2,1},{3,2},{4,3},{5,4},{6,5},{7,6},{8,7},{9,8},{10,9},{11,1... | collective-permute-start | bytes 786440 | tf_op jit(solution)/shard_map/ppermute | solution.py:381
  59.4 12.1 %collective-permute-start.11 = (f32[8,8,8,128]{3,2,1,0:T(8,128)S(1)}, f32[8,8,8,128]{3,2,1,0:T(8,128)S(1)}, u32[]{:S(2)}, u32[]{:S(2)}) collective-permute-start(f32[8,8,8,128]{3,2,1,0:T(8,128)S(1)} %get-tuple-element.135.refs_14_.refs_8_), channel_id=1, source_target_pairs={{0,1},{1,2},{2,3},{3,4},{4,5},{5,6},{6,7},{7,8},{8,9},{9,10},{10,1... | collective-permute-start | bytes 786440 | tf_op jit(solution)/shard_map/ppermute | solution.py:381
  61.6 12.3 %collective-permute-start.10 = (f32[8,8,8,128]{3,2,1,0:T(8,128)S(1)}, f32[8,8,8,128]{3,2,1,0:T(8,128)S(1)}, u32[]{:S(2)}, u32[]{:S(2)}) collective-permute-start(f32[8,8,8,128]{3,2,1,0:T(8,128)S(1)} %get-tuple-element.136.token.refs_11_.refs_7_), channel_id=1, source_target_pairs={{1,0},{2,1},{3,2},{4,3},{5,4},{6,5},{7,6},{8,7},{9,8},{10,9},{11,1... | collective-permute-start | bytes 786440 | tf_op jit(solution)/shard_map/ppermute | solution.py:381
  66.8 8.5 %collective-permute-start.16 = (f32[4,8,8,128]{3,2,1,0:T(8,128)S(1)}, f32[4,8,8,128]{3,2,1,0:T(8,128)S(1)}, u32[]{:S(2)}, u32[]{:S(2)}) collective-permute-start(f32[4,8,8,128]{3,2,1,0:T(8,128)S(1)} %get-tuple-element.157), channel_id=1, source_target_pairs={{1,0},{2,1},{3,2},{4,3},{5,4},{6,5},{7,6},{8,7},{9,8},{10,9},{11,1... | collective-permute-start | bytes 393224 | tf_op jit(solution)/shard_map/ppermute | solution.py:381
  67.5 8.8 %collective-permute-start.15 = (f32[4,8,8,128]{3,2,1,0:T(8,128)S(1)}, f32[4,8,8,128]{3,2,1,0:T(8,128)S(1)}, u32[]{:S(2)}, u32[]{:S(2)}) collective-permute-start(f32[4,8,8,128]{3,2,1,0:T(8,128)S(1)} %get-tuple-element.155), channel_id=1, source_target_pairs={{0,1},{1,2},{2,3},{3,4},{4,5},{5,6},{6,7},{7,8},{8,9},{9,10},{10,1... | collective-permute-start | bytes 393224 | tf_op jit(solution)/shard_map/ppermute | solution.py:381
  72.4 4.8 %collective-permute-start.17 = (f32[4,8,8,128]{3,2,1,0:T(8,128)S(1)}, f32[4,8,8,128]{3,2,1,0:T(8,128)S(1)}, u32[]{:S(2)}, u32[]{:S(2)}) collective-permute-start(f32[4,8,8,128]{3,2,1,0:T(8,128)S(1)} %get-tuple-element.160), channel_id=1, source_target_pairs={{1,0},{2,1},{3,2},{4,3},{5,4},{6,5},{7,6},{8,7},{9,8},{10,9},{11,1... | collective-permute-start | bytes 393224 | tf_op jit(solution)/shard_map/ppermute | solution.py:381
  74.5 8.9 %collective-permute-start.14 = (f32[4,8,8,128]{3,2,1,0:T(8,128)S(1)}, f32[4,8,8,128]{3,2,1,0:T(8,128)S(1)}, u32[]{:S(2)}, u32[]{:S(2)}) collective-permute-start(f32[4,8,8,128]{3,2,1,0:T(8,128)S(1)} %get-tuple-element.152), channel_id=1, source_target_pairs={{0,1},{1,2},{2,3},{3,4},{4,5},{5,6},{6,7},{7,8},{8,9},{9,10},{10,1... | collective-permute-start | bytes 393224 | tf_op jit(solution)/shard_map/ppermute | solution.py:381
  84.9 20.3 %all-to-all-start.1 = ((f32[16,64,128]{2,1,0:T(8,128)}), f32[16,64,128]{2,1,0:T(8,128)S(1)}, u32[]{:S(2)}, u32[]{:S(2)}) async-start(f32[16,64,128]{2,1,0:T(8,128)} %bitcast.9), calls=%async_computation.1 | async-start | bytes 1048576 | tf_op jit(solution)/shard_map/all_to_all | solution.py:390

commit v5 on v4

--- a/solution.py
+++ b/solution.py
@@ -335,8 +335,10 @@
         changes = [None, None]
         inj = call(functools.partial(inject_kernel, step=step, steps=length),
                    (*marks, mat if block == 0 else token), (tiles(length, 8), tiles(length, 8)), 1 << 24)
-        for field in range(2):
-            for n, side in enumerate(order):
+        walk = [(f, n) for f in range(2) for n in range(2)] if length == 2 else [(f, n) for n in range(2) for f in range(2)]
+        for field, n in walk:
+            if True:
+                side = order[n]
                 if block == 1 and field == 0:
                     edge = call(edge_kernel, (keep[side], beyond[0][side]), quarter, 1 << 16)
                     vels[side] = [(vel, (0, 16)), (edge, (16 if side else -4, 4))]

time: 106 us -> 105 us (level)
  starting transfers between devices: 52.5 us -> 50.6 us
    ppermute x16, starting transfers between devices: 27.4 us -> 25.9 us  [body(): lax.ppermute(rest[-1] if send else out, 'slab', up if side else down)]
where the time goes in v5:
time: 105 us; the launch traced here: 104 us
  starting transfers between devices  50.6 us (48%)
  waiting for transfers between devices  29.1 us (28%)
  Pallas kernels  20.7 us (20%)
  local copies, waits for them, and re-layouts  2.68 us (3%)
    ppermute x16, starting transfers between devices, body(): lax.ppermute(rest[-1] if send else out, 'slab', up if side else down)  25.9 us
    pallas_call x33, Pallas kernels, call(): pl.pallas_call(kernel, in_specs=[whole] * len(args), out_specs=jax.tree.m...  20.7 us
    ppermute x16, waiting for transfers between devices, body(): lax.ppermute(rest[-1] if send else out, 'slab', up if side else down)  15.2 us
    all_to_all x1, starting transfers between devices, body(): lax.all_to_all(terms.reshape(shots, 64, NY), 'shot', 0, 0, tiled=True)  10.1 us
    all_to_all x1, waiting for transfers between devices, body(): lax.all_to_all(terms.reshape(shots, 64, NY), 'shot', 0, 0, tiled=True)  8.25 us
    all_to_all x1, starting transfers between devices, body(): lax.all_to_all(spread.reshape(shots, 64, NY), 'shot', 0, 0, tiled=True)  6.91 us
    ppermute x1, starting transfers between devices, body(): lax.ppermute(down_msg, 'slab', down)  6.11 us
    ppermute x1, waiting for transfers between devices, body(): lax.ppermute(up_msg, 'slab', up)  5.68 us
  transfers between devices with their start and end apart: 20, of which 9 were waited for; matrix products, arithmetic and copies ran while one was open for 0% of the time, Pallas kernels for 15%

profile of v5, /device:TPU:1, one launch (start us, length us, event | category | flops | bytes accessed | tf_op | source)
XLA Modules:
  0.0 104.1 jit_solution(16077645113412893495)
XLA Ops:
  1.4 0.8 shard_map.96
  2.2 6.9 %all-to-all-start = ((f32[16,64,128]{2,1,0:T(8,128)}), f32[16,64,128]{2,1,0:T(8,128)S(1)}, u32[]{:S(2)}, u32[]{:S(2)}) async-start(f32[16,64,128]{2,1,0:T(8,128)} %bitcast.6), calls=%async_computation | async-start | bytes 1048576 | tf_op jit(solution)/shard_map/all_to_all | solution.py:313
  9.1 1.2 %copy-done.1 = f32[1,2,16,64,128]{4,3,2,1,0:T(8,128)S(1)} copy-done((f32[1,2,16,64,128]{4,3,2,1,0:T(8,128)S(1)}, f32[1,2,16,64,128]{4,3,2,1,0:T(8,128)}, u32[]{:S(2)}) %copy-start.1) | copy-done | bytes 1048600
  10.4 0.9 shard_map.94
  11.2 1.7 %collective-permute-start = (f32[2,4,8,8,128]{4,3,2,1,0:T(8,128)}, f32[2,4,8,8,128]{4,3,2,1,0:T(8,128)S(1)}, u32[]{:S(2)}, u32[]{:S(2)}) collective-permute-start(f32[2,4,8,8,128]{4,3,2,1,0:T(8,128)} %get-tuple-element.91), channel_id=1, source_target_pairs={{0,1},{1,2},{2,3},{3,4},{4,5},{5,6},{6,7},{7,8},{8,9},{9,10},{10,1... | collective-permute-start | bytes 786440 | tf_op jit(solution)/shard_map/ppermute | solution.py:319
  12.9 6.1 %collective-permute-start.1 = (f32[2,4,8,8,128]{4,3,2,1,0:T(8,128)}, f32[2,4,8,8,128]{4,3,2,1,0:T(8,128)}, u32[]{:S(2)}, u32[]{:S(2)}) collective-permute-start(f32[2,4,8,8,128]{4,3,2,1,0:T(8,128)} %get-tuple-element.92), channel_id=1, source_target_pairs={{1,0},{2,1},{3,2},{4,3},{5,4},{6,5},{7,6},{8,7},{9,8},{10,9},{11,1... | collective-permute-start | bytes 786440 | tf_op jit(solution)/shard_map/ppermute | solution.py:319
  20.1 5.7 %collective-permute-done.below = f32[2,4,8,8,128]{4,3,2,1,0:T(8,128)S(1)} collective-permute-done((f32[2,4,8,8,128]{4,3,2,1,0:T(8,128)}, f32[2,4,8,8,128]{4,3,2,1,0:T(8,128)S(1)}, u32[]{:S(2)}, u32[]{:S(2)}) %collective-permute-start) | collective-permute-done | bytes 262176 | tf_op jit(solution)/shard_map/ppermute | solution.py:319
  25.8 1.3 %shard_map.97 = (f32[16,8,8,128]{3,2,1,0:T(8,128)S(1)}, f32[16,8,8,128]{3,2,1,0:T(8,128)S(1)}, f32[4,8,8,128]{3,2,1,0:T(8,128)S(1)}, f32[4,8,8,128]{3,2,1,0:T(8,...) custom-call(f32[8,128]{1,0:T(8,128)S(1)} %broadcast_in_dim.6.keep_below.refs_0_.keep, ...), custom_call_target="tpu_custom_call" | custom-call | flops 4194304 | bytes 1048576 | tf_op jit(solution)/shard_map/pallas_call | solution.py:290
  28.4 5.1 %collective-permute-start.2 = (f32[12,8,8,128]{3,2,1,0:T(8,128)S(1)}, f32[12,8,8,128]{3,2,1,0:T(8,128)S(1)}, u32[]{:S(2)}, u32[]{:S(2)}) collective-permute-start(f32[12,8,8,128]{3,2,1,0:T(8,128)S(1)} %get-tuple-element.109.refs_11_.refs_7_), channel_id=1, source_target_pairs={{1,0},{2,1},{3,2},{4,3},{5,4},{6,5},{7,6},{8,7},{9,8},{10,9},{11,1... | collective-permute-start | bytes 1179656 | tf_op jit(solution)/shard_map/ppermute | solution.py:383
  34.0 5.2 %collective-permute-start.3 = (f32[8,8,8,128]{3,2,1,0:T(8,128)S(1)}, f32[8,8,8,128]{3,2,1,0:T(8,128)S(1)}, u32[]{:S(2)}, u32[]{:S(2)}) collective-permute-start(f32[8,8,8,128]{3,2,1,0:T(8,128)S(1)} %get-tuple-element.110.token.refs_13_.refs_7_), channel_id=1, source_target_pairs={{1,0},{2,1},{3,2},{4,3},{5,4},{6,5},{7,6},{8,7},{9,8},{10,9},{11,1... | collective-permute-start | bytes 786440 | tf_op jit(solution)/shard_map/ppermute | solution.py:383
  39.7 0.9 shard_map.105
  40.5 1.0 collective-permute-start.8
  42.8 2.8 %collective-permute-done.5.refs_6_ = f32[8,8,8,128]{3,2,1,0:T(8,128)S(1)} collective-permute-done((f32[8,8,8,128]{3,2,1,0:T(8,128)S(1)}, f32[8,8,8,128]{3,2,1,0:T(8,128)S(1)}, u32[]{:S(2)}, u32[]{:S(2)}) %collective-permute-start.5) | collective-permute-done | bytes 262176 | tf_op jit(solution)/shard_map/ppermute | solution.py:383
  45.6 0.9 shard_map.107
  46.5 2.0 %collective-permute-start.7 = (f32[8,8,8,128]{3,2,1,0:T(8,128)S(1)}, f32[8,8,8,128]{3,2,1,0:T(8,128)S(1)}, u32[]{:S(2)}, u32[]{:S(2)}) collective-permute-start(f32[8,8,8,128]{3,2,1,0:T(8,128)S(1)} %get-tuple-element.121.refs_16_.refs_7_), channel_id=1, source_target_pairs={{1,0},{2,1},{3,2},{4,3},{5,4},{6,5},{7,6},{8,7},{9,8},{10,9},{11,1... | collective-permute-start | bytes 786440 | tf_op jit(solution)/shard_map/ppermute | solution.py:383
  49.6 1.3 %collective-permute-done.8.refs_6_ = f32[8,8,8,128]{3,2,1,0:T(8,128)S(1)} collective-permute-done((f32[8,8,8,128]{3,2,1,0:T(8,128)S(1)}, f32[8,8,8,128]{3,2,1,0:T(8,128)S(1)}, u32[]{:S(2)}, u32[]{:S(2)}) %collective-permute-start.8) | collective-permute-done | bytes 262176 | tf_op jit(solution)/shard_map/ppermute | solution.py:383
  51.0 0.8 shard_map.110
  52.6 5.9 %collective-permute-start.13 = (f32[8,8,8,128]{3,2,1,0:T(8,128)S(1)}, f32[8,8,8,128]{3,2,1,0:T(8,128)S(1)}, u32[]{:S(2)}, u32[]{:S(2)}) collective-permute-start(f32[8,8,8,128]{3,2,1,0:T(8,128)S(1)} %get-tuple-element.131.refs_13_.refs_7_), channel_id=1, source_target_pairs={{1,0},{2,1},{3,2},{4,3},{5,4},{6,5},{7,6},{8,7},{9,8},{10,9},{11,1... | collective-permute-start | bytes 786440 | tf_op jit(solution)/shard_map/ppermute | solution.py:383
  58.5 0.9 shard_map.112
  59.4 1.4 %collective-permute-done.6.refs_6_ = f32[8,8,8,128]{3,2,1,0:T(8,128)S(1)} collective-permute-done((f32[8,8,8,128]{3,2,1,0:T(8,128)S(1)}, f32[8,8,8,128]{3,2,1,0:T(8,128)S(1)}, u32[]{:S(2)}, u32[]{:S(2)}) %collective-permute-start.6) | collective-permute-done | bytes 262176 | tf_op jit(solution)/shard_map/ppermute | solution.py:383
  61.6 3.7 %collective-permute-start.10 = (f32[8,8,8,128]{3,2,1,0:T(8,128)S(1)}, f32[8,8,8,128]{3,2,1,0:T(8,128)S(1)}, u32[]{:S(2)}, u32[]{:S(2)}) collective-permute-start(f32[8,8,8,128]{3,2,1,0:T(8,128)S(1)} %get-tuple-element.136.token.refs_11_.refs_7_), channel_id=1, source_target_pairs={{1,0},{2,1},{3,2},{4,3},{5,4},{6,5},{7,6},{8,7},{9,8},{10,9},{11,1... | collective-permute-start | bytes 786440 | tf_op jit(solution)/shard_map/ppermute | solution.py:383
  65.8 0.9 shard_map.115
  67.7 3.8 %collective-permute-done.11.refs_6_ = f32[8,8,8,128]{3,2,1,0:T(8,128)S(1)} collective-permute-done((f32[8,8,8,128]{3,2,1,0:T(8,128)S(1)}, f32[8,8,8,128]{3,2,1,0:T(8,128)S(1)}, u32[]{:S(2)}, u32[]{:S(2)}) %collective-permute-start.11) | collective-permute-done | bytes 262176 | tf_op jit(solution)/shard_map/ppermute | solution.py:383
  71.4 0.9 shard_map.117
  72.4 1.5 %collective-permute-start.15 = (f32[4,8,8,128]{3,2,1,0:T(8,128)S(1)}, f32[4,8,8,128]{3,2,1,0:T(8,128)S(1)}, u32[]{:S(2)}, u32[]{:S(2)}) collective-permute-start(f32[4,8,8,128]{3,2,1,0:T(8,128)S(1)} %get-tuple-element.155), channel_id=1, source_target_pairs={{0,1},{1,2},{2,3},{3,4},{4,5},{5,6},{6,7},{7,8},{8,9},{9,10},{10,1... | collective-permute-start | bytes 393224 | tf_op jit(solution)/shard_map/ppermute | solution.py:383
  75.3 0.9 collective-permute-done.16.refs_6_
  76.6 3.5 %collective-permute-done.15.refs_6_ = f32[4,8,8,128]{3,2,1,0:T(8,128)S(1)} collective-permute-done((f32[4,8,8,128]{3,2,1,0:T(8,128)S(1)}, f32[4,8,8,128]{3,2,1,0:T(8,128)S(1)}, u32[]{:S(2)}, u32[]{:S(2)}) %collective-permute-start.15) | collective-permute-done | bytes 131104 | tf_op jit(solution)/shard_map/ppermute | solution.py:383
  80.5 1.5 %collective-permute-done.14.refs_6_ = f32[4,8,8,128]{3,2,1,0:T(8,128)S(1)} collective-permute-done((f32[4,8,8,128]{3,2,1,0:T(8,128)S(1)}, f32[4,8,8,128]{3,2,1,0:T(8,128)S(1)}, u32[]{:S(2)}, u32[]{:S(2)}) %collective-permute-start.14) | collective-permute-done | bytes 131104 | tf_op jit(solution)/shard_map/ppermute | solution.py:383
  82.4 1.1 %shard_map.124 = f32[1024,128]{1,0:T(8,128)} custom-call(f32[16,8,8,128]{3,2,1,0:T(8,128)S(1)} %get-tuple-element.166.image), custom_call_target="tpu_custom_call" | custom-call | flops 1048576 | bytes 1048576 | tf_op jit(solution)/shard_map/pallas_call | solution.py:290
  83.5 10.1 %all-to-all-start.1 = ((f32[16,64,128]{2,1,0:T(8,128)}), f32[16,64,128]{2,1,0:T(8,128)S(1)}, u32[]{:S(2)}, u32[]{:S(2)}) async-start(f32[16,64,128]{2,1,0:T(8,128)} %bitcast.9), calls=%async_computation.1 | async-start | bytes 1048576 | tf_op jit(solution)/shard_map/all_to_all | solution.py:392
  93.6 1.6 %shard_map.126 = (f32[2048,128]{1,0:T(8,128)}, f32[2048,128]{1,0:T(8,128)}) custom-call(f32[8,8,8,128]{3,2,1,0:T(8,128)S(1)} %get-tuple-element.144.refs_12_.refs_7_.before_low_0, f32[8,8,8,128]{3,2,1,0:T(8,128)S(1)} %get-tuple-element.145.refs_13_.refs_8_.before_high_0, f32[8,8,8,128]{3,2,1,0:T(8,128)S(1)} %get-tuple-element.165.refs_13_.low_0, ...), custom_call_target="tpu_custom_call" | custom-call | flops 4194304 | bytes 1048576 | tf_op jit(solution)/shard_map/pallas_call | solution.py:290
  95.2 8.3 %all-to-all-done.1 = f32[16,64,128]{2,1,0:T(8,128)S(1)} async-done(((f32[16,64,128]{2,1,0:T(8,128)}), f32[16,64,128]{2,1,0:T(8,128)S(1)}, u32[]{:S(2)}, u32[]{:S(2)}) %all-to-all-start.1) | async-done | bytes 524320 | tf_op jit(solution)/shard_map/all_to_all | solution.py:392
  (59 shorter events, 12.8 us)
Async XLA Ops:
  0.6 0.8 copy-start.3
  2.2 23.6 %all-to-all-start = ((f32[16,64,128]{2,1,0:T(8,128)}), f32[16,64,128]{2,1,0:T(8,128)S(1)}, u32[]{:S(2)}, u32[]{:S(2)}) async-start(f32[16,64,128]{2,1,0:T(8,128)} %bitcast.6), calls=%async_computation | async-start | bytes 1048576 | tf_op jit(solution)/shard_map/all_to_all | solution.py:313
  9.1 1.2 %copy-start.1 = (f32[1,2,16,64,128]{4,3,2,1,0:T(8,128)S(1)}, f32[1,2,16,64,128]{4,3,2,1,0:T(8,128)}, u32[]{:S(2)}) copy-start(f32[1,2,16,64,128]{4,3,2,1,0:T(8,128)} %param.9) | copy-start | bytes 3145732
  10.4 8.7 %copy-start.5 = (s32[1,256]{1,0:T(1,128)S(1)}, s32[1,256]{1,0:T(1,128)}, u32[]{:S(2)}) copy-start(s32[1,256]{1,0:T(1,128)} %cells.9) | copy-start | bytes 3076
  10.4 16.8 %copy-start = (f32[1,2,16,64,128]{4,3,2,1,0:T(8,128)S(1)}, f32[1,2,16,64,128]{4,3,2,1,0:T(8,128)}, u32[]{:S(2)}) copy-start(f32[1,2,16,64,128]{4,3,2,1,0:T(8,128)} %param.8) | copy-start | bytes 3145732
  11.2 14.5 %collective-permute-start = (f32[2,4,8,8,128]{4,3,2,1,0:T(8,128)}, f32[2,4,8,8,128]{4,3,2,1,0:T(8,128)S(1)}, u32[]{:S(2)}, u32[]{:S(2)}) collective-permute-start(f32[2,4,8,8,128]{4,3,2,1,0:T(8,128)} %get-tuple-element.91), channel_id=1, source_target_pairs={{0,1},{1,2},{2,3},{3,4},{4,5},{5,6},{6,7},{7,8},{8,9},{9,10},{10,1... | collective-permute-start | bytes 786440 | tf_op jit(solution)/shard_map/ppermute | solution.py:319
  12.9 12.9 %collective-permute-start.1 = (f32[2,4,8,8,128]{4,3,2,1,0:T(8,128)}, f32[2,4,8,8,128]{4,3,2,1,0:T(8,128)}, u32[]{:S(2)}, u32[]{:S(2)}) collective-permute-start(f32[2,4,8,8,128]{4,3,2,1,0:T(8,128)} %get-tuple-element.92), channel_id=1, source_target_pairs={{1,0},{2,1},{3,2},{4,3},{5,4},{6,5},{7,6},{8,7},{9,8},{10,9},{11,1... | collective-permute-start | bytes 786440 | tf_op jit(solution)/shard_map/ppermute | solution.py:319
  19.0 0.7 copy-start.2
  19.0 0.7 copy-start.4
  19.0 0.7 copy-start.6
  27.5 12.1 %collective-permute-start.4 = (f32[12,8,8,128]{3,2,1,0:T(8,128)S(1)}, f32[12,8,8,128]{3,2,1,0:T(8,128)S(1)}, u32[]{:S(2)}, u32[]{:S(2)}) collective-permute-start(f32[12,8,8,128]{3,2,1,0:T(8,128)S(1)} %get-tuple-element.105.refs_11_.refs_8_), channel_id=1, source_target_pairs={{0,1},{1,2},{2,3},{3,4},{4,5},{5,6},{6,7},{7,8},{8,9},{9,10},{10,1... | collective-permute-start | bytes 1179656 | tf_op jit(solution)/shard_map/ppermute | solution.py:383
  28.4 13.1 %collective-permute-start.2 = (f32[12,8,8,128]{3,2,1,0:T(8,128)S(1)}, f32[12,8,8,128]{3,2,1,0:T(8,128)S(1)}, u32[]{:S(2)}, u32[]{:S(2)}) collective-permute-start(f32[12,8,8,128]{3,2,1,0:T(8,128)S(1)} %get-tuple-element.109.refs_11_.refs_7_), channel_id=1, source_target_pairs={{1,0},{2,1},{3,2},{4,3},{5,4},{6,5},{7,6},{8,7},{9,8},{10,9},{11,1... | collective-permute-start | bytes 1179656 | tf_op jit(solution)/shard_map/ppermute | solution.py:383
  33.6 12.0 %collective-permute-start.5 = (f32[8,8,8,128]{3,2,1,0:T(8,128)S(1)}, f32[8,8,8,128]{3,2,1,0:T(8,128)S(1)}, u32[]{:S(2)}, u32[]{:S(2)}) collective-permute-start(f32[8,8,8,128]{3,2,1,0:T(8,128)S(1)} %get-tuple-element.106.refs_9_.refs_8_), channel_id=1, source_target_pairs={{0,1},{1,2},{2,3},{3,4},{4,5},{5,6},{6,7},{7,8},{8,9},{9,10},{10,1... | collective-permute-start | bytes 786440 | tf_op jit(solution)/shard_map/ppermute | solution.py:383
  34.0 5.2 %copy-start.7 = (s32[1,2]{1,0:T(1,128)S(1)}, s32[1,2]{1,0:T(1,128)}, u32[]{:S(2)}) copy-start(s32[1,2]{1,0:T(1,128)} %source_cells.9) | copy-start | bytes 28
  34.0 14.5 %collective-permute-start.3 = (f32[8,8,8,128]{3,2,1,0:T(8,128)S(1)}, f32[8,8,8,128]{3,2,1,0:T(8,128)S(1)}, u32[]{:S(2)}, u32[]{:S(2)}) collective-permute-start(f32[8,8,8,128]{3,2,1,0:T(8,128)S(1)} %get-tuple-element.110.token.refs_13_.refs_7_), channel_id=1, source_target_pairs={{1,0},{2,1},{3,2},{4,3},{5,4},{6,5},{7,6},{8,7},{9,8},{10,9},{11,1... | collective-permute-start | bytes 786440 | tf_op jit(solution)/shard_map/ppermute | solution.py:383
  40.5 10.4 %collective-permute-start.8 = (f32[8,8,8,128]{3,2,1,0:T(8,128)S(1)}, f32[8,8,8,128]{3,2,1,0:T(8,128)S(1)}, u32[]{:S(2)}, u32[]{:S(2)}) collective-permute-start(f32[8,8,8,128]{3,2,1,0:T(8,128)S(1)} %get-tuple-element.116.refs_14_.refs_7_), channel_id=1, source_target_pairs={{1,0},{2,1},{3,2},{4,3},{5,4},{6,5},{7,6},{8,7},{9,8},{10,9},{11,1... | collective-permute-start | bytes 786440 | tf_op jit(solution)/shard_map/ppermute | solution.py:383
  42.2 9.7 %collective-permute-start.9 = (f32[8,8,8,128]{3,2,1,0:T(8,128)S(1)}, f32[8,8,8,128]{3,2,1,0:T(8,128)S(1)}, u32[]{:S(2)}, u32[]{:S(2)}) collective-permute-start(f32[8,8,8,128]{3,2,1,0:T(8,128)S(1)} %get-tuple-element.117.refs_15_.refs_8_), channel_id=1, source_target_pairs={{0,1},{1,2},{2,3},{3,4},{4,5},{5,6},{6,7},{7,8},{8,9},{9,10},{10,1... | collective-permute-start | bytes 786440 | tf_op jit(solution)/shard_map/ppermute | solution.py:383
  46.5 12.0 %collective-permute-start.7 = (f32[8,8,8,128]{3,2,1,0:T(8,128)S(1)}, f32[8,8,8,128]{3,2,1,0:T(8,128)S(1)}, u32[]{:S(2)}, u32[]{:S(2)}) collective-permute-start(f32[8,8,8,128]{3,2,1,0:T(8,128)S(1)} %get-tuple-element.121.refs_16_.refs_7_), channel_id=1, source_target_pairs={{1,0},{2,1},{3,2},{4,3},{5,4},{6,5},{7,6},{8,7},{9,8},{10,9},{11,1... | collective-permute-start | bytes 786440 | tf_op jit(solution)/shard_map/ppermute | solution.py:383
  49.1 11.8 %collective-permute-start.6 = (f32[8,8,8,128]{3,2,1,0:T(8,128)S(1)}, f32[8,8,8,128]{3,2,1,0:T(8,128)S(1)}, u32[]{:S(2)}, u32[]{:S(2)}) collective-permute-start(f32[8,8,8,128]{3,2,1,0:T(8,128)S(1)} %get-tuple-element.122.token.refs_11_.refs_8_), channel_id=1, source_target_pairs={{0,1},{1,2},{2,3},{3,4},{4,5},{5,6},{6,7},{7,8},{8,9},{9,10},{10,1... | collective-permute-start | bytes 786440 | tf_op jit(solution)/shard_map/ppermute | solution.py:383
  51.8 14.0 %collective-permute-start.12 = (f32[8,8,8,128]{3,2,1,0:T(8,128)S(1)}, f32[8,8,8,128]{3,2,1,0:T(8,128)S(1)}, u32[]{:S(2)}, u32[]{:S(2)}) collective-permute-start(f32[8,8,8,128]{3,2,1,0:T(8,128)S(1)} %get-tuple-element.130.refs_12_.refs_8_), channel_id=1, source_target_pairs={{0,1},{1,2},{2,3},{3,4},{4,5},{5,6},{6,7},{7,8},{8,9},{9,10},{10,1... | collective-permute-start | bytes 786440 | tf_op jit(solution)/shard_map/ppermute | solution.py:383
  52.6 14.5 %collective-permute-start.13 = (f32[8,8,8,128]{3,2,1,0:T(8,128)S(1)}, f32[8,8,8,128]{3,2,1,0:T(8,128)S(1)}, u32[]{:S(2)}, u32[]{:S(2)}) collective-permute-start(f32[8,8,8,128]{3,2,1,0:T(8,128)S(1)} %get-tuple-element.131.refs_13_.refs_7_), channel_id=1, source_target_pairs={{1,0},{2,1},{3,2},{4,3},{5,4},{6,5},{7,6},{8,7},{9,8},{10,9},{11,1... | collective-permute-start | bytes 786440 | tf_op jit(solution)/shard_map/ppermute | solution.py:383
  59.4 12.1 %collective-permute-start.11 = (f32[8,8,8,128]{3,2,1,0:T(8,128)S(1)}, f32[8,8,8,128]{3,2,1,0:T(8,128)S(1)}, u32[]{:S(2)}, u32[]{:S(2)}) collective-permute-start(f32[8,8,8,128]{3,2,1,0:T(8,128)S(1)} %get-tuple-element.135.refs_14_.refs_8_), channel_id=1, source_target_pairs={{0,1},{1,2},{2,3},{3,4},{4,5},{5,6},{6,7},{7,8},{8,9},{9,10},{10,1... | collective-permute-start | bytes 786440 | tf_op jit(solution)/shard_map/ppermute | solution.py:383
  61.6 12.3 %collective-permute-start.10 = (f32[8,8,8,128]{3,2,1,0:T(8,128)S(1)}, f32[8,8,8,128]{3,2,1,0:T(8,128)S(1)}, u32[]{:S(2)}, u32[]{:S(2)}) collective-permute-start(f32[8,8,8,128]{3,2,1,0:T(8,128)S(1)} %get-tuple-element.136.token.refs_11_.refs_7_), channel_id=1, source_target_pairs={{1,0},{2,1},{3,2},{4,3},{5,4},{6,5},{7,6},{8,7},{9,8},{10,9},{11,1... | collective-permute-start | bytes 786440 | tf_op jit(solution)/shard_map/ppermute | solution.py:383
  66.7 8.3 %collective-permute-start.17 = (f32[4,8,8,128]{3,2,1,0:T(8,128)S(1)}, f32[4,8,8,128]{3,2,1,0:T(8,128)S(1)}, u32[]{:S(2)}, u32[]{:S(2)}) collective-permute-start(f32[4,8,8,128]{3,2,1,0:T(8,128)S(1)} %get-tuple-element.158), channel_id=1, source_target_pairs={{1,0},{2,1},{3,2},{4,3},{5,4},{6,5},{7,6},{8,7},{9,8},{10,9},{11,1... | collective-permute-start | bytes 393224 | tf_op jit(solution)/shard_map/ppermute | solution.py:383
  72.3 3.9 %collective-permute-start.16 = (f32[4,8,8,128]{3,2,1,0:T(8,128)S(1)}, f32[4,8,8,128]{3,2,1,0:T(8,128)S(1)}, u32[]{:S(2)}, u32[]{:S(2)}) collective-permute-start(f32[4,8,8,128]{3,2,1,0:T(8,128)S(1)} %get-tuple-element.157), channel_id=1, source_target_pairs={{1,0},{2,1},{3,2},{4,3},{5,4},{6,5},{7,6},{8,7},{9,8},{10,9},{11,1... | collective-permute-start | bytes 393224 | tf_op jit(solution)/shard_map/ppermute | solution.py:383
  72.4 7.7 %collective-permute-start.15 = (f32[4,8,8,128]{3,2,1,0:T(8,128)S(1)}, f32[4,8,8,128]{3,2,1,0:T(8,128)S(1)}, u32[]{:S(2)}, u32[]{:S(2)}) collective-permute-start(f32[4,8,8,128]{3,2,1,0:T(8,128)S(1)} %get-tuple-element.155), channel_id=1, source_target_pairs={{0,1},{1,2},{2,3},{3,4},{4,5},{5,6},{6,7},{7,8},{8,9},{9,10},{10,1... | collective-permute-start | bytes 393224 | tf_op jit(solution)/shard_map/ppermute | solution.py:383
  74.5 7.5 %collective-permute-start.14 = (f32[4,8,8,128]{3,2,1,0:T(8,128)S(1)}, f32[4,8,8,128]{3,2,1,0:T(8,128)S(1)}, u32[]{:S(2)}, u32[]{:S(2)}) collective-permute-start(f32[4,8,8,128]{3,2,1,0:T(8,128)S(1)} %get-tuple-element.152), channel_id=1, source_target_pairs={{0,1},{1,2},{2,3},{3,4},{4,5},{5,6},{6,7},{7,8},{8,9},{9,10},{10,1... | collective-permute-start | bytes 393224 | tf_op jit(solution)/shard_map/ppermute | solution.py:383
  83.5 19.9 %all-to-all-start.1 = ((f32[16,64,128]{2,1,0:T(8,128)}), f32[16,64,128]{2,1,0:T(8,128)S(1)}, u32[]{:S(2)}, u32[]{:S(2)}) async-start(f32[16,64,128]{2,1,0:T(8,128)} %bitcast.9), calls=%async_computation.1 | async-start | bytes 1048576 | tf_op jit(solution)/shard_map/all_to_all | solution.py:392

commit v6 on v5

--- a/solution.py
+++ b/solution.py
@@ -335,7 +335,7 @@
         changes = [None, None]
         inj = call(functools.partial(inject_kernel, step=step, steps=length),
                    (*marks, mat if block == 0 else token), (tiles(length, 8), tiles(length, 8)), 1 << 24)
-        walk = [(f, n) for f in range(2) for n in range(2)] if length == 2 else [(f, n) for n in range(2) for f in range(2)]
+        walk = [(f, n) for f in range(2) for n in range(2)] if length == 2 or final else [(f, n) for n in range(2) for f in range(2)]
         for field, n in walk:
             if True:
                 side = order[n]

time: 105 us -> 107 us (1.019)
  starting transfers between devices: 50.6 us -> 52.4 us
    ppermute x16, starting transfers between devices: 25.9 us -> 27.3 us  [body(): lax.ppermute(rest[-1] if send else out, 'slab', up if side else down)]
where the time goes in v6:
time: 107 us; the launch traced here: 106 us
  starting transfers between devices  52.4 us (49%)
  waiting for transfers between devices  29.3 us (27%)
  Pallas kernels  20.7 us (19%)
  local copies, waits for them, and re-layouts  2.68 us (3%)
    ppermute x16, starting transfers between devices, body(): lax.ppermute(rest[-1] if send else out, 'slab', up if side else down)  27.3 us
    pallas_call x33, Pallas kernels, call(): pl.pallas_call(kernel, in_specs=[whole] * len(args), out_specs=jax.tree.m...  20.7 us
    ppermute x16, waiting for transfers between devices, body(): lax.ppermute(rest[-1] if send else out, 'slab', up if side else down)  15.3 us
    all_to_all x1, starting transfers between devices, body(): lax.all_to_all(terms.reshape(shots, 64, NY), 'shot', 0, 0, tiled=True)  10.4 us
    all_to_all x1, waiting for transfers between devices, body(): lax.all_to_all(terms.reshape(shots, 64, NY), 'shot', 0, 0, tiled=True)  8.25 us
    all_to_all x1, starting transfers between devices, body(): lax.all_to_all(spread.reshape(shots, 64, NY), 'shot', 0, 0, tiled=True)  6.91 us
    ppermute x1, starting transfers between devices, body(): lax.ppermute(down_msg, 'slab', down)  6.11 us
    ppermute x1, waiting for transfers between devices, body(): lax.ppermute(up_msg, 'slab', up)  5.68 us
  transfers between devices with their start and end apart: 20, of which 9 were waited for; matrix products, arithmetic and copies ran while one was open for 0% of the time, Pallas kernels for 15%

profile of v6, /device:TPU:1, one launch (start us, length us, event | category | flops | bytes accessed | tf_op | source)
XLA Modules:
  0.0 106.0 jit_solution(6140103704850766169)
XLA Ops:
  1.4 0.8 shard_map.96
  2.2 6.9 %all-to-all-start = ((f32[16,64,128]{2,1,0:T(8,128)}), f32[16,64,128]{2,1,0:T(8,128)S(1)}, u32[]{:S(2)}, u32[]{:S(2)}) async-start(f32[16,64,128]{2,1,0:T(8,128)} %bitcast.6), calls=%async_computation | async-start | bytes 1048576 | tf_op jit(solution)/shard_map/all_to_all | solution.py:313
  9.1 1.2 %copy-done.1 = f32[1,2,16,64,128]{4,3,2,1,0:T(8,128)S(1)} copy-done((f32[1,2,16,64,128]{4,3,2,1,0:T(8,128)S(1)}, f32[1,2,16,64,128]{4,3,2,1,0:T(8,128)}, u32[]{:S(2)}) %copy-start.1) | copy-done | bytes 1048600
  10.4 0.9 shard_map.94
  11.2 1.7 %collective-permute-start = (f32[2,4,8,8,128]{4,3,2,1,0:T(8,128)}, f32[2,4,8,8,128]{4,3,2,1,0:T(8,128)S(1)}, u32[]{:S(2)}, u32[]{:S(2)}) collective-permute-start(f32[2,4,8,8,128]{4,3,2,1,0:T(8,128)} %get-tuple-element.91), channel_id=1, source_target_pairs={{0,1},{1,2},{2,3},{3,4},{4,5},{5,6},{6,7},{7,8},{8,9},{9,10},{10,1... | collective-permute-start | bytes 786440 | tf_op jit(solution)/shard_map/ppermute | solution.py:319
  12.9 6.1 %collective-permute-start.1 = (f32[2,4,8,8,128]{4,3,2,1,0:T(8,128)}, f32[2,4,8,8,128]{4,3,2,1,0:T(8,128)}, u32[]{:S(2)}, u32[]{:S(2)}) collective-permute-start(f32[2,4,8,8,128]{4,3,2,1,0:T(8,128)} %get-tuple-element.92), channel_id=1, source_target_pairs={{1,0},{2,1},{3,2},{4,3},{5,4},{6,5},{7,6},{8,7},{9,8},{10,9},{11,1... | collective-permute-start | bytes 786440 | tf_op jit(solution)/shard_map/ppermute | solution.py:319
  20.1 5.7 %collective-permute-done.below = f32[2,4,8,8,128]{4,3,2,1,0:T(8,128)S(1)} collective-permute-done((f32[2,4,8,8,128]{4,3,2,1,0:T(8,128)}, f32[2,4,8,8,128]{4,3,2,1,0:T(8,128)S(1)}, u32[]{:S(2)}, u32[]{:S(2)}) %collective-permute-start) | collective-permute-done | bytes 262176 | tf_op jit(solution)/shard_map/ppermute | solution.py:319
  25.8 1.3 %shard_map.97 = (f32[16,8,8,128]{3,2,1,0:T(8,128)S(1)}, f32[16,8,8,128]{3,2,1,0:T(8,128)S(1)}, f32[4,8,8,128]{3,2,1,0:T(8,128)S(1)}, f32[4,8,8,128]{3,2,1,0:T(8,...) custom-call(f32[8,128]{1,0:T(8,128)S(1)} %broadcast_in_dim.6.keep_below.refs_0_.keep, ...), custom_call_target="tpu_custom_call" | custom-call | flops 4194304 | bytes 1048576 | tf_op jit(solution)/shard_map/pallas_call | solution.py:290
  28.4 5.1 %collective-permute-start.2 = (f32[12,8,8,128]{3,2,1,0:T(8,128)S(1)}, f32[12,8,8,128]{3,2,1,0:T(8,128)S(1)}, u32[]{:S(2)}, u32[]{:S(2)}) collective-permute-start(f32[12,8,8,128]{3,2,1,0:T(8,128)S(1)} %get-tuple-element.109.refs_11_.refs_7_), channel_id=1, source_target_pairs={{1,0},{2,1},{3,2},{4,3},{5,4},{6,5},{7,6},{8,7},{9,8},{10,9},{11,1... | collective-permute-start | bytes 1179656 | tf_op jit(solution)/shard_map/ppermute | solution.py:383
  34.0 5.2 %collective-permute-start.3 = (f32[8,8,8,128]{3,2,1,0:T(8,128)S(1)}, f32[8,8,8,128]{3,2,1,0:T(8,128)S(1)}, u32[]{:S(2)}, u32[]{:S(2)}) collective-permute-start(f32[8,8,8,128]{3,2,1,0:T(8,128)S(1)} %get-tuple-element.110.token.refs_13_.refs_7_), channel_id=1, source_target_pairs={{1,0},{2,1},{3,2},{4,3},{5,4},{6,5},{7,6},{8,7},{9,8},{10,9},{11,1... | collective-permute-start | bytes 786440 | tf_op jit(solution)/shard_map/ppermute | solution.py:383
  39.7 0.9 shard_map.105
  40.5 1.0 collective-permute-start.8
  42.8 2.8 %collective-permute-done.5.refs_6_ = f32[8,8,8,128]{3,2,1,0:T(8,128)S(1)} collective-permute-done((f32[8,8,8,128]{3,2,1,0:T(8,128)S(1)}, f32[8,8,8,128]{3,2,1,0:T(8,128)S(1)}, u32[]{:S(2)}, u32[]{:S(2)}) %collective-permute-start.5) | collective-permute-done | bytes 262176 | tf_op jit(solution)/shard_map/ppermute | solution.py:383
  45.6 0.9 shard_map.107
  46.5 2.0 %collective-permute-start.7 = (f32[8,8,8,128]{3,2,1,0:T(8,128)S(1)}, f32[8,8,8,128]{3,2,1,0:T(8,128)S(1)}, u32[]{:S(2)}, u32[]{:S(2)}) collective-permute-start(f32[8,8,8,128]{3,2,1,0:T(8,128)S(1)} %get-tuple-element.121.refs_16_.refs_7_), channel_id=1, source_target_pairs={{1,0},{2,1},{3,2},{4,3},{5,4},{6,5},{7,6},{8,7},{9,8},{10,9},{11,1... | collective-permute-start | bytes 786440 | tf_op jit(solution)/shard_map/ppermute | solution.py:383
  49.6 1.3 %collective-permute-done.8.refs_6_ = f32[8,8,8,128]{3,2,1,0:T(8,128)S(1)} collective-permute-done((f32[8,8,8,128]{3,2,1,0:T(8,128)S(1)}, f32[8,8,8,128]{3,2,1,0:T(8,128)S(1)}, u32[]{:S(2)}, u32[]{:S(2)}) %collective-permute-start.8) | collective-permute-done | bytes 262176 | tf_op jit(solution)/shard_map/ppermute | solution.py:383
  51.0 0.8 shard_map.110
  52.6 5.9 %collective-permute-start.13 = (f32[8,8,8,128]{3,2,1,0:T(8,128)S(1)}, f32[8,8,8,128]{3,2,1,0:T(8,128)S(1)}, u32[]{:S(2)}, u32[]{:S(2)}) collective-permute-start(f32[8,8,8,128]{3,2,1,0:T(8,128)S(1)} %get-tuple-element.131.refs_13_.refs_7_), channel_id=1, source_target_pairs={{1,0},{2,1},{3,2},{4,3},{5,4},{6,5},{7,6},{8,7},{9,8},{10,9},{11,1... | collective-permute-start | bytes 786440 | tf_op jit(solution)/shard_map/ppermute | solution.py:383
  58.5 0.9 shard_map.112
  59.4 1.4 %collective-permute-done.6.refs_6_ = f32[8,8,8,128]{3,2,1,0:T(8,128)S(1)} collective-permute-done((f32[8,8,8,128]{3,2,1,0:T(8,128)S(1)}, f32[8,8,8,128]{3,2,1,0:T(8,128)S(1)}, u32[]{:S(2)}, u32[]{:S(2)}) %collective-permute-start.6) | collective-permute-done | bytes 262176 | tf_op jit(solution)/shard_map/ppermute | solution.py:383
  61.6 3.7 %collective-permute-start.10 = (f32[8,8,8,128]{3,2,1,0:T(8,128)S(1)}, f32[8,8,8,128]{3,2,1,0:T(8,128)S(1)}, u32[]{:S(2)}, u32[]{:S(2)}) collective-permute-start(f32[8,8,8,128]{3,2,1,0:T(8,128)S(1)} %get-tuple-element.136.token.refs_11_.refs_7_), channel_id=1, source_target_pairs={{1,0},{2,1},{3,2},{4,3},{5,4},{6,5},{7,6},{8,7},{9,8},{10,9},{11,1... | collective-permute-start | bytes 786440 | tf_op jit(solution)/shard_map/ppermute | solution.py:383
  65.8 0.9 shard_map.115
  67.7 1.2 %collective-permute-start.15 = (f32[4,8,8,128]{3,2,1,0:T(8,128)S(1)}, f32[4,8,8,128]{3,2,1,0:T(8,128)S(1)}, u32[]{:S(2)}, u32[]{:S(2)}) collective-permute-start(f32[4,8,8,128]{3,2,1,0:T(8,128)S(1)} %get-tuple-element.155), channel_id=1, source_target_pairs={{0,1},{1,2},{2,3},{3,4},{4,5},{5,6},{6,7},{7,8},{8,9},{9,10},{10,1... | collective-permute-start | bytes 393224 | tf_op jit(solution)/shard_map/ppermute | solution.py:383
  68.9 2.5 %collective-permute-done.11.refs_6_ = f32[8,8,8,128]{3,2,1,0:T(8,128)S(1)} collective-permute-done((f32[8,8,8,128]{3,2,1,0:T(8,128)S(1)}, f32[8,8,8,128]{3,2,1,0:T(8,128)S(1)}, u32[]{:S(2)}, u32[]{:S(2)}) %collective-permute-start.11) | collective-permute-done | bytes 262176 | tf_op jit(solution)/shard_map/ppermute | solution.py:383
  71.4 0.9 shard_map.117
  72.3 1.7 %collective-permute-start.17 = (f32[4,8,8,128]{3,2,1,0:T(8,128)S(1)}, f32[4,8,8,128]{3,2,1,0:T(8,128)S(1)}, u32[]{:S(2)}, u32[]{:S(2)}) collective-permute-start(f32[4,8,8,128]{3,2,1,0:T(8,128)S(1)} %get-tuple-element.160), channel_id=1, source_target_pairs={{1,0},{2,1},{3,2},{4,3},{5,4},{6,5},{7,6},{8,7},{9,8},{10,9},{11,1... | collective-permute-start | bytes 393224 | tf_op jit(solution)/shard_map/ppermute | solution.py:383
  75.5 0.8 collective-permute-done.15.refs_6_
  77.8 5.7 %collective-permute-done.14.refs_6_ = f32[4,8,8,128]{3,2,1,0:T(8,128)S(1)} collective-permute-done((f32[4,8,8,128]{3,2,1,0:T(8,128)S(1)}, f32[4,8,8,128]{3,2,1,0:T(8,128)S(1)}, u32[]{:S(2)}, u32[]{:S(2)}) %collective-permute-start.14) | collective-permute-done | bytes 131104 | tf_op jit(solution)/shard_map/ppermute | solution.py:383
  84.0 1.1 %shard_map.124 = f32[1024,128]{1,0:T(8,128)} custom-call(f32[16,8,8,128]{3,2,1,0:T(8,128)S(1)} %get-tuple-element.166.image), custom_call_target="tpu_custom_call" | custom-call | flops 1048576 | bytes 1048576 | tf_op jit(solution)/shard_map/pallas_call | solution.py:290
  85.1 10.4 %all-to-all-start.1 = ((f32[16,64,128]{2,1,0:T(8,128)}), f32[16,64,128]{2,1,0:T(8,128)S(1)}, u32[]{:S(2)}, u32[]{:S(2)}) async-start(f32[16,64,128]{2,1,0:T(8,128)} %bitcast.9), calls=%async_computation.1 | async-start | bytes 1048576 | tf_op jit(solution)/shard_map/all_to_all | solution.py:392
  95.5 1.6 %shard_map.126 = (f32[2048,128]{1,0:T(8,128)}, f32[2048,128]{1,0:T(8,128)}) custom-call(f32[8,8,8,128]{3,2,1,0:T(8,128)S(1)} %get-tuple-element.144.refs_12_.refs_7_.before_low_0, f32[8,8,8,128]{3,2,1,0:T(8,128)S(1)} %get-tuple-element.145.refs_13_.refs_8_.before_high_0, f32[8,8,8,128]{3,2,1,0:T(8,128)S(1)} %get-tuple-element.163.refs_13_.low_0, ...), custom_call_target="tpu_custom_call" | custom-call | flops 4194304 | bytes 1048576 | tf_op jit(solution)/shard_map/pallas_call | solution.py:290
  97.1 8.3 %all-to-all-done.1 = f32[16,64,128]{2,1,0:T(8,128)S(1)} async-done(((f32[16,64,128]{2,1,0:T(8,128)}), f32[16,64,128]{2,1,0:T(8,128)S(1)}, u32[]{:S(2)}, u32[]{:S(2)}) %all-to-all-start.1) | async-done | bytes 524320 | tf_op jit(solution)/shard_map/all_to_all | solution.py:392
  (59 shorter events, 13.5 us)
Async XLA Ops:
  0.6 0.8 copy-start.3
  2.2 23.6 %all-to-all-start = ((f32[16,64,128]{2,1,0:T(8,128)}), f32[16,64,128]{2,1,0:T(8,128)S(1)}, u32[]{:S(2)}, u32[]{:S(2)}) async-start(f32[16,64,128]{2,1,0:T(8,128)} %bitcast.6), calls=%async_computation | async-start | bytes 1048576 | tf_op jit(solution)/shard_map/all_to_all | solution.py:313
  9.1 1.2 %copy-start.1 = (f32[1,2,16,64,128]{4,3,2,1,0:T(8,128)S(1)}, f32[1,2,16,64,128]{4,3,2,1,0:T(8,128)}, u32[]{:S(2)}) copy-start(f32[1,2,16,64,128]{4,3,2,1,0:T(8,128)} %param.9) | copy-start | bytes 3145732
  10.4 8.7 %copy-start.5 = (s32[1,256]{1,0:T(1,128)S(1)}, s32[1,256]{1,0:T(1,128)}, u32[]{:S(2)}) copy-start(s32[1,256]{1,0:T(1,128)} %cells.9) | copy-start | bytes 3076
  10.4 16.8 %copy-start = (f32[1,2,16,64,128]{4,3,2,1,0:T(8,128)S(1)}, f32[1,2,16,64,128]{4,3,2,1,0:T(8,128)}, u32[]{:S(2)}) copy-start(f32[1,2,16,64,128]{4,3,2,1,0:T(8,128)} %param.8) | copy-start | bytes 3145732
  11.2 14.5 %collective-permute-start = (f32[2,4,8,8,128]{4,3,2,1,0:T(8,128)}, f32[2,4,8,8,128]{4,3,2,1,0:T(8,128)S(1)}, u32[]{:S(2)}, u32[]{:S(2)}) collective-permute-start(f32[2,4,8,8,128]{4,3,2,1,0:T(8,128)} %get-tuple-element.91), channel_id=1, source_target_pairs={{0,1},{1,2},{2,3},{3,4},{4,5},{5,6},{6,7},{7,8},{8,9},{9,10},{10,1... | collective-permute-start | bytes 786440 | tf_op jit(solution)/shard_map/ppermute | solution.py:319
  12.9 12.9 %collective-permute-start.1 = (f32[2,4,8,8,128]{4,3,2,1,0:T(8,128)}, f32[2,4,8,8,128]{4,3,2,1,0:T(8,128)}, u32[]{:S(2)}, u32[]{:S(2)}) collective-permute-start(f32[2,4,8,8,128]{4,3,2,1,0:T(8,128)} %get-tuple-element.92), channel_id=1, source_target_pairs={{1,0},{2,1},{3,2},{4,3},{5,4},{6,5},{7,6},{8,7},{9,8},{10,9},{11,1... | collective-permute-start | bytes 786440 | tf_op jit(solution)/shard_map/ppermute | solution.py:319
  19.0 0.7 copy-start.2
  19.0 0.7 copy-start.4
  19.0 0.7 copy-start.6
  27.5 12.1 %collective-permute-start.4 = (f32[12,8,8,128]{3,2,1,0:T(8,128)S(1)}, f32[12,8,8,128]{3,2,1,0:T(8,128)S(1)}, u32[]{:S(2)}, u32[]{:S(2)}) collective-permute-start(f32[12,8,8,128]{3,2,1,0:T(8,128)S(1)} %get-tuple-element.105.refs_11_.refs_8_), channel_id=1, source_target_pairs={{0,1},{1,2},{2,3},{3,4},{4,5},{5,6},{6,7},{7,8},{8,9},{9,10},{10,1... | collective-permute-start | bytes 1179656 | tf_op jit(solution)/shard_map/ppermute | solution.py:383
  28.4 13.1 %collective-permute-start.2 = (f32[12,8,8,128]{3,2,1,0:T(8,128)S(1)}, f32[12,8,8,128]{3,2,1,0:T(8,128)S(1)}, u32[]{:S(2)}, u32[]{:S(2)}) collective-permute-start(f32[12,8,8,128]{3,2,1,0:T(8,128)S(1)} %get-tuple-element.109.refs_11_.refs_7_), channel_id=1, source_target_pairs={{1,0},{2,1},{3,2},{4,3},{5,4},{6,5},{7,6},{8,7},{9,8},{10,9},{11,1... | collective-permute-start | bytes 1179656 | tf_op jit(solution)/shard_map/ppermute | solution.py:383
  33.6 12.0 %collective-permute-start.5 = (f32[8,8,8,128]{3,2,1,0:T(8,128)S(1)}, f32[8,8,8,128]{3,2,1,0:T(8,128)S(1)}, u32[]{:S(2)}, u32[]{:S(2)}) collective-permute-start(f32[8,8,8,128]{3,2,1,0:T(8,128)S(1)} %get-tuple-element.106.refs_9_.refs_8_), channel_id=1, source_target_pairs={{0,1},{1,2},{2,3},{3,4},{4,5},{5,6},{6,7},{7,8},{8,9},{9,10},{10,1... | collective-permute-start | bytes 786440 | tf_op jit(solution)/shard_map/ppermute | solution.py:383
  34.0 5.2 %copy-start.7 = (s32[1,2]{1,0:T(1,128)S(1)}, s32[1,2]{1,0:T(1,128)}, u32[]{:S(2)}) copy-start(s32[1,2]{1,0:T(1,128)} %source_cells.9) | copy-start | bytes 28
  34.0 14.5 %collective-permute-start.3 = (f32[8,8,8,128]{3,2,1,0:T(8,128)S(1)}, f32[8,8,8,128]{3,2,1,0:T(8,128)S(1)}, u32[]{:S(2)}, u32[]{:S(2)}) collective-permute-start(f32[8,8,8,128]{3,2,1,0:T(8,128)S(1)} %get-tuple-element.110.token.refs_13_.refs_7_), channel_id=1, source_target_pairs={{1,0},{2,1},{3,2},{4,3},{5,4},{6,5},{7,6},{8,7},{9,8},{10,9},{11,1... | collective-permute-start | bytes 786440 | tf_op jit(solution)/shard_map/ppermute | solution.py:383
  40.5 10.4 %collective-permute-start.8 = (f32[8,8,8,128]{3,2,1,0:T(8,128)S(1)}, f32[8,8,8,128]{3,2,1,0:T(8,128)S(1)}, u32[]{:S(2)}, u32[]{:S(2)}) collective-permute-start(f32[8,8,8,128]{3,2,1,0:T(8,128)S(1)} %get-tuple-element.116.refs_14_.refs_7_), channel_id=1, source_target_pairs={{1,0},{2,1},{3,2},{4,3},{5,4},{6,5},{7,6},{8,7},{9,8},{10,9},{11,1... | collective-permute-start | bytes 786440 | tf_op jit(solution)/shard_map/ppermute | solution.py:383
  42.2 9.7 %collective-permute-start.9 = (f32[8,8,8,128]{3,2,1,0:T(8,128)S(1)}, f32[8,8,8,128]{3,2,1,0:T(8,128)S(1)}, u32[]{:S(2)}, u32[]{:S(2)}) collective-permute-start(f32[8,8,8,128]{3,2,1,0:T(8,128)S(1)} %get-tuple-element.117.refs_15_.refs_8_), channel_id=1, source_target_pairs={{0,1},{1,2},{2,3},{3,4},{4,5},{5,6},{6,7},{7,8},{8,9},{9,10},{10,1... | collective-permute-start | bytes 786440 | tf_op jit(solution)/shard_map/ppermute | solution.py:383
  46.5 12.0 %collective-permute-start.7 = (f32[8,8,8,128]{3,2,1,0:T(8,128)S(1)}, f32[8,8,8,128]{3,2,1,0:T(8,128)S(1)}, u32[]{:S(2)}, u32[]{:S(2)}) collective-permute-start(f32[8,8,8,128]{3,2,1,0:T(8,128)S(1)} %get-tuple-element.121.refs_16_.refs_7_), channel_id=1, source_target_pairs={{1,0},{2,1},{3,2},{4,3},{5,4},{6,5},{7,6},{8,7},{9,8},{10,9},{11,1... | collective-permute-start | bytes 786440 | tf_op jit(solution)/shard_map/ppermute | solution.py:383
  49.1 11.8 %collective-permute-start.6 = (f32[8,8,8,128]{3,2,1,0:T(8,128)S(1)}, f32[8,8,8,128]{3,2,1,0:T(8,128)S(1)}, u32[]{:S(2)}, u32[]{:S(2)}) collective-permute-start(f32[8,8,8,128]{3,2,1,0:T(8,128)S(1)} %get-tuple-element.122.token.refs_11_.refs_8_), channel_id=1, source_target_pairs={{0,1},{1,2},{2,3},{3,4},{4,5},{5,6},{6,7},{7,8},{8,9},{9,10},{10,1... | collective-permute-start | bytes 786440 | tf_op jit(solution)/shard_map/ppermute | solution.py:383
  51.8 14.0 %collective-permute-start.12 = (f32[8,8,8,128]{3,2,1,0:T(8,128)S(1)}, f32[8,8,8,128]{3,2,1,0:T(8,128)S(1)}, u32[]{:S(2)}, u32[]{:S(2)}) collective-permute-start(f32[8,8,8,128]{3,2,1,0:T(8,128)S(1)} %get-tuple-element.130.refs_12_.refs_8_), channel_id=1, source_target_pairs={{0,1},{1,2},{2,3},{3,4},{4,5},{5,6},{6,7},{7,8},{8,9},{9,10},{10,1... | collective-permute-start | bytes 786440 | tf_op jit(solution)/shard_map/ppermute | solution.py:383
  52.6 14.5 %collective-permute-start.13 = (f32[8,8,8,128]{3,2,1,0:T(8,128)S(1)}, f32[8,8,8,128]{3,2,1,0:T(8,128)S(1)}, u32[]{:S(2)}, u32[]{:S(2)}) collective-permute-start(f32[8,8,8,128]{3,2,1,0:T(8,128)S(1)} %get-tuple-element.131.refs_13_.refs_7_), channel_id=1, source_target_pairs={{1,0},{2,1},{3,2},{4,3},{5,4},{6,5},{7,6},{8,7},{9,8},{10,9},{11,1... | collective-permute-start | bytes 786440 | tf_op jit(solution)/shard_map/ppermute | solution.py:383
  59.4 12.1 %collective-permute-start.11 = (f32[8,8,8,128]{3,2,1,0:T(8,128)S(1)}, f32[8,8,8,128]{3,2,1,0:T(8,128)S(1)}, u32[]{:S(2)}, u32[]{:S(2)}) collective-permute-start(f32[8,8,8,128]{3,2,1,0:T(8,128)S(1)} %get-tuple-element.135.refs_14_.refs_8_), channel_id=1, source_target_pairs={{0,1},{1,2},{2,3},{3,4},{4,5},{5,6},{6,7},{7,8},{8,9},{9,10},{10,1... | collective-permute-start | bytes 786440 | tf_op jit(solution)/shard_map/ppermute | solution.py:383
  61.6 12.5 %collective-permute-start.10 = (f32[8,8,8,128]{3,2,1,0:T(8,128)S(1)}, f32[8,8,8,128]{3,2,1,0:T(8,128)S(1)}, u32[]{:S(2)}, u32[]{:S(2)}) collective-permute-start(f32[8,8,8,128]{3,2,1,0:T(8,128)S(1)} %get-tuple-element.136.token.refs_11_.refs_7_), channel_id=1, source_target_pairs={{1,0},{2,1},{3,2},{4,3},{5,4},{6,5},{7,6},{8,7},{9,8},{10,9},{11,1... | collective-permute-start | bytes 786440 | tf_op jit(solution)/shard_map/ppermute | solution.py:383
  66.7 8.5 %collective-permute-start.16 = (f32[4,8,8,128]{3,2,1,0:T(8,128)S(1)}, f32[4,8,8,128]{3,2,1,0:T(8,128)S(1)}, u32[]{:S(2)}, u32[]{:S(2)}) collective-permute-start(f32[4,8,8,128]{3,2,1,0:T(8,128)S(1)} %get-tuple-element.157), channel_id=1, source_target_pairs={{1,0},{2,1},{3,2},{4,3},{5,4},{6,5},{7,6},{8,7},{9,8},{10,9},{11,1... | collective-permute-start | bytes 393224 | tf_op jit(solution)/shard_map/ppermute | solution.py:383
  67.7 8.7 %collective-permute-start.15 = (f32[4,8,8,128]{3,2,1,0:T(8,128)S(1)}, f32[4,8,8,128]{3,2,1,0:T(8,128)S(1)}, u32[]{:S(2)}, u32[]{:S(2)}) collective-permute-start(f32[4,8,8,128]{3,2,1,0:T(8,128)S(1)} %get-tuple-element.155), channel_id=1, source_target_pairs={{0,1},{1,2},{2,3},{3,4},{4,5},{5,6},{6,7},{7,8},{8,9},{9,10},{10,1... | collective-permute-start | bytes 393224 | tf_op jit(solution)/shard_map/ppermute | solution.py:383
  72.3 5.1 %collective-permute-start.17 = (f32[4,8,8,128]{3,2,1,0:T(8,128)S(1)}, f32[4,8,8,128]{3,2,1,0:T(8,128)S(1)}, u32[]{:S(2)}, u32[]{:S(2)}) collective-permute-start(f32[4,8,8,128]{3,2,1,0:T(8,128)S(1)} %get-tuple-element.160), channel_id=1, source_target_pairs={{1,0},{2,1},{3,2},{4,3},{5,4},{6,5},{7,6},{8,7},{9,8},{10,9},{11,1... | collective-permute-start | bytes 393224 | tf_op jit(solution)/shard_map/ppermute | solution.py:383
  74.7 8.9 %collective-permute-start.14 = (f32[4,8,8,128]{3,2,1,0:T(8,128)S(1)}, f32[4,8,8,128]{3,2,1,0:T(8,128)S(1)}, u32[]{:S(2)}, u32[]{:S(2)}) collective-permute-start(f32[4,8,8,128]{3,2,1,0:T(8,128)S(1)} %get-tuple-element.152), channel_id=1, source_target_pairs={{0,1},{1,2},{2,3},{3,4},{4,5},{5,6},{6,7},{7,8},{8,9},{9,10},{10,1... | collective-permute-start | bytes 393224 | tf_op jit(solution)/shard_map/ppermute | solution.py:383
  85.1 20.3 %all-to-all-start.1 = ((f32[16,64,128]{2,1,0:T(8,128)}), f32[16,64,128]{2,1,0:T(8,128)S(1)}, u32[]{:S(2)}, u32[]{:S(2)}) async-start(f32[16,64,128]{2,1,0:T(8,128)} %bitcast.9), calls=%async_computation.1 | async-start | bytes 1048576 | tf_op jit(solution)/shard_map/all_to_all | solution.py:392
